TPU v7x, 32 devices: a whole 2x2x4 slice. The times are simulated.
32 devices in a mesh: ctx: 8 (over z, x), seq: 4 (over y, core).
Axes of the slice: x: 2, y: 2, z: 4, core: 2. Of those that a mesh axis runs over, the one named last changes fastest.
Arguments:
- queries: bfloat16 [4096, 8192], P('ctx', 'seq'), may hold values from -0.5 to 0.5
- keys: bfloat16 [4096, 8192], P('ctx', 'seq'), may hold values from -0.5 to 0.5
- values: bfloat16 [4096, 8192], P('ctx', 'seq'), may hold values from -6 to 6
- out_grad: bfloat16 [4096, 8192], P('ctx', 'seq'), may hold values from -0.5 to 0.5
Outputs:
- attended: bfloat16 [4096, 8192], P('ctx', 'seq')
- query_grad: bfloat16 [4096, 8192], P('ctx', 'seq')
- key_grad: bfloat16 [4096, 8192], P('ctx', 'seq')
- value_grad: bfloat16 [4096, 8192], P('ctx', 'seq')
All inputs are finite; a program needn't handle non-finite values.
Results may differ from a plain program's by a relative error of at most 0.0049.
Values sent between devices are 32-bit elements; how exact they have to be, the bound alone decides.
No kernel may reach another device: no remote copies, remote signals or barrier semaphores. Data moves between devices by JAX's collectives and lax.ppermute only.
A program may use at most 128 MiB of HBM per device.

v0:
```python
import jax
import jax.numpy as jnp
from jax import lax
from jax.sharding import PartitionSpec as P

DH = 128
BLOCK = 128


def prefix(part, axis, combine, identity, reverse):
    count = lax.axis_size(axis)
    place = lax.axis_index(axis)
    ahead = count - 1 - place if reverse else place
    gathered = lax.all_gather(part, axis)
    state = jnp.zeros_like(part) + jnp.asarray(identity, part.dtype)

    def one(turn, state):
        source = count - 1 - turn if reverse else turn
        return combine(state, lax.dynamic_index_in_dim(gathered, source, 0, False))

    return lax.fori_loop(0, ahead, one, state)


def add_states(earlier, later):
    return earlier + later


def body(queries, keys, values, out_grad):
    count = queries.shape[0]
    heads = queries.shape[1] // DH
    nblocks = count // BLOCK
    shape = (nblocks, BLOCK, heads, DH)
    qloc = queries.reshape(shape)
    kloc = keys.reshape(shape)
    vloc = values.reshape(shape)
    gloc = out_grad.reshape(shape)
    f32 = jnp.float32
    kv_blocks = jnp.einsum("bthi,bthj->bhij", kloc, vloc, preferred_element_type=f32)
    qg_blocks = jnp.einsum("bthi,bthj->bhij", qloc, gloc, preferred_element_type=f32)
    kv_run = jnp.sum(kv_blocks, axis=0)
    qg_run = jnp.sum(qg_blocks, axis=0)
    kv_before = prefix(kv_run, "ctx", add_states, jnp.zeros_like(kv_run), False)
    qg_after = prefix(qg_run, "ctx", add_states, jnp.zeros_like(qg_run), True)
    kv_local = lax.cumsum(kv_blocks, axis=0) - kv_blocks
    qg_local = lax.cumsum(qg_blocks, axis=0, reverse=True) - qg_blocks
    prefix_low = (kv_before[None] + kv_local).astype(jnp.bfloat16)
    suffix_low = (qg_after[None] + qg_local).astype(jnp.bfloat16)
    rows = lax.broadcasted_iota(jnp.int32, (BLOCK, BLOCK), 0)
    cols = lax.broadcasted_iota(jnp.int32, (BLOCK, BLOCK), 1)
    causal = (cols <= rows)[None, None]
    attn = jnp.where(
        causal, jnp.einsum("bthi,bshi->bhts", qloc, kloc, preferred_element_type=f32), 0.0
    ).astype(jnp.bfloat16)
    grads = jnp.where(
        causal, jnp.einsum("bthj,bshj->bhts", gloc, vloc, preferred_element_type=f32), 0.0
    ).astype(jnp.bfloat16)
    attended = jnp.einsum("bhts,bshj->bthj", attn, vloc, preferred_element_type=f32)
    attended = attended + jnp.einsum(
        "bthi,bhij->bthj", qloc, prefix_low, preferred_element_type=f32
    )
    query_grad = jnp.einsum("bhts,bshi->bthi", grads, kloc, preferred_element_type=f32)
    query_grad = query_grad + jnp.einsum(
        "bthj,bhij->bthi", gloc, prefix_low, preferred_element_type=f32
    )
    key_grad = jnp.einsum("bhts,bthi->bshi", grads, qloc, preferred_element_type=f32)
    key_grad = key_grad + jnp.einsum(
        "bshj,bhij->bshi", vloc, suffix_low, preferred_element_type=f32
    )
    value_grad = jnp.einsum("bhts,bthj->bshj", attn, gloc, preferred_element_type=f32)
    value_grad = value_grad + jnp.einsum(
        "bshi,bhij->bshj", kloc, suffix_low, preferred_element_type=f32
    )
    flat = (count, heads * DH)
    return (
        attended.astype(jnp.bfloat16).reshape(flat),
        query_grad.astype(jnp.bfloat16).reshape(flat),
        key_grad.astype(jnp.bfloat16).reshape(flat),
        value_grad.astype(jnp.bfloat16).reshape(flat),
    )


def solution(mesh):
    in_specs = (P("ctx", "seq"), P("ctx", "seq"), P("ctx", "seq"), P("ctx", "seq"))
    out_specs = (P("ctx", "seq"), P("ctx", "seq"), P("ctx", "seq"), P("ctx", "seq"))
    return jax.shard_map(body, mesh=mesh, in_specs=in_specs, out_specs=out_specs, check_vma=False)
```

profile of v0, /device:TPU:0, one launch (start us, length us, event | category | flops | bytes accessed | tf_op | source)
XLA Modules:
  0.0 305.8 jit_solution(8850966653678798229)
XLA Ops:
  7.2 2.4 copy.98
  10.2 4.1 %fusion.21 = (f32[16,128,128]{2,1,0:T(8,128)}, f32[4,16,128,128]{3,2,1,0:T(8,128)}) fusion(bf16[4,128,16,128]{3,2,1,0:T(8,128)(2,1)S(1)} %bitcast.76, bf16[4,128,16,128]{3,2,1,0:T(8,128)(2,1)S(1)} %bitcast.80), kind=kOutput, calls=%fused_computation.36 | convolution fusion | flops 269221888 | bytes 9437184 | tf_op jit(solution)/shard_map/bthi,bthj->bhij/dot_general | solution.py:38
  14.5 3.7 %copy.100 = bf16[64,8,16,128]{3,2,1,0:T(8,128)(2,1)} copy(bf16[64,8,16,128]{3,1,2,0:T(8,128)(2,1)} %bitcast.97) | data formatting | bytes 4194304
  18.2 2.0 copy.96
  20.1 4.5 %copy.77 = bf16[4,128,16,128]{1,3,2,0:T(8,128)(2,1)} copy(bf16[4,128,16,128]{3,2,1,0:T(8,128)(2,1)} %bitcast.88) | data formatting | bytes 4194304 | tf_op jit(solution)/shard_map/reshape | solution.py:33
  24.6 6.4 %fusion.22 = (f32[16,128,128]{2,1,0:T(8,128)}, f32[4,16,128,128]{3,2,1,0:T(8,128)}) fusion(bf16[4,128,16,128]{1,3,2,0:T(8,128)(2,1)} %copy.77, bf16[4,128,16,128]{3,2,1,0:T(8,128)(2,1)} %bitcast.84), kind=kOutput, calls=%fused_computation.37 | convolution fusion | flops 269221888 | bytes 9437184 | tf_op jit(solution)/shard_map/bthi,bthj->bhij/dot_general | solution.py:39
  31.1 4.0 %select_convert_fusion.1 = bf16[4,16,128,128]{3,2,1,0:T(8,128)(2,1)S(1)} fusion(bf16[4,128,16,128]{1,3,2,0:T(8,128)(2,1)} %copy.77, pred[128,128]{1,0:T(8,128)(4,1)S(1)} %iota_compare_fusion, bf16[4,128,16,128]{3,2,1,0:T(8,128)(2,1)} %bitcast.81), kind=kOutput, calls=%fused_computation.13 | convolution fusion | flops 270532608 | bytes 6307840 | tf_op jit(solution)/shard_map/bthi,bshi->bhts/dot_general | solution.py:52
  35.1 1.6 select_convert_fusion
  36.7 2.8 fusion.14
  39.5 2.9 fusion.4
  42.4 2.7 fusion.18
  45.0 3.6 %fusion.23 = f32[4,16,128,128]{3,2,1,0:T(8,128)} fusion(bf16[4,16,128,128]{3,2,1,0:T(8,128)(2,1)S(1)} %select_convert_fusion, bf16[4,128,16,128]{1,3,2,0:T(8,128)(2,1)S(1)} %copy-done.3), kind=kOutput, calls=%fused_computation.38 | convolution fusion | flops 268435456 | bytes 8388608 | tf_op jit(solution)/shard_map/bhts,bthi->bshi/dot_general | solution.py:65
  48.6 93.6 %all-gather.5.cloned.1.call-done = f32[128,128,128]{2,1,0:T(8,128)} async-done(((f32[16,128,128]{2,1,0:T(8,128)}), f32[128,128,128]{2,1,0:T(8,128)}) %all-gather.5.cloned.1.call-update) | async-done | bytes 8388624 | tf_op jit(solution)/shard_map/all_gather | solution.py:14
  142.5 4.7 %add_convert_fusion.1 = bf16[4,16,128,128]{3,2,1,0:T(8,128)(2,1)S(1)} fusion(f32[4,16,128,128]{3,2,1,0:T(8,128)} %get-tuple-element.102, f32[16,128,128]{2,1,0:T(8,128)S(1)} %get-tuple-element.83), kind=kOutput, calls=%fused_computation.12 | output fusion | flops 6291456 | bytes 7340032 | tf_op jit(solution)/shard_map/body/reduce_window_sum | solution.py:44
  147.8 1.6 fusion.2
  149.4 2.7 copy.74
  153.0 2.7 copy.68
  155.7 111.8 %all-gather.7.cloned.1.call-done = f32[128,128,128]{2,1,0:T(8,128)} async-done(((f32[16,128,128]{2,1,0:T(8,128)}), f32[128,128,128]{2,1,0:T(8,128)}) %all-gather.7.cloned.1.call-update) | async-done | bytes 8388624 | tf_op jit(solution)/shard_map/all_gather | solution.py:14
  267.6 10.8 %while.23 = (s32[]{:T(128)}, f32[16,128,128]{2,1,0:T(8,128)S(1)}, s32[]{:T(128)}, f32[8,16,128,128]{3,2,1,0:T(8,128)}, s32[]{:T(128)}, /*index=5*/s32[]{:T(128)}, s32[]{:T(128)}, s32[]{:T(128)}) while((s32[]{:T(128)}, f32[16,128,128]{2,1,0:T(8,128)S(1)}, s32[]{:T(128)}, f32[8,16,128,128]{3,2,1,0:T(8,128)}, s32[]{:T(128)}, ...), condition=%wide.region_6.7_spmd, body=%wide.region_5.6_spmd.sunk | while | flops 262150 | bytes 3145871 | solution.py:21
  272.1 1.5 bitcast_add_fusion.9
  278.4 4.8 %add_convert_fusion = bf16[4,16,128,128]{3,2,1,0:T(8,128)(2,1)S(1)} fusion(f32[4,16,128,128]{3,2,1,0:T(8,128)} %get-tuple-element.104, f32[16,128,128]{2,1,0:T(8,128)S(1)} %get-tuple-element.84), kind=kOutput, calls=%fused_computation.10 | output fusion | flops 6291456 | bytes 7340032 | tf_op jit(solution)/shard_map/body/reduce_window_sum | solution.py:45
  286.8 1.6 fusion.1
  290.7 4.1 %copy_bitcast_fusion.2 = (bf16[512,2048]{1,0:T(8,128)(2,1)}, bf16[512,2048]{1,0:T(8,128)(2,1)}) fusion(bf16[64,8,16,128]{3,2,1,0:T(8,128)(2,1)S(1)} %bitcast.89, bf16[64,8,16,128]{3,2,1,0:T(8,128)(2,1)S(1)} %bitcast.90), kind=kLoop, calls=%fused_computation.16 | loop fusion | bytes 8388608 | tf_op jit(solution)/shard_map/reshape | solution.py:76
  294.8 4.1 %copy_bitcast_fusion = (bf16[512,2048]{1,0:T(8,128)(2,1)}, bf16[512,2048]{1,0:T(8,128)(2,1)}) fusion(bf16[64,8,16,128]{3,2,1,0:T(8,128)(2,1)S(1)} %bitcast.91, bf16[64,8,16,128]{3,2,1,0:T(8,128)(2,1)S(1)} %bitcast.92), kind=kLoop, calls=%fused_computation.14 | loop fusion | bytes 8388608 | tf_op jit(solution)/shard_map/reshape | solution.py:78
  (49 shorter events, 17.4 us)
Async XLA Ops:
  7.2 135.0 %all-gather.5.cloned.1.call-start = ((), (), s32[]{:S(2)}) async-start(), calls=%async_computation | async-start | bytes 9437184 | tf_op jit(solution)/shard_map/all_gather | solution.py:14
  7.2 2.4 copy-start.13
  10.2 4.2 %copy-start = (bf16[64,8,16,128]{3,2,1,0:T(8,128)(2,1)}, bf16[64,8,16,128]{3,2,1,0:T(8,128)(2,1)S(1)}, u32[]{:S(2)}) copy-start(bf16[64,8,16,128]{3,2,1,0:T(8,128)(2,1)S(1)} %copy.97) | copy-start | bytes 6291460
  14.4 253.1 %all-gather.7.cloned.1.call-start = ((), (), s32[]{:S(2)}) async-start(), calls=%async_computation.1 | async-start | bytes 9437184 | tf_op jit(solution)/shard_map/all_gather | solution.py:14
  14.5 3.7 %copy-start.14 = (bf16[512,2048]{1,0:T(8,128)(2,1)S(1)}, bf16[512,2048]{1,0:T(8,128)(2,1)}, u32[]{:S(2)}) copy-start(bf16[512,2048]{1,0:T(8,128)(2,1)} %param.8) | copy-start | bytes 6291460
  31.1 4.0 %copy-start.5 = (bf16[64,8,16,128]{3,2,1,0:T(8,128)(2,1)S(1)}, bf16[64,8,16,128]{3,2,1,0:T(8,128)(2,1)}, u32[]{:S(2)}) copy-start(bf16[64,8,16,128]{3,2,1,0:T(8,128)(2,1)} %copy.100) | copy-start | bytes 6291460
  39.5 2.9 copy-start.1
  42.4 2.7 copy-start.3
  142.5 4.7 %copy-start.6 = (bf16[64,8,16,128]{3,2,1,0:T(8,128)(2,1)S(1)}, bf16[64,8,16,128]{3,2,1,0:T(8,128)(2,1)}, u32[]{:S(2)}) copy-start(bf16[64,8,16,128]{3,2,1,0:T(8,128)(2,1)} %copy.100) | copy-start | bytes 6291460
  142.5 5.3 %copy-start.10 = (f32[4,16,128,128]{3,2,1,0:T(8,128)S(1)}, f32[4,16,128,128]{3,2,1,0:T(8,128)}, u32[]{:S(2)}) copy-start(f32[4,16,128,128]{3,2,1,0:T(8,128)} %fusion.18) | copy-start | bytes 12582916
  147.8 4.3 %copy-start.9 = (f32[4,16,128,128]{3,2,1,0:T(8,128)S(1)}, f32[4,16,128,128]{3,2,1,0:T(8,128)}, u32[]{:S(2)}) copy-start(f32[4,16,128,128]{3,2,1,0:T(8,128)} %fusion.14) | copy-start | bytes 12582916
  149.3 2.7 copy-start.4
  278.4 4.9 %copy-start.2 = (bf16[64,8,16,128]{3,2,1,0:T(8,128)(2,1)S(1)}, bf16[64,8,16,128]{3,2,1,0:T(8,128)(2,1)}, u32[]{:S(2)}) copy-start(bf16[64,8,16,128]{3,2,1,0:T(8,128)(2,1)} %copy-done) | copy-start | bytes 6291460
  278.4 5.3 %copy-start.8 = (f32[4,16,128,128]{3,2,1,0:T(8,128)S(1)}, f32[4,16,128,128]{3,2,1,0:T(8,128)}, u32[]{:S(2)}) copy-start(f32[4,16,128,128]{3,2,1,0:T(8,128)} %fusion.4) | copy-start | bytes 12582916
  284.7 2.2 copy-start.7
  288.5 1.6 copy-start.11
  288.5 2.2 copy-start.12
Sparse Core Ops, SparseCore 0:
  14.5 127.6 all-gather.4
  144.3 123.1 all-gather.6
where the time goes:
time: 306 us
  waiting for transfers between devices  205 us (67%)
  matrix products  33.2 us (11%)
  local copies, waits for them, and re-layouts  32.3 us (11%)
  other arithmetic  20 us (7%)
  between operations  14.3 us (5%)
    all_gather x2, waiting for transfers between devices, prefix(): gathered = lax.all_gather(part, axis)  205 us
    unnamed x34, local copies, waits for them, and re-layouts  11.3 us
    add x7, other arithmetic, add_states(): return earlier + later  10.4 us
    dot_general x1, matrix products, body(): jnp.einsum('bthi,bthj->bhij', qloc, gloc, preferred_element_type=f32)  6.43 us
  transfers between devices with their start and end apart: 2, of which 2 were waited for; matrix products, arithmetic and copies ran while one was open for 15% of the time, Pallas kernels for 0%

commit v1 on v0

v1 whole, which is shorter than its diff:
```python
import functools

import jax
import jax.numpy as jnp
from jax import lax
from jax.experimental import pallas as pl
from jax.experimental.pallas import tpu as pltpu
from jax.sharding import PartitionSpec as P

DH = 128
BLOCK = 128
F32 = jnp.float32
BF16 = jnp.bfloat16
ROWS = ((0,), (0,))
LANES = ((1,), (1,))
PLAIN = ((1,), (0,))


def dot(a, b, dims):
    return lax.dot_general(a, b, (dims, ((), ())), preferred_element_type=F32)


def states_kernel(q_ref, k_ref, v_ref, g_ref, out_ref):
    for h in range(out_ref.shape[1]):
        cols = slice(h * DH, (h + 1) * DH)
        out_ref[0, h] = dot(k_ref[:, cols], v_ref[:, cols], ROWS)
        out_ref[1, h] = dot(q_ref[:, cols], g_ref[:, cols], ROWS)


def states_of(arrays, first, size, step):
    rows = arrays[0].shape[0]
    spec = pl.BlockSpec((rows, step * DH), lambda i: (0, first // step + i))
    return pl.pallas_call(
        states_kernel,
        grid=(size // step,),
        in_specs=[spec] * 4,
        out_specs=pl.BlockSpec((2, step, DH, DH), lambda i: (0, i, 0, 0)),
        out_shape=jax.ShapeDtypeStruct((2, size, DH, DH), F32),
        name="states",
    )(*arrays)


def outputs_kernel(step, *refs):
    q_ref, k_ref, v_ref, g_ref, before_ref, after_ref = refs[:6]
    attended_ref, query_ref, key_ref, value_ref = refs[-4:]
    nblocks = q_ref.shape[0] // BLOCK
    rows = lax.broadcasted_iota(jnp.int32, (BLOCK, BLOCK), 0)
    cols = lax.broadcasted_iota(jnp.int32, (BLOCK, BLOCK), 1)
    causal = cols <= rows

    def scores(a, b):
        return jnp.where(causal, dot(a, b, LANES), 0.0).astype(BF16)

    for h in range(step):
        lanes = slice(h * DH, (h + 1) * DH)
        at = [(slice(b * BLOCK, (b + 1) * BLOCK), lanes) for b in range(nblocks)]
        lows = []
        state = before_ref[h]
        for b in range(nblocks):
            lows.append(state.astype(BF16))
            if b < nblocks - 1:
                state = state + dot(k_ref[at[b]], v_ref[at[b]], ROWS)
        for b in range(nblocks):
            q, k, v, g = q_ref[at[b]], k_ref[at[b]], v_ref[at[b]], g_ref[at[b]]
            low = lows[b]
            attn, grads = scores(q, k), scores(g, v)
            attended_ref[at[b]] = dot(
                jnp.concatenate([attn, q], 1), jnp.concatenate([v, low], 0), PLAIN
            ).astype(BF16)
            query_ref[at[b]] = dot(
                jnp.concatenate([grads, g], 1), jnp.concatenate([k, low.T], 0), PLAIN
            ).astype(BF16)
        state = after_ref[h]
        for b in reversed(range(nblocks)):
            q, k, v, g = q_ref[at[b]], k_ref[at[b]], v_ref[at[b]], g_ref[at[b]]
            low = state.astype(BF16)
            if b > 0:
                state = state + dot(q, g, ROWS)
            attn, grads = scores(q, k), scores(g, v)
            key_ref[at[b]] = dot(
                jnp.concatenate([grads.T, v], 1), jnp.concatenate([q, low.T], 0), PLAIN
            ).astype(BF16)
            value_ref[at[b]] = dot(
                jnp.concatenate([attn.T, k], 1), jnp.concatenate([g, low], 0), PLAIN
            ).astype(BF16)


def outputs_of(arrays, before, after, outs, first, size, step):
    rows = arrays[0].shape[0]
    spec = pl.BlockSpec((rows, step * DH), lambda i: (0, first // step + i))
    state = pl.BlockSpec((step, DH, DH), lambda i: (i, 0, 0))
    held = () if outs is None else tuple(outs)
    return pl.pallas_call(
        functools.partial(outputs_kernel, step),
        grid=(size // step,),
        in_specs=[spec] * 4 + [state] * 2 + [pl.BlockSpec(memory_space=pl.ANY)] * len(held),
        out_specs=[spec] * 4,
        out_shape=[jax.ShapeDtypeStruct(a.shape, BF16) for a in arrays],
        input_output_aliases={6 + i: i for i in range(len(held))},
        name="outputs",
    )(*arrays, before, after, *held)


def any_of(place, places):
    return functools.reduce(jnp.logical_or, [place == p for p in places])


def body(*arrays):
    heads = arrays[0].shape[1] // DH
    runs = lax.axis_size("ctx")
    chain = runs // 2
    place = lax.axis_index("ctx")
    row, column = place // 2, place % 2
    parts = 4
    size = heads // parts
    own = [None] * parts
    for p in (2, 0, 1, 3):
        own[p] = states_of(arrays, p * size, size, min(size, 2))
    pair = [(r, r ^ 1) for r in range(runs)]
    swapped = [None] * parts
    swapped[2] = lax.ppermute(own[2], "ctx", pair)
    swapped[3] = lax.ppermute(own[3], "ctx", pair)

    def along(p):
        return own[p] if p < 2 else own[p] + swapped[p]

    carried = [along(p) for p in range(parts)]
    got = {}

    def arrival(p, z, way):
        if way == 0:
            return None if z == 0 else ((z - 1) % 2, p + z - 1)
        return None if z == chain - 1 else (z % 2, p + chain - 2 - z)

    def chained(p, way):
        total = jnp.zeros_like(own[p][0])
        by_key = {}
        for z in range(chain):
            key = arrival(p, z, way)
            if key is not None:
                by_key.setdefault(key, []).append(z)
        for key, places in by_key.items():
            total = jnp.where(any_of(row, places), got[key], total)
        return total

    for slot in range(parts + chain - 2):
        for parity in range(2):
            groups, perm = {}, []
            for link in range(parity, chain - 1, 2):
                for way, p, z, to in ((0, slot - link, link, link + 1), (1, slot - (chain - 2 - link), link + 1, link)):
                    if 0 <= p < parts:
                        groups.setdefault((p, arrival(p, z, way)), {}).setdefault(way, []).append(z)
                        perm += [(2 * z + c, 2 * to + c) for c in range(2)]
            if not perm:
                continue
            payload = None
            for (p, key), ways in groups.items():
                if len(ways) == 2:
                    value = jnp.where(any_of(row, ways[0]), carried[p][0], carried[p][1])
                else:
                    value = carried[p][next(iter(ways))]
                if key is not None:
                    value = value + got[key]
                places = [z for zs in ways.values() for z in zs]
                payload = value if payload is None else jnp.where(any_of(row, places), value, payload)
            got[parity, slot] = lax.ppermute(payload, "ctx", perm)

    outs = None
    for p in (0, 2, 1, 3):
        before, after = chained(p, 0), chained(p, 1)
        if p < 2:
            first = jnp.where(column == 0, own[p][0], 0.0)
            second = jnp.where(column == 1, own[p][1], 0.0)
            swapped[p] = lax.ppermute(jnp.stack([before + first, after + second]), "ctx", pair)
            before, after = before + swapped[p][0], after + swapped[p][1]
        else:
            before = before + jnp.where(column == 1, swapped[p][0], 0.0)
            after = after + jnp.where(column == 0, swapped[p][1], 0.0)
        outs = outputs_of(arrays, before, after, outs, p * size, size, 1)
    return tuple(outs)


def solution(mesh):
    spec = P("ctx", "seq")
    return jax.shard_map(body, mesh=mesh, in_specs=(spec,) * 4, out_specs=(spec,) * 4, check_vma=False)
```

time: 306 us -> 113 us (0.37)
  waiting for transfers between devices: 205 us -> 26.9 us
  Pallas kernels: 0 us -> 46.8 us
  matrix products: 33.2 us -> 0 us
  local copies, waits for them, and re-layouts: 32.3 us -> 0.04 us
  starting transfers between devices: 0.08 us -> 25.6 us
  between operations: 14.3 us -> 0.83 us
  other arithmetic: 20 us -> 12.6 us
    all_gather x2 -> x0, waiting for transfers between devices: 205 us -> none  [prefix(): gathered = lax.all_gather(part, axis)]
    pallas_call x0 -> x8, Pallas kernels: none -> 46.8 us  [the longest x4 36.2 us: outputs_of(): pl.pallas_call(functools.partial(outputs_kernel, step), grid=(size // ste...]
    dot_general x12 -> x0, matrix products: 33.2 us -> none  [the longest x1 6.43 us: body(): jnp.einsum('bthi,bthj->bhij', qloc, gloc, preferred_element_type=f32)]
    ppermute x0 -> x14, waiting for transfers between devices: none -> 26.9 us  [the longest x10 14.6 us: body(): got[parity, slot] = lax.ppermute(payload, 'ctx', perm)]
    ppermute x0 -> x14, starting transfers between devices: none -> 25.6 us  [the longest x10 20.4 us: body(): got[parity, slot] = lax.ppermute(payload, 'ctx', perm)]
    reshape x3 -> x0, local copies, waits for them, and re-layouts: 12.7 us -> none  [the longest x1 4.49 us: body(): qloc = queries.reshape(shape)]
    unnamed x34 -> x18, local copies, waits for them, and re-layouts: 11.3 us -> 0.04 us
    convert_element_type x4 -> x0, local copies, waits for them, and re-layouts: 8.06 us -> none  [the longest x1 2.67 us: body(): query_grad.astype(jnp.bfloat16).reshape(flat)]
  transfers between devices with their start and end apart: 2 -> 14, of which waited for: 2 -> 8; matrix products, arithmetic and copies ran while one was open for 15% -> 9% of each run, Pallas kernels for 0% -> 23%
where the time goes in v1:
time: 113 us
  Pallas kernels  46.8 us (41%)
  waiting for transfers between devices  26.9 us (24%)
  starting transfers between devices  25.6 us (23%)
  other arithmetic  12.6 us (11%)
    pallas_call x4, Pallas kernels, outputs_of(): pl.pallas_call(functools.partial(outputs_kernel, step), grid=(size // ste...  36.2 us
    ppermute x10, starting transfers between devices, body(): got[parity, slot] = lax.ppermute(payload, 'ctx', perm)  20.4 us
    ppermute x10, waiting for transfers between devices, body(): got[parity, slot] = lax.ppermute(payload, 'ctx', perm)  14.6 us
    pallas_call x4, Pallas kernels, states_of(): pl.pallas_call(states_kernel, grid=(size // step,), in_specs=[spec] * 4,...  10.6 us
    ppermute x2, waiting for transfers between devices, body(): lax.ppermute(jnp.stack([before + first, after + second]), 'ctx', pair)  8.18 us
    another operation x4, other arithmetic, body(): jnp.stack([before + first, after + second])  4.3 us
    add x6, other arithmetic, body(): value = value + got[key]  3.46 us
    ppermute x2, starting transfers between devices, body(): lax.ppermute(jnp.stack([before + first, after + second]), 'ctx', pair)  3.16 us
  transfers between devices with their start and end apart: 14, of which 8 were waited for; matrix products, arithmetic and copies ran while one was open for 9% of the time, Pallas kernels for 23%

profile of v1, /device:TPU:0, one launch (start us, length us, event | category | flops | bytes accessed | tf_op | source)
XLA Modules:
  0.0 112.8 jit_solution(3263745992272430946)
XLA Ops:
  0.6 2.6 %states.7 = f32[2,4,128,128]{3,2,1,0:T(8,128)} custom-call(bf16[512,2048]{1,0:T(8,128)(2,1)} %refs_0_.7, bf16[512,2048]{1,0:T(8,128)(2,1)} %refs_1_.7, bf16[512,2048]{1,0:T(8,128)(2,1)} %refs_2_.7, bf16[512,2048]{1,0:T(8,128)(2,1)} %refs_3_.7), custom_call_target="tpu_custom_call" | custom-call | tf_op jit(solution)/shard_map/states/pallas_call | solution.py:33
  4.4 4.9 %collective-permute-start.8 = (f32[4,128,128]{2,1,0:T(8,128)S(1)}, f32[4,128,128]{2,1,0:T(8,128)S(1)}, u32[]{:S(2)}, u32[]{:S(2)}) collective-permute-start(f32[4,128,128]{2,1,0:T(8,128)S(1)} %select_bitcast_fusion), channel_id=1, source_target_pairs={{0,8},{4,12},{24,16},{28,20},{1,9},{5,13},{25,17},{29,21},{2,10},{... | collective-permute-start | bytes 786440 | tf_op jit(solution)/shard_map/ppermute | solution.py:166
  9.3 2.7 %states.6 = f32[2,4,128,128]{3,2,1,0:T(8,128)} custom-call(bf16[512,2048]{1,0:T(8,128)(2,1)} %refs_0_.7, bf16[512,2048]{1,0:T(8,128)(2,1)} %refs_1_.7, bf16[512,2048]{1,0:T(8,128)(2,1)} %refs_2_.7, bf16[512,2048]{1,0:T(8,128)(2,1)} %refs_3_.7), custom_call_target="tpu_custom_call" | custom-call | tf_op jit(solution)/shard_map/states/pallas_call | solution.py:33
  12.0 1.5 %collective-permute-start.7 = (f32[2,4,128,128]{3,2,1,0:T(8,128)}, f32[2,4,128,128]{3,2,1,0:T(8,128)S(1)}, u32[]{:S(2)}, u32[]{:S(2)}) collective-permute-start(f32[2,4,128,128]{3,2,1,0:T(8,128)} %states.6), channel_id=1, source_target_pairs={{0,4},{4,0},{8,12},{12,8},{16,20},{20,16},{24,28},{28,24},{1,5},{5... | collective-permute-start | bytes 1572872 | tf_op jit(solution)/shard_map/ppermute | solution.py:121
  13.5 2.6 %states.5 = f32[2,4,128,128]{3,2,1,0:T(8,128)} custom-call(bf16[512,2048]{1,0:T(8,128)(2,1)} %refs_0_.7, bf16[512,2048]{1,0:T(8,128)(2,1)} %refs_1_.7, bf16[512,2048]{1,0:T(8,128)(2,1)} %refs_2_.7, bf16[512,2048]{1,0:T(8,128)(2,1)} %refs_3_.7), custom_call_target="tpu_custom_call" | custom-call | tf_op jit(solution)/shard_map/states/pallas_call | solution.py:33
  16.1 1.8 %select_bitcast_fusion.1 = f32[4,128,128]{2,1,0:T(8,128)} fusion(f32[2,4,128,128]{3,2,1,0:T(8,128)} %states.5, pred[]{:T(512)S(6)} %eq.17), kind=kLoop, calls=%fused_computation.45 | loop fusion | flops 65536 | bytes 786433 | tf_op jit(solution)/shard_map/jit(_where)/select_n | solution.py:159
  17.9 1.4 %collective-permute-start.1 = (f32[4,128,128]{2,1,0:T(8,128)}, f32[4,128,128]{2,1,0:T(8,128)S(1)}, u32[]{:S(2)}, u32[]{:S(2)}) collective-permute-start(f32[4,128,128]{2,1,0:T(8,128)} %select_bitcast_fusion.1), channel_id=1, source_target_pairs={{0,8},{4,12},{24,16},{28,20},{1,9},{5,13},{25,17},{29,21},{2,10},{... | collective-permute-start | bytes 786440 | tf_op jit(solution)/shard_map/ppermute | solution.py:166
  19.3 2.7 %states.4 = f32[2,4,128,128]{3,2,1,0:T(8,128)} custom-call(bf16[512,2048]{1,0:T(8,128)(2,1)} %refs_0_.7, bf16[512,2048]{1,0:T(8,128)(2,1)} %refs_1_.7, bf16[512,2048]{1,0:T(8,128)(2,1)} %refs_2_.7, bf16[512,2048]{1,0:T(8,128)(2,1)} %refs_3_.7), custom_call_target="tpu_custom_call" | custom-call | tf_op jit(solution)/shard_map/states/pallas_call | solution.py:33
  25.6 1.4 %collective-permute-done.7 = f32[2,4,128,128]{3,2,1,0:T(8,128)S(1)} collective-permute-done((f32[2,4,128,128]{3,2,1,0:T(8,128)}, f32[2,4,128,128]{3,2,1,0:T(8,128)S(1)}, u32[]{:S(2)}, u32[]{:S(2)}) %collective-permute-start.7) | collective-permute-done | bytes 524320 | tf_op jit(solution)/shard_map/ppermute | solution.py:121
  27.2 6.9 %collective-permute-start.10 = (f32[4,128,128]{2,1,0:T(8,128)S(1)}, f32[4,128,128]{2,1,0:T(8,128)S(1)}, u32[]{:S(2)}, u32[]{:S(2)}) collective-permute-start(f32[4,128,128]{2,1,0:T(8,128)S(1)} %bitcast_select_fusion), channel_id=1, source_target_pairs={{0,8},{4,12},{8,0},{12,4},{16,24},{20,28},{24,16},{28,20},{1,9},{5... | collective-permute-start | bytes 786440 | tf_op jit(solution)/shard_map/ppermute | solution.py:166
  34.2 2.6 %collective-permute-done = f32[2,4,128,128]{3,2,1,0:T(8,128)S(1)} collective-permute-done((f32[2,4,128,128]{3,2,1,0:T(8,128)}, f32[2,4,128,128]{3,2,1,0:T(8,128)S(1)}, u32[]{:S(2)}, u32[]{:S(2)}) %collective-permute-start) | collective-permute-done | bytes 524320 | tf_op jit(solution)/shard_map/ppermute | solution.py:122
  38.0 1.6 %collective-permute-done.10 = f32[4,128,128]{2,1,0:T(8,128)S(1)} collective-permute-done((f32[4,128,128]{2,1,0:T(8,128)S(1)}, f32[4,128,128]{2,1,0:T(8,128)S(1)}, u32[]{:S(2)}, u32[]{:S(2)}) %collective-permute-start.10) | collective-permute-done | bytes 262176 | tf_op jit(solution)/shard_map/ppermute | solution.py:166
  40.4 3.8 %collective-permute-done.3 = f32[4,128,128]{2,1,0:T(8,128)S(1)} collective-permute-done((f32[4,128,128]{2,1,0:T(8,128)S(1)}, f32[4,128,128]{2,1,0:T(8,128)S(1)}, u32[]{:S(2)}, u32[]{:S(2)}) %collective-permute-start.3) | collective-permute-done | bytes 262176 | tf_op jit(solution)/shard_map/ppermute | solution.py:166
  50.9 6.8 %collective-permute-done.12 = f32[4,128,128]{2,1,0:T(8,128)} collective-permute-done((f32[4,128,128]{2,1,0:T(8,128)}, f32[4,128,128]{2,1,0:T(8,128)}, u32[]{:S(2)}, u32[]{:S(2)}) %collective-permute-start.12) | collective-permute-done | bytes 262176 | tf_op jit(solution)/shard_map/ppermute | solution.py:166
  57.7 2.2 %fusion.12 = (f32[1,4,128,128]{3,2,1,0:T(8,128)S(1)}, f32[4,128,128]{2,1,0:T(8,128)S(1)}, f32[1,4,128,128]{3,2,1,0:T(8,128)S(1)}, f32[4,128,128]{2,1,0:T(8,128)S...) fusion(f32[2,4,128,128]{3,2,1,0:T(8,128)S(1)} %copy-done.1, pred[]{:T(512)S(6)} %eq.18, f32[4,128,128]{2,1,0:T(8,128)} %copy-done.4, ...), kind=kLoop, calls=%fused_computation.23 | loop fusion | flops 1310720 | bytes 3932166 | tf_op jit(solution)/shard_map/stack | solution.py:174
  60.0 1.6 %collective-permute-start.13 = (f32[2,4,128,128]{3,2,1,0:T(8,128)S(1)}, f32[2,4,128,128]{3,2,1,0:T(8,128)S(1)}, u32[]{:S(2)}, u32[]{:S(2)}) collective-permute-start(f32[2,4,128,128]{3,2,1,0:T(8,128)S(1)} %pad_maximum_fusion.1), channel_id=1, source_target_pairs={{0,4},{4,0},{8,12},{12,8},{16,20},{20,16},{24,28},{28,24},{1,5},{5... | collective-permute-start | bytes 1572872 | tf_op jit(solution)/shard_map/ppermute | solution.py:174
  61.6 1.5 %collective-permute-done.5 = f32[4,128,128]{2,1,0:T(8,128)S(1)} collective-permute-done((f32[4,128,128]{2,1,0:T(8,128)S(1)}, f32[4,128,128]{2,1,0:T(8,128)S(1)}, u32[]{:S(2)}, u32[]{:S(2)}) %collective-permute-start.5) | collective-permute-done | bytes 262176 | tf_op jit(solution)/shard_map/ppermute | solution.py:166
  63.1 2.0 %fusion.14 = (f32[1,4,128,128]{3,2,1,0:T(8,128)S(1)}, f32[4,128,128]{2,1,0:T(8,128)S(1)}, f32[1,4,128,128]{3,2,1,0:T(8,128)S(1)}, f32[4,128,128]{2,1,0:T(8,128)S...) fusion(f32[2,4,128,128]{3,2,1,0:T(8,128)S(1)} %copy-done, pred[]{:T(512)S(6)} %eq.18, ...), kind=kLoop, calls=%fused_computation.32 | loop fusion | flops 1310720 | bytes 3932166 | tf_op jit(solution)/shard_map/stack | solution.py:174
  65.1 1.6 %collective-permute-start.6 = (f32[2,4,128,128]{3,2,1,0:T(8,128)S(1)}, f32[2,4,128,128]{3,2,1,0:T(8,128)S(1)}, u32[]{:S(2)}, u32[]{:S(2)}) collective-permute-start(f32[2,4,128,128]{3,2,1,0:T(8,128)S(1)} %pad_maximum_fusion), channel_id=1, source_target_pairs={{0,4},{4,0},{8,12},{12,8},{16,20},{20,16},{24,28},{28,24},{1,5},{5... | collective-permute-start | bytes 1572872 | tf_op jit(solution)/shard_map/ppermute | solution.py:174
  66.7 8.2 %collective-permute-done.13 = f32[2,4,128,128]{3,2,1,0:T(8,128)S(1)} collective-permute-done((f32[2,4,128,128]{3,2,1,0:T(8,128)S(1)}, f32[2,4,128,128]{3,2,1,0:T(8,128)S(1)}, u32[]{:S(2)}, u32[]{:S(2)}) %collective-permute-start.13) | collective-permute-done | bytes 524320 | tf_op jit(solution)/shard_map/ppermute | solution.py:174
  75.8 9.0 %outputs.4 = (bf16[512,2048]{1,0:T(8,128)(2,1)}, bf16[512,2048]{1,0:T(8,128)(2,1)}, bf16[512,2048]{1,0:T(8,128)(2,1)}, bf16[512,2048]{1,0:T(8,128)(2,1)}) custom-call(bf16[512,2048]{1,0:T(8,128)(2,1)} %refs_0_.7, bf16[512,2048]{1,0:T(8,128)(2,1)} %refs_1_.7, bf16[512,2048]{1,0:T(8,128)(2,1)} %refs_2_.7, bf16[512,2048]{1,0:T(8,128)(2,1)} %refs_3_.7, ...), custom_call_target="tpu_custom_call" | custom-call | tf_op jit(solution)/shard_map/outputs/pallas_call | solution.py:93
  84.8 9.0 %outputs.5 = (bf16[512,2048]{1,0:T(8,128)(2,1)}, bf16[512,2048]{1,0:T(8,128)(2,1)}, bf16[512,2048]{1,0:T(8,128)(2,1)}, bf16[512,2048]{1,0:T(8,128)(2,1)}) custom-call(bf16[512,2048]{1,0:T(8,128)(2,1)} %refs_0_.7, bf16[512,2048]{1,0:T(8,128)(2,1)} %refs_1_.7, ...), custom_call_target="tpu_custom_call", output_to_operand_aliasing={{0}: (6, {}), {1}: (7, {}), {2}: (8, {}), {3}: (9, {})} | custom-call | tf_op jit(solution)/shard_map/outputs/pallas_call | solution.py:93
  94.7 9.0 %outputs.6 = (bf16[512,2048]{1,0:T(8,128)(2,1)}, bf16[512,2048]{1,0:T(8,128)(2,1)}, bf16[512,2048]{1,0:T(8,128)(2,1)}, bf16[512,2048]{1,0:T(8,128)(2,1)}) custom-call(bf16[512,2048]{1,0:T(8,128)(2,1)} %refs_0_.7, bf16[512,2048]{1,0:T(8,128)(2,1)} %refs_1_.7, ...), custom_call_target="tpu_custom_call", output_to_operand_aliasing={{0}: (6, {}), {1}: (7, {}), {2}: (8, {}), {3}: (9, {})} | custom-call | tf_op jit(solution)/shard_map/outputs/pallas_call | solution.py:93
  103.8 9.0 %outputs.7 = (bf16[512,2048]{1,0:T(8,128)(2,1)}, bf16[512,2048]{1,0:T(8,128)(2,1)}, bf16[512,2048]{1,0:T(8,128)(2,1)}, bf16[512,2048]{1,0:T(8,128)(2,1)}) custom-call(bf16[512,2048]{1,0:T(8,128)(2,1)} %refs_0_.7, bf16[512,2048]{1,0:T(8,128)(2,1)} %refs_1_.7, ...), custom_call_target="tpu_custom_call", output_to_operand_aliasing={{0}: (6, {}), {1}: (7, {}), {2}: (8, {}), {3}: (9, {})} | custom-call | tf_op jit(solution)/shard_map/outputs/pallas_call | solution.py:93
  (48 shorter events, 15.2 us)
Async XLA Ops:
  4.4 18.2 %collective-permute-start.8 = (f32[4,128,128]{2,1,0:T(8,128)S(1)}, f32[4,128,128]{2,1,0:T(8,128)S(1)}, u32[]{:S(2)}, u32[]{:S(2)}) collective-permute-start(f32[4,128,128]{2,1,0:T(8,128)S(1)} %select_bitcast_fusion), channel_id=1, source_target_pairs={{0,8},{4,12},{24,16},{28,20},{1,9},{5,13},{25,17},{29,21},{2,10},{... | collective-permute-start | bytes 786440 | tf_op jit(solution)/shard_map/ppermute | solution.py:166
  12.0 15.1 %collective-permute-start.7 = (f32[2,4,128,128]{3,2,1,0:T(8,128)}, f32[2,4,128,128]{3,2,1,0:T(8,128)S(1)}, u32[]{:S(2)}, u32[]{:S(2)}) collective-permute-start(f32[2,4,128,128]{3,2,1,0:T(8,128)} %states.6), channel_id=1, source_target_pairs={{0,4},{4,0},{8,12},{12,8},{16,20},{20,16},{24,28},{28,24},{1,5},{5... | collective-permute-start | bytes 1572872 | tf_op jit(solution)/shard_map/ppermute | solution.py:121
  17.9 4.6 %copy-start.1 = (f32[2,4,128,128]{3,2,1,0:T(8,128)S(1)}, f32[2,4,128,128]{3,2,1,0:T(8,128)}, u32[]{:S(2)}) copy-start(f32[2,4,128,128]{3,2,1,0:T(8,128)} %states.7) | copy-start | bytes 1572868
  17.9 7.0 %copy-start = (f32[2,4,128,128]{3,2,1,0:T(8,128)S(1)}, f32[2,4,128,128]{3,2,1,0:T(8,128)}, u32[]{:S(2)}) copy-start(f32[2,4,128,128]{3,2,1,0:T(8,128)} %states.5) | copy-start | bytes 1572868
  17.9 7.0 %collective-permute-start.1 = (f32[4,128,128]{2,1,0:T(8,128)}, f32[4,128,128]{2,1,0:T(8,128)S(1)}, u32[]{:S(2)}, u32[]{:S(2)}) collective-permute-start(f32[4,128,128]{2,1,0:T(8,128)} %select_bitcast_fusion.1), channel_id=1, source_target_pairs={{0,8},{4,12},{24,16},{28,20},{1,9},{5,13},{25,17},{29,21},{2,10},{... | collective-permute-start | bytes 786440 | tf_op jit(solution)/shard_map/ppermute | solution.py:166
  22.0 5.1 %copy-start.3 = (f32[2,4,128,128]{3,2,1,0:T(8,128)S(1)}, f32[2,4,128,128]{3,2,1,0:T(8,128)}, u32[]{:S(2)}) copy-start(f32[2,4,128,128]{3,2,1,0:T(8,128)} %states.6) | copy-start | bytes 1572868
  22.0 14.8 %collective-permute-start = (f32[2,4,128,128]{3,2,1,0:T(8,128)}, f32[2,4,128,128]{3,2,1,0:T(8,128)S(1)}, u32[]{:S(2)}, u32[]{:S(2)}) collective-permute-start(f32[2,4,128,128]{3,2,1,0:T(8,128)} %states.4), channel_id=1, source_target_pairs={{0,4},{4,0},{8,12},{12,8},{16,20},{20,16},{24,28},{28,24},{1,5},{5... | collective-permute-start | bytes 1572872 | tf_op jit(solution)/shard_map/ppermute | solution.py:122
  22.5 2.4 %copy-start.4 = (f32[4,128,128]{2,1,0:T(8,128)}, f32[4,128,128]{2,1,0:T(8,128)S(1)}, u32[]{:S(2)}) copy-start(f32[4,128,128]{2,1,0:T(8,128)S(1)} %collective-permute-done.8) | copy-start | bytes 786436
  23.3 3.8 %collective-permute-start.9 = (f32[4,128,128]{2,1,0:T(8,128)}, f32[4,128,128]{2,1,0:T(8,128)S(1)}, u32[]{:S(2)}, u32[]{:S(2)}) collective-permute-start(f32[4,128,128]{2,1,0:T(8,128)} %bitcast_add_fusion.2), channel_id=1, source_target_pairs={{8,16},{12,20},{16,8},{20,12},{9,17},{13,21},{17,9},{21,13},{10,18... | collective-permute-start | bytes 786440 | tf_op jit(solution)/shard_map/ppermute | solution.py:166
  24.0 12.8 %copy-start.2 = (f32[2,4,128,128]{3,2,1,0:T(8,128)S(1)}, f32[2,4,128,128]{3,2,1,0:T(8,128)}, u32[]{:S(2)}) copy-start(f32[2,4,128,128]{3,2,1,0:T(8,128)} %states.4) | copy-start | bytes 1572868
  24.9 12.0 %collective-permute-start.2 = (f32[4,128,128]{2,1,0:T(8,128)S(1)}, f32[4,128,128]{2,1,0:T(8,128)S(1)}, u32[]{:S(2)}, u32[]{:S(2)}) collective-permute-start(f32[4,128,128]{2,1,0:T(8,128)S(1)} %bitcast_add_fusion.8), channel_id=1, source_target_pairs={{8,16},{12,20},{16,8},{20,12},{9,17},{13,21},{17,9},{21,13},{10,18... | collective-permute-start | bytes 786440 | tf_op jit(solution)/shard_map/ppermute | solution.py:166
  27.2 12.4 %collective-permute-start.10 = (f32[4,128,128]{2,1,0:T(8,128)S(1)}, f32[4,128,128]{2,1,0:T(8,128)S(1)}, u32[]{:S(2)}, u32[]{:S(2)}) collective-permute-start(f32[4,128,128]{2,1,0:T(8,128)S(1)} %bitcast_select_fusion), channel_id=1, source_target_pairs={{0,8},{4,12},{8,0},{12,4},{16,24},{20,28},{24,16},{28,20},{1,9},{5... | collective-permute-start | bytes 786440 | tf_op jit(solution)/shard_map/ppermute | solution.py:166
  37.0 7.2 %collective-permute-start.3 = (f32[4,128,128]{2,1,0:T(8,128)S(1)}, f32[4,128,128]{2,1,0:T(8,128)S(1)}, u32[]{:S(2)}, u32[]{:S(2)}) collective-permute-start(f32[4,128,128]{2,1,0:T(8,128)S(1)} %bitcast_select_fusion.1), channel_id=1, source_target_pairs={{0,8},{4,12},{8,0},{12,4},{16,24},{20,28},{24,16},{28,20},{1,9},{5... | collective-permute-start | bytes 786440 | tf_op jit(solution)/shard_map/ppermute | solution.py:166
  39.6 7.5 %copy-start.7 = (f32[4,128,128]{2,1,0:T(8,128)}, f32[4,128,128]{2,1,0:T(8,128)S(1)}, u32[]{:S(2)}) copy-start(f32[4,128,128]{2,1,0:T(8,128)S(1)} %collective-permute-done.10) | copy-start | bytes 786436
  39.7 6.6 %collective-permute-start.11 = (f32[4,128,128]{2,1,0:T(8,128)S(1)}, f32[4,128,128]{2,1,0:T(8,128)S(1)}, u32[]{:S(2)}, u32[]{:S(2)}) collective-permute-start(f32[4,128,128]{2,1,0:T(8,128)S(1)} %bitcast_add_fusion.4), channel_id=1, source_target_pairs={{8,16},{12,20},{16,8},{20,12},{9,17},{13,21},{17,9},{21,13},{10,18... | collective-permute-start | bytes 786440 | tf_op jit(solution)/shard_map/ppermute | solution.py:166
  44.1 3.0 %copy-start.5 = (f32[4,128,128]{2,1,0:T(8,128)}, f32[4,128,128]{2,1,0:T(8,128)S(1)}, u32[]{:S(2)}) copy-start(f32[4,128,128]{2,1,0:T(8,128)S(1)} %collective-permute-done.3) | copy-start | bytes 786436
  44.9 3.5 %collective-permute-start.4 = (f32[4,128,128]{2,1,0:T(8,128)}, f32[4,128,128]{2,1,0:T(8,128)}, u32[]{:S(2)}, u32[]{:S(2)}) collective-permute-start(f32[4,128,128]{2,1,0:T(8,128)} %bitcast_add_fusion.10), channel_id=1, source_target_pairs={{8,16},{12,20},{16,8},{20,12},{9,17},{13,21},{17,9},{21,13},{10,18... | collective-permute-start | bytes 786440 | tf_op jit(solution)/shard_map/ppermute | solution.py:166
  46.3 0.8 copy-start.8
  47.1 10.6 %collective-permute-start.12 = (f32[4,128,128]{2,1,0:T(8,128)}, f32[4,128,128]{2,1,0:T(8,128)}, u32[]{:S(2)}, u32[]{:S(2)}) collective-permute-start(f32[4,128,128]{2,1,0:T(8,128)} %bitcast_add_fusion.5), channel_id=1, source_target_pairs={{8,0},{12,4},{16,24},{20,28},{9,1},{13,5},{17,25},{21,29},{10,2},{... | collective-permute-start | bytes 786440 | tf_op jit(solution)/shard_map/ppermute | solution.py:166
  49.4 13.6 %copy-start.6 = (f32[4,128,128]{2,1,0:T(8,128)S(1)}, f32[4,128,128]{2,1,0:T(8,128)}, u32[]{:S(2)}) copy-start(f32[4,128,128]{2,1,0:T(8,128)} %copy-done.5) | copy-start | bytes 786436
  49.5 13.6 %collective-permute-start.5 = (f32[4,128,128]{2,1,0:T(8,128)S(1)}, f32[4,128,128]{2,1,0:T(8,128)S(1)}, u32[]{:S(2)}, u32[]{:S(2)}) collective-permute-start(f32[4,128,128]{2,1,0:T(8,128)S(1)} %bitcast_add_fusion.11), channel_id=1, source_target_pairs={{8,0},{12,4},{16,24},{20,28},{9,1},{13,5},{17,25},{21,29},{10,2},{... | collective-permute-start | bytes 786440 | tf_op jit(solution)/shard_map/ppermute | solution.py:166
  60.0 14.9 %collective-permute-start.13 = (f32[2,4,128,128]{3,2,1,0:T(8,128)S(1)}, f32[2,4,128,128]{3,2,1,0:T(8,128)S(1)}, u32[]{:S(2)}, u32[]{:S(2)}) collective-permute-start(f32[2,4,128,128]{3,2,1,0:T(8,128)S(1)} %pad_maximum_fusion.1), channel_id=1, source_target_pairs={{0,4},{4,0},{8,12},{12,8},{16,20},{20,16},{24,28},{28,24},{1,5},{5... | collective-permute-start | bytes 1572872 | tf_op jit(solution)/shard_map/ppermute | solution.py:174
  65.1 28.7 %collective-permute-start.6 = (f32[2,4,128,128]{3,2,1,0:T(8,128)S(1)}, f32[2,4,128,128]{3,2,1,0:T(8,128)S(1)}, u32[]{:S(2)}, u32[]{:S(2)}) collective-permute-start(f32[2,4,128,128]{3,2,1,0:T(8,128)S(1)} %pad_maximum_fusion), channel_id=1, source_target_pairs={{0,4},{4,0},{8,12},{12,8},{16,20},{20,16},{24,28},{28,24},{1,5},{5... | collective-permute-start | bytes 1572872 | tf_op jit(solution)/shard_map/ppermute | solution.py:174

commit v2 on v0

v2 whole, which is shorter than its diff:
```python
import functools

import jax
import jax.numpy as jnp
from jax import lax
from jax.experimental import pallas as pl
from jax.experimental.pallas import tpu as pltpu
from jax.sharding import PartitionSpec as P

DH = 128
F32 = jnp.float32
BF16 = jnp.bfloat16
ROWS = ((0,), (0,))
LANES = ((1,), (1,))
PLAIN = ((1,), (0,))
VMEM = pl.BlockSpec(memory_space=pltpu.VMEM)
HBM = pl.BlockSpec(memory_space=pltpu.HBM)
PARAMS = pltpu.CompilerParams(vmem_limit_bytes=8 << 20)


def dot(a, b, dims):
    return lax.dot_general(a, b, (dims, ((), ())), preferred_element_type=F32)


def kept(arrays):
    return [pltpu.with_memory_space_constraint(a, pltpu.VMEM) for a in arrays]


def any_of(place, places):
    return functools.reduce(jnp.logical_or, [place == p for p in places])


def spot():
    place = lax.axis_index("ctx")
    return place // 2, place % 2


def load_kernel(first, chain, q_hbm, k_hbm, v_hbm, g_hbm, *refs):
    q_ref, k_ref, v_ref, g_ref, state_ref, opening_ref, sems = refs[-7:]
    size = state_ref.shape[1]
    moves = []
    for h in range(size):
        here, there = pl.ds(h * DH, DH), pl.ds((first + h) * DH, DH)
        pairs = ((k_hbm, k_ref), (v_hbm, v_ref), (q_hbm, q_ref), (g_hbm, g_ref))
        for i, (src, dst) in enumerate(pairs):
            moves.append(pltpu.make_async_copy(src.at[:, there], dst.at[:, here], sems.at[h, i]))
    for move in moves:
        move.start()
    row, _ = spot()
    for h in range(size):
        for move in moves[4 * h : 4 * h + 4]:
            move.wait()
        cols = slice(h * DH, (h + 1) * DH)
        kv, qg = dot(k_ref[:, cols], v_ref[:, cols], ROWS), dot(q_ref[:, cols], g_ref[:, cols], ROWS)
        state_ref[0, h], state_ref[1, h] = kv, qg
        opening_ref[h] = jnp.where(row < chain // 2, kv, qg)


def load(arrays, first, size, chain, after):
    rows = arrays[0].shape[0]
    *run, state, opening = pl.pallas_call(
        functools.partial(load_kernel, first, chain),
        in_specs=[HBM] * 4 + [VMEM] * len(after),
        out_specs=[VMEM] * 6,
        out_shape=[pltpu.VMEM((rows, size * DH), BF16)] * 4
        + [pltpu.VMEM((2, size, DH, DH), F32), pltpu.VMEM((size, DH, DH), F32)],
        scratch_shapes=[pltpu.SemaphoreType.DMA((size, 4))],
        compiler_params=PARAMS,
        name="load",
    )(*[pltpu.with_memory_space_constraint(a, pltpu.HBM) for a in arrays], *kept(after))
    return run, state, opening


def within_kernel(tile, *refs):
    q_ref, k_ref, v_ref, g_ref = refs[:4]
    attended_ref, query_ref, key_ref, value_ref = refs[-4:]
    rows, width = q_ref.shape
    count = rows // tile
    causal = lax.broadcasted_iota(jnp.int32, (tile, tile), 1) <= lax.broadcasted_iota(jnp.int32, (tile, tile), 0)

    def head(h, _):
        lanes = pl.ds(pl.multiple_of(h * DH, DH), DH)
        at = [pl.ds(i * tile, tile) for i in range(count)]
        q, k, v, g = ([ref[a, lanes] for a in at] for ref in (q_ref, k_ref, v_ref, g_ref))
        attn, grads = {}, {}
        for i in range(count):
            for j in range(i + 1):
                a, b = dot(q[i], k[j], LANES), dot(g[i], v[j], LANES)
                if i == j:
                    a, b = jnp.where(causal, a, 0.0), jnp.where(causal, b, 0.0)
                attn[i, j], grads[i, j] = a.astype(BF16), b.astype(BF16)
        for i in range(count):
            attended_ref[at[i], lanes] = sum(dot(attn[i, j], v[j], PLAIN) for j in range(i + 1))
            query_ref[at[i], lanes] = sum(dot(grads[i, j], k[j], PLAIN) for j in range(i + 1))
        for j in range(count):
            key_ref[at[j], lanes] = sum(dot(grads[i, j], q[i], ROWS) for i in range(j, count))
            value_ref[at[j], lanes] = sum(dot(attn[i, j], g[i], ROWS) for i in range(j, count))
        return 0

    lax.fori_loop(0, width // DH, head, 0, unroll=2 if width > DH else 1)


def within(run, after):
    rows, width = run[0].shape
    return pl.pallas_call(
        functools.partial(within_kernel, min(rows, 256)),
        in_specs=[VMEM] * (4 + len(after)),
        out_specs=[VMEM] * 4,
        out_shape=[pltpu.VMEM((rows, width), F32)] * 4,
        compiler_params=PARAMS,
        name="within",
    )(*kept(run), *kept(after))


def mix(function, shape, arrays, after, name):
    def kernel(*refs):
        row, column = spot()
        function(row, column, refs[: len(arrays)], refs[-1])

    return pl.pallas_call(
        kernel,
        in_specs=[VMEM] * (len(arrays) + len(after)),
        out_specs=VMEM,
        out_shape=pltpu.VMEM(shape, F32),
        compiler_params=PARAMS,
        name=name,
    )(*kept(arrays), *kept(after))


def across_kernel(total, count, *refs):
    q_ref, k_ref, v_ref, g_ref = refs[:4]
    parts = refs[4:8]
    sources = refs[8 : 8 + count]
    *outs, token_ref = refs[-5:]
    row, column = spot()
    head = pl.program_id(0)
    there = pl.ds(pl.multiple_of(head * DH, DH), DH)
    before, after = (x.astype(BF16) for x in total(row, column, sources, head))
    terms = (
        dot(q_ref[:, there], before, PLAIN),
        dot(g_ref[:, there], before, LANES),
        dot(v_ref[:, there], after, LANES),
        dot(k_ref[:, there], after, PLAIN),
    )
    for out, part, term in zip(outs, parts, terms, strict=True):
        out[...] = (part[:, there] + term).astype(BF16)
    token_ref[...] = jnp.zeros_like(token_ref)


def across(total, run, parts, sources, outs, shape, first, size, after):
    held = () if outs is None else tuple(outs)
    spec = pl.BlockSpec((shape[0], DH), lambda i: (0, first + i))
    fixed = 8 + len(sources)
    *outs, token = pl.pallas_call(
        functools.partial(across_kernel, total, len(sources)),
        grid=(size,),
        in_specs=[VMEM] * fixed + [HBM] * len(held) + [VMEM] * len(after),
        out_specs=[spec] * 4 + [VMEM],
        out_shape=[jax.ShapeDtypeStruct(shape, BF16)] * 4 + [pltpu.VMEM((8, DH), F32)],
        input_output_aliases={fixed + i: i for i in range(len(held))},
        compiler_params=PARAMS,
        name="across",
    )(*kept(run), *kept(parts), *kept(sources), *held, *kept(after))
    return outs, token


def body(*arrays):
    heads = arrays[0].shape[1] // DH
    runs, groups_of_heads = lax.axis_size("ctx"), lax.axis_size("seq")
    chain = runs // 2
    parts = 4
    size = heads // parts
    shape = (size, DH, DH)
    run, own, opening, local = ([None] * parts for _ in range(4))
    swapped = {}
    got = {}
    last = []
    pair = [(r, r ^ 1) for r in range(runs)]

    def swap(parity):
        perm = []
        for r in range(runs):
            z, c = r // 2, r % 2
            mate = z + 1 if z % 2 == parity else z - 1
            for s in range(groups_of_heads):
                if 0 <= mate < chain:
                    to = (2 * mate + c) * groups_of_heads + s
                else:
                    to = r * groups_of_heads + (s ^ 1)
                perm.append((r * groups_of_heads + s, to))
        return perm

    def arrival(p, z, way):
        if way == 0:
            return None if z == 0 else ((z - 1) % 2, p + z - 1)
        return None if z == chain - 1 else (z % 2, p + chain - 2 - z)

    def bring(p):
        run[p], own[p], opening[p] = load(arrays, p * size, size, chain, last)
        last[:] = [own[p]]

    def inside(p):
        local[p] = within(run[p], last)
        last[:] = [local[p][0]]

    def trade(p):
        if p >= 2:
            swapped[p] = lax.ppermute(own[p], "ctx", pair)
            return
        keys = sorted({arrival(p, z, way) for z in range(chain) for way in range(2)} - {None})

        def function(row, column, refs, out):
            for way, near in ((0, 0), (1, 1)):
                value = jnp.where(column == near, refs[0][way], 0.0)
                out[way] = value + chained(p, way, row, refs[1:], keys, slice(None))

        payload = mix(function, (2,) + shape, [own[p]] + [got[k] for k in keys], last, "trade")
        last[:] = [payload]
        swapped[p] = lax.ppermute(payload, "ctx", pair)

    def chained(p, way, row, refs, keys, at):
        total = jnp.zeros(refs[0][at].shape, F32)
        for key, ref in zip(keys, refs, strict=True):
            places = [z for z in range(chain) if arrival(p, z, way) == key]
            if places:
                total = jnp.where(any_of(row, places), ref[at], total)
        return total

    def hop(parity, slot):
        groups = {}
        for link in range(parity, chain - 1, 2):
            for way, p, z in ((0, slot - link, link), (1, slot - (chain - 2 - link), link + 1)):
                if 0 <= p < parts:
                    groups.setdefault((p, arrival(p, z, way)), ([], []))[way].append(z)
        if not groups:
            return
        names = []

        def use(name):
            if name not in names:
                names.append(name)

        for p, key in groups:
            use(("own", p))
            if p >= 2:
                use(("swapped", p))
            if key is not None:
                use(("got", key))
        tables = {"own": own, "swapped": swapped, "got": got}
        values = [tables[kind][key] for kind, key in names]

        def function(row, column, refs, out):
            refs = dict(zip(names, refs, strict=True))
            payload = None
            for (p, key), (up, down) in groups.items():
                def state(way):
                    value = refs["own", p][way]
                    return value + refs["swapped", p][way] if p >= 2 else value

                if up and down:
                    value = jnp.where(any_of(row, up), state(0), state(1))
                else:
                    value = state(0 if up else 1)
                if key is not None:
                    value = value + refs["got", key][...]
                payload = value if payload is None else jnp.where(any_of(row, up + down), value, payload)
            out[...] = payload

        plain = len(groups) == 1 and next(iter(groups)) in ((0, None), (1, None))
        if plain and chain > 2:
            payload = opening[next(iter(groups))[0]]
        else:
            payload = mix(function, shape, values, last, "hop")
            last[:] = [payload]
        got[parity, slot] = lax.ppermute(payload, ("ctx", "seq"), swap(parity))

    outs = [None]

    def finish(p):
        keys = sorted({arrival(p, z, way) for z in range(chain) for way in range(2)} - {None})

        def total(row, column, refs, head):
            for way, far in ((0, 1), (1, 0)):
                value = refs[0][way, head]
                if p >= 2:
                    value = jnp.where(column == far, value, 0.0)
                yield value + chained(p, way, row, refs[1:], keys, head)

        outs[0], token = across(
            total, run[p], local[p], [swapped[p]] + [got[k] for k in keys], outs[0], arrays[0].shape, p * size, size, last
        )
        last[:] = [token]

    bring(2)
    trade(2)
    bring(0)
    hop(0, 0)
    bring(3)
    trade(3)
    bring(1)
    hop(0, 1)
    if chain == 4:
        inside(2)
        hop(1, 1)
        inside(0)
        inside(1)
        hop(0, 2)
        hop(1, 2)
        inside(3)
        trade(0)
        hop(1, 3)
        hop(0, 3)
        hop(0, 4)
        hop(1, 4)
        trade(1)
        finish(0)
        hop(0, 5)
        finish(2)
        finish(3)
        finish(1)
    else:
        for p in range(parts):
            inside(p)
        for slot in range(parts + chain - 2):
            for parity in range(2):
                if (parity, slot) not in got:
                    hop(parity, slot)
        trade(0)
        trade(1)
        for p in (2, 3, 0, 1):
            finish(p)
    return tuple(outs[0])


def solution(mesh):
    spec = P("ctx", "seq")
    return jax.shard_map(body, mesh=mesh, in_specs=(spec,) * 4, out_specs=(spec,) * 4, check_vma=False)
```

time: 306 us -> 66.2 us (0.22)
  waiting for transfers between devices: 205 us -> 15.1 us
  matrix products: 33.2 us -> 0 us
  Pallas kernels: 0 us -> 32.9 us
  local copies, waits for them, and re-layouts: 32.3 us -> 0 us
  other arithmetic: 20 us -> 0 us
  starting transfers between devices: 0.08 us -> 17.2 us
  between operations: 14.3 us -> 0.84 us
    all_gather x2 -> x0, waiting for transfers between devices: 205 us -> none  [prefix(): gathered = lax.all_gather(part, axis)]
    dot_general x12 -> x0, matrix products: 33.2 us -> none  [the longest x1 6.43 us: body(): jnp.einsum('bthi,bthj->bhij', qloc, gloc, preferred_element_type=f32)]
    pallas_call x0 -> x22, Pallas kernels: none -> 32.9 us  [the longest x4 11.5 us: within(): pl.pallas_call(functools.partial(within_kernel, min(rows, 256)), in_specs...]
    ppermute x0 -> x14, starting transfers between devices: none -> 17.2 us  [the longest x10 13 us: hop(): got[parity, slot] = lax.ppermute(payload, ('ctx', 'seq'), swap(parity))]
    ppermute x0 -> x14, waiting for transfers between devices: none -> 15.1 us  [the longest x10 15.1 us: hop(): got[parity, slot] = lax.ppermute(payload, ('ctx', 'seq'), swap(parity))]
    reshape x3 -> x0, local copies, waits for them, and re-layouts: 12.7 us -> none  [the longest x1 4.49 us: body(): qloc = queries.reshape(shape)]
    unnamed x34 -> x0, local copies, waits for them, and re-layouts: 11.3 us -> none
    add x7 -> x0, other arithmetic: 10.4 us -> none  [add_states(): return earlier + later]
  transfers between devices with their start and end apart: 2 -> 14, of which waited for: 2 -> 4; matrix products, arithmetic and copies ran while one was open for 15% -> 0% of each run, Pallas kernels for 0% -> 38%
where the time goes in v2:
time: 66.2 us; the launch traced here: 66 us
  Pallas kernels  32.9 us (50%)
  starting transfers between devices  17.2 us (26%)
  waiting for transfers between devices  15.1 us (23%)
  between operations  0.84 us (1%)
    ppermute x10, waiting for transfers between devices, hop(): got[parity, slot] = lax.ppermute(payload, ('ctx', 'seq'), swap(parity))  15.1 us
    ppermute x10, starting transfers between devices, hop(): got[parity, slot] = lax.ppermute(payload, ('ctx', 'seq'), swap(parity))  13 us
    pallas_call x4, Pallas kernels, within(): pl.pallas_call(functools.partial(within_kernel, min(rows, 256)), in_specs...  11.5 us
    pallas_call x4, Pallas kernels, load(): pl.pallas_call(functools.partial(load_kernel, first, chain), in_specs=[HB...  10.9 us
    pallas_call x4, Pallas kernels, across(): pl.pallas_call(functools.partial(across_kernel, total, len(sources)), gri...  9.58 us
    ppermute x2, starting transfers between devices, trade(): swapped[p] = lax.ppermute(payload, 'ctx', pair)  2.16 us
    ppermute x2, starting transfers between devices, trade(): swapped[p] = lax.ppermute(own[p], 'ctx', pair)  2.02 us
  transfers between devices with their start and end apart: 14, of which 4 were waited for; matrix products, arithmetic and copies ran while one was open for 0% of the time, Pallas kernels for 38%

profile of v2, /device:TPU:0, one launch (start us, length us, event | category | flops | bytes accessed | tf_op | source)
XLA Modules:
  0.0 66.0 jit_solution(2259859469278362193)
XLA Ops:
  0.6 3.1 %load.4 = (bf16[512,512]{1,0:T(8,128)(2,1)S(1)}, bf16[512,512]{1,0:T(8,128)(2,1)S(1)}, bf16[512,512]{1,0:T(8,128)(2,1)S(1)}, bf16[512,512]{1,0:T(8,128)(2,1)S(1)...) custom-call(bf16[512,2048]{1,0:T(8,128)(2,1)} %q_hbm.7, bf16[512,2048]{1,0:T(8,128)(2,1)} %k_hbm.7, ...), custom_call_target="tpu_custom_call" | custom-call | tf_op jit(solution)/shard_map/load/pallas_call | solution.py:61
  3.7 2.4 %load.5 = (bf16[512,512]{1,0:T(8,128)(2,1)S(1)}, bf16[512,512]{1,0:T(8,128)(2,1)S(1)}, bf16[512,512]{1,0:T(8,128)(2,1)S(1)}, bf16[512,512]{1,0:T(8,128)(2,1)S(1)...) custom-call(bf16[512,2048]{1,0:T(8,128)(2,1)} %q_hbm.7, bf16[512,2048]{1,0:T(8,128)(2,1)} %k_hbm.7, ...), custom_call_target="tpu_custom_call" | custom-call | tf_op jit(solution)/shard_map/load/pallas_call | solution.py:61
  6.1 3.1 %collective-permute-start = (f32[4,128,128]{2,1,0:T(8,128)S(1)}, f32[4,128,128]{2,1,0:T(8,128)S(1)}, u32[]{:S(2)}, u32[]{:S(2)}) collective-permute-start(f32[4,128,128]{2,1,0:T(8,128)S(1)} %get-tuple-element.72), channel_id=1, source_target_pairs={{0,8},{1,9},{2,10},{3,11},{4,12},{5,13},{6,14},{7,15},{8,0},{9,1},... | collective-permute-start | bytes 786440 | tf_op jit(solution)/shard_map/ppermute | solution.py:275
  9.2 1.5 %collective-permute-start.3 = (f32[2,4,128,128]{3,2,1,0:T(8,128)S(1)}, f32[2,4,128,128]{3,2,1,0:T(8,128)S(1)}, u32[]{:S(2)}, u32[]{:S(2)}) collective-permute-start(f32[2,4,128,128]{3,2,1,0:T(8,128)S(1)} %get-tuple-element.61.refs_0_), channel_id=1, source_target_pairs={{0,4},{4,0},{8,12},{12,8},{16,20},{20,16},{24,28},{28,24},{1,5},{5... | collective-permute-start | bytes 1572872 | tf_op jit(solution)/shard_map/ppermute | solution.py:208
  10.7 3.1 %load.6 = (bf16[512,512]{1,0:T(8,128)(2,1)S(1)}, bf16[512,512]{1,0:T(8,128)(2,1)S(1)}, bf16[512,512]{1,0:T(8,128)(2,1)S(1)}, bf16[512,512]{1,0:T(8,128)(2,1)S(1)...) custom-call(bf16[512,2048]{1,0:T(8,128)(2,1)} %q_hbm.7, bf16[512,2048]{1,0:T(8,128)(2,1)} %k_hbm.7, ...), custom_call_target="tpu_custom_call" | custom-call | tf_op jit(solution)/shard_map/load/pallas_call | solution.py:61
  13.7 2.4 %load.7 = (bf16[512,512]{1,0:T(8,128)(2,1)S(1)}, bf16[512,512]{1,0:T(8,128)(2,1)S(1)}, bf16[512,512]{1,0:T(8,128)(2,1)S(1)}, bf16[512,512]{1,0:T(8,128)(2,1)S(1)...) custom-call(bf16[512,2048]{1,0:T(8,128)(2,1)} %q_hbm.7, bf16[512,2048]{1,0:T(8,128)(2,1)} %k_hbm.7, ...), custom_call_target="tpu_custom_call" | custom-call | tf_op jit(solution)/shard_map/load/pallas_call | solution.py:61
  16.1 3.0 %within.4 = (f32[512,512]{1,0:T(8,128)S(1)}, f32[512,512]{1,0:T(8,128)S(1)}, f32[512,512]{1,0:T(8,128)S(1)}, f32[512,512]{1,0:T(8,128)S(1)}) custom-call(bf16[512,512]{1,0:T(8,128)(2,1)S(1)} %get-tuple-element.73.refs_0_, bf16[512,512]{1,0:T(8,128)(2,1)S(1)} %get-tuple-element.74.refs_1_, bf16[512,512]{1,0:T(8,128)(2,1)S(1)} %get-tuple-element.75.refs_2_, ...), custom_call_target="tpu_custom_call" | custom-call | tf_op jit(solution)/shard_map/within/pallas_call | solution.py:105
  19.3 3.1 %collective-permute-start.1 = (f32[4,128,128]{2,1,0:T(8,128)S(1)}, f32[4,128,128]{2,1,0:T(8,128)S(1)}, u32[]{:S(2)}, u32[]{:S(2)}) collective-permute-start(f32[4,128,128]{2,1,0:T(8,128)S(1)} %get-tuple-element.84), channel_id=1, source_target_pairs={{0,8},{1,9},{2,10},{3,11},{4,12},{5,13},{6,14},{7,15},{8,0},{9,1},... | collective-permute-start | bytes 786440 | tf_op jit(solution)/shard_map/ppermute | solution.py:275
  23.0 2.8 %within.5 = (f32[512,512]{1,0:T(8,128)S(1)}, f32[512,512]{1,0:T(8,128)S(1)}, f32[512,512]{1,0:T(8,128)S(1)}, f32[512,512]{1,0:T(8,128)S(1)}) custom-call(bf16[512,512]{1,0:T(8,128)(2,1)S(1)} %get-tuple-element.68.refs_0_, bf16[512,512]{1,0:T(8,128)(2,1)S(1)} %get-tuple-element.69.refs_1_, bf16[512,512]{1,0:T(8,128)(2,1)S(1)} %get-tuple-element.70.refs_2_, ...), custom_call_target="tpu_custom_call" | custom-call | tf_op jit(solution)/shard_map/within/pallas_call | solution.py:105
  25.8 2.8 %within.6 = (f32[512,512]{1,0:T(8,128)S(1)}, f32[512,512]{1,0:T(8,128)S(1)}, f32[512,512]{1,0:T(8,128)S(1)}, f32[512,512]{1,0:T(8,128)S(1)}) custom-call(bf16[512,512]{1,0:T(8,128)(2,1)S(1)} %get-tuple-element.64.refs_0_, bf16[512,512]{1,0:T(8,128)(2,1)S(1)} %get-tuple-element.65.refs_1_, bf16[512,512]{1,0:T(8,128)(2,1)S(1)} %get-tuple-element.66.refs_2_, ...), custom_call_target="tpu_custom_call" | custom-call | tf_op jit(solution)/shard_map/within/pallas_call | solution.py:105
  29.0 2.8 %within.7 = (f32[512,512]{1,0:T(8,128)S(1)}, f32[512,512]{1,0:T(8,128)S(1)}, f32[512,512]{1,0:T(8,128)S(1)}, f32[512,512]{1,0:T(8,128)S(1)}) custom-call(bf16[512,512]{1,0:T(8,128)(2,1)S(1)} %get-tuple-element.85.refs_0_, bf16[512,512]{1,0:T(8,128)(2,1)S(1)} %get-tuple-element.86.refs_1_, bf16[512,512]{1,0:T(8,128)(2,1)S(1)} %get-tuple-element.87.refs_2_, ...), custom_call_target="tpu_custom_call" | custom-call | tf_op jit(solution)/shard_map/within/pallas_call | solution.py:105
  31.9 3.6 %collective-permute-done.6.refs_2_.refs_10_.refs_9_ = f32[4,128,128]{2,1,0:T(8,128)S(1)} collective-permute-done((f32[4,128,128]{2,1,0:T(8,128)S(1)}, f32[4,128,128]{2,1,0:T(8,128)S(1)}, u32[]{:S(2)}, u32[]{:S(2)}) %collective-permute-start.6) | collective-permute-done | bytes 262176 | tf_op jit(solution)/shard_map/ppermute | solution.py:275
  35.7 1.5 %collective-permute-start.11 = (f32[2,4,128,128]{3,2,1,0:T(8,128)S(1)}, f32[2,4,128,128]{3,2,1,0:T(8,128)S(1)}, u32[]{:S(2)}, u32[]{:S(2)}) collective-permute-start(f32[2,4,128,128]{3,2,1,0:T(8,128)S(1)} %trade.2.refs_3_), channel_id=1, source_target_pairs={{0,4},{4,0},{8,12},{12,8},{16,20},{20,16},{24,28},{28,24},{1,5},{5... | collective-permute-start | bytes 1572872 | tf_op jit(solution)/shard_map/ppermute | solution.py:219
  37.5 2.0 %collective-permute-start.7 = (f32[4,128,128]{2,1,0:T(8,128)S(1)}, f32[4,128,128]{2,1,0:T(8,128)S(1)}, u32[]{:S(2)}, u32[]{:S(2)}) collective-permute-start(f32[4,128,128]{2,1,0:T(8,128)S(1)} %hop.12.refs_3_), channel_id=1, source_target_pairs={{0,8},{1,9},{2,10},{3,11},{4,12},{5,13},{6,14},{7,15},{8,0},{9,1},... | collective-permute-start | bytes 786440 | tf_op jit(solution)/shard_map/ppermute | solution.py:275
  39.6 6.6 %collective-permute-done.7.refs_2_.refs_9_.refs_10_ = f32[4,128,128]{2,1,0:T(8,128)S(1)} collective-permute-done((f32[4,128,128]{2,1,0:T(8,128)S(1)}, f32[4,128,128]{2,1,0:T(8,128)S(1)}, u32[]{:S(2)}, u32[]{:S(2)}) %collective-permute-start.7) | collective-permute-done | bytes 262176 | tf_op jit(solution)/shard_map/ppermute | solution.py:275
  46.5 0.6 collective-permute-start.9
  47.2 0.6 collective-permute-start.13
  47.8 2.4 %across.4 = (bf16[512,2048]{1,0:T(8,128)(2,1)}, bf16[512,2048]{1,0:T(8,128)(2,1)}, bf16[512,2048]{1,0:T(8,128)(2,1)}, bf16[512,2048]{1,0:T(8,128)(2,1)}, f32[8,128]{1,0:T(8,128)S(1)}) custom-call(bf16[512,512]{1,0:T(8,128)(2,1)S(1)} %get-tuple-element.68.refs_0_, bf16[512,512]{1,0:T(8,128)(2,1)S(1)} %get-tuple-element.69.refs_1_, ...), custom_call_target="tpu_custom_call" | custom-call | tf_op jit(solution)/shard_map/across/pallas_call | solution.py:154
  50.2 3.7 %collective-permute-start.12 = (f32[4,128,128]{2,1,0:T(8,128)S(1)}, f32[4,128,128]{2,1,0:T(8,128)S(1)}, u32[]{:S(2)}, u32[]{:S(2)}) collective-permute-start(f32[4,128,128]{2,1,0:T(8,128)S(1)} %hop.15.refs_16_), channel_id=1, source_target_pairs={{0,8},{1,9},{2,10},{3,11},{4,12},{5,13},{6,14},{7,15},{8,0},{9,1},... | collective-permute-start | bytes 786440 | tf_op jit(solution)/shard_map/ppermute | solution.py:275
  54.0 2.3 %collective-permute-done.13.refs_10_ = f32[4,128,128]{2,1,0:T(8,128)S(1)} collective-permute-done((f32[4,128,128]{2,1,0:T(8,128)S(1)}, f32[4,128,128]{2,1,0:T(8,128)S(1)}, u32[]{:S(2)}, u32[]{:S(2)}) %collective-permute-start.13) | collective-permute-done | bytes 262176 | tf_op jit(solution)/shard_map/ppermute | solution.py:275
  56.3 2.4 %across.5 = (bf16[512,2048]{1,0:T(8,128)(2,1)}, bf16[512,2048]{1,0:T(8,128)(2,1)}, bf16[512,2048]{1,0:T(8,128)(2,1)}, bf16[512,2048]{1,0:T(8,128)(2,1)}, f32[8,128]{1,0:T(8,128)S(1)}) custom-call(bf16[512,512]{1,0:T(8,128)(2,1)S(1)} %get-tuple-element.73.refs_0_, ...), custom_call_target="tpu_custom_call", output_to_operand_aliasing={{0}: (12, {}), {1}: (13, {}), {2}: (14, {}), {3}: (15, {})} | custom-call | tf_op jit(solution)/shard_map/across/pallas_call | solution.py:154
  58.7 2.5 %collective-permute-done.12.refs_10_ = f32[4,128,128]{2,1,0:T(8,128)S(1)} collective-permute-done((f32[4,128,128]{2,1,0:T(8,128)S(1)}, f32[4,128,128]{2,1,0:T(8,128)S(1)}, u32[]{:S(2)}, u32[]{:S(2)}) %collective-permute-start.12) | collective-permute-done | bytes 262176 | tf_op jit(solution)/shard_map/ppermute | solution.py:275
  61.2 2.4 %across.6 = (bf16[512,2048]{1,0:T(8,128)(2,1)}, bf16[512,2048]{1,0:T(8,128)(2,1)}, bf16[512,2048]{1,0:T(8,128)(2,1)}, bf16[512,2048]{1,0:T(8,128)(2,1)}, f32[8,128]{1,0:T(8,128)S(1)}) custom-call(bf16[512,512]{1,0:T(8,128)(2,1)S(1)} %get-tuple-element.85.refs_0_, ...), custom_call_target="tpu_custom_call", output_to_operand_aliasing={{0}: (12, {}), {1}: (13, {}), {2}: (14, {}), {3}: (15, {})} | custom-call | tf_op jit(solution)/shard_map/across/pallas_call | solution.py:154
  63.6 2.4 %across.7 = (bf16[512,2048]{1,0:T(8,128)(2,1)}, bf16[512,2048]{1,0:T(8,128)(2,1)}, bf16[512,2048]{1,0:T(8,128)(2,1)}, bf16[512,2048]{1,0:T(8,128)(2,1)}, f32[8,128]{1,0:T(8,128)}) custom-call(bf16[512,512]{1,0:T(8,128)(2,1)S(1)} %get-tuple-element.64.refs_0_, ...), custom_call_target="tpu_custom_call", output_to_operand_aliasing={{0}: (12, {}), {1}: (13, {}), {2}: (14, {}), {3}: (15, {})} | custom-call | tf_op jit(solution)/shard_map/across/pallas_call | solution.py:154
  (26 shorter events, 1.8 us)
Async XLA Ops:
  6.1 13.1 %collective-permute-start = (f32[4,128,128]{2,1,0:T(8,128)S(1)}, f32[4,128,128]{2,1,0:T(8,128)S(1)}, u32[]{:S(2)}, u32[]{:S(2)}) collective-permute-start(f32[4,128,128]{2,1,0:T(8,128)S(1)} %get-tuple-element.72), channel_id=1, source_target_pairs={{0,8},{1,9},{2,10},{3,11},{4,12},{5,13},{6,14},{7,15},{8,0},{9,1},... | collective-permute-start | bytes 786440 | tf_op jit(solution)/shard_map/ppermute | solution.py:275
  9.2 19.5 %collective-permute-start.3 = (f32[2,4,128,128]{3,2,1,0:T(8,128)S(1)}, f32[2,4,128,128]{3,2,1,0:T(8,128)S(1)}, u32[]{:S(2)}, u32[]{:S(2)}) collective-permute-start(f32[2,4,128,128]{3,2,1,0:T(8,128)S(1)} %get-tuple-element.61.refs_0_), channel_id=1, source_target_pairs={{0,4},{4,0},{8,12},{12,8},{16,20},{20,16},{24,28},{28,24},{1,5},{5... | collective-permute-start | bytes 1572872 | tf_op jit(solution)/shard_map/ppermute | solution.py:208
  19.2 9.5 %collective-permute-start.4 = (f32[4,128,128]{2,1,0:T(8,128)S(1)}, f32[4,128,128]{2,1,0:T(8,128)S(1)}, u32[]{:S(2)}, u32[]{:S(2)}) collective-permute-start(f32[4,128,128]{2,1,0:T(8,128)S(1)} %hop.8.refs_4_), channel_id=1, source_target_pairs={{0,1},{1,0},{2,3},{3,2},{4,5},{5,4},{6,7},{7,6},{8,16},{9,17},{10,... | collective-permute-start | bytes 786440 | tf_op jit(solution)/shard_map/ppermute | solution.py:275
  19.3 9.6 %collective-permute-start.1 = (f32[4,128,128]{2,1,0:T(8,128)S(1)}, f32[4,128,128]{2,1,0:T(8,128)S(1)}, u32[]{:S(2)}, u32[]{:S(2)}) collective-permute-start(f32[4,128,128]{2,1,0:T(8,128)S(1)} %get-tuple-element.84), channel_id=1, source_target_pairs={{0,8},{1,9},{2,10},{3,11},{4,12},{5,13},{6,14},{7,15},{8,0},{9,1},... | collective-permute-start | bytes 786440 | tf_op jit(solution)/shard_map/ppermute | solution.py:275
  22.4 14.9 %collective-permute-start.2 = (f32[2,4,128,128]{3,2,1,0:T(8,128)S(1)}, f32[2,4,128,128]{3,2,1,0:T(8,128)S(1)}, u32[]{:S(2)}, u32[]{:S(2)}) collective-permute-start(f32[2,4,128,128]{3,2,1,0:T(8,128)S(1)} %get-tuple-element.63.refs_0_), channel_id=1, source_target_pairs={{0,4},{4,0},{8,12},{12,8},{16,20},{20,16},{24,28},{28,24},{1,5},{5... | collective-permute-start | bytes 1572872 | tf_op jit(solution)/shard_map/ppermute | solution.py:208
  28.8 6.7 %collective-permute-start.6 = (f32[4,128,128]{2,1,0:T(8,128)S(1)}, f32[4,128,128]{2,1,0:T(8,128)S(1)}, u32[]{:S(2)}, u32[]{:S(2)}) collective-permute-start(f32[4,128,128]{2,1,0:T(8,128)S(1)} %hop.9.refs_2_), channel_id=1, source_target_pairs={{0,8},{1,9},{2,10},{3,11},{4,12},{5,13},{6,14},{7,15},{8,0},{9,1},... | collective-permute-start | bytes 786440 | tf_op jit(solution)/shard_map/ppermute | solution.py:275
  29.0 8.4 %collective-permute-start.5 = (f32[4,128,128]{2,1,0:T(8,128)S(1)}, f32[4,128,128]{2,1,0:T(8,128)S(1)}, u32[]{:S(2)}, u32[]{:S(2)}) collective-permute-start(f32[4,128,128]{2,1,0:T(8,128)S(1)} %hop.10.refs_4_), channel_id=1, source_target_pairs={{0,1},{1,0},{2,3},{3,2},{4,5},{5,4},{6,7},{7,6},{8,16},{9,17},{10,... | collective-permute-start | bytes 786440 | tf_op jit(solution)/shard_map/ppermute | solution.py:275
  35.7 12.1 %collective-permute-start.11 = (f32[2,4,128,128]{3,2,1,0:T(8,128)S(1)}, f32[2,4,128,128]{3,2,1,0:T(8,128)S(1)}, u32[]{:S(2)}, u32[]{:S(2)}) collective-permute-start(f32[2,4,128,128]{3,2,1,0:T(8,128)S(1)} %trade.2.refs_3_), channel_id=1, source_target_pairs={{0,4},{4,0},{8,12},{12,8},{16,20},{20,16},{24,28},{28,24},{1,5},{5... | collective-permute-start | bytes 1572872 | tf_op jit(solution)/shard_map/ppermute | solution.py:219
  37.3 2.2 %collective-permute-start.8 = (f32[4,128,128]{2,1,0:T(8,128)S(1)}, f32[4,128,128]{2,1,0:T(8,128)S(1)}, u32[]{:S(2)}, u32[]{:S(2)}) collective-permute-start(f32[4,128,128]{2,1,0:T(8,128)S(1)} %hop.11.refs_4_), channel_id=1, source_target_pairs={{0,1},{1,0},{2,3},{3,2},{4,5},{5,4},{6,7},{7,6},{8,16},{9,17},{10,... | collective-permute-start | bytes 786440 | tf_op jit(solution)/shard_map/ppermute | solution.py:275
  37.5 8.8 %collective-permute-start.7 = (f32[4,128,128]{2,1,0:T(8,128)S(1)}, f32[4,128,128]{2,1,0:T(8,128)S(1)}, u32[]{:S(2)}, u32[]{:S(2)}) collective-permute-start(f32[4,128,128]{2,1,0:T(8,128)S(1)} %hop.12.refs_3_), channel_id=1, source_target_pairs={{0,8},{1,9},{2,10},{3,11},{4,12},{5,13},{6,14},{7,15},{8,0},{9,1},... | collective-permute-start | bytes 786440 | tf_op jit(solution)/shard_map/ppermute | solution.py:275
  46.3 3.8 %collective-permute-start.10 = (f32[4,128,128]{2,1,0:T(8,128)S(1)}, f32[4,128,128]{2,1,0:T(8,128)S(1)}, u32[]{:S(2)}, u32[]{:S(2)}) collective-permute-start(f32[4,128,128]{2,1,0:T(8,128)S(1)} %hop.14.refs_4_), channel_id=1, source_target_pairs={{0,1},{1,0},{2,3},{3,2},{4,5},{5,4},{6,7},{7,6},{8,16},{9,17},{10,... | collective-permute-start | bytes 786440 | tf_op jit(solution)/shard_map/ppermute | solution.py:275
  46.5 17.0 %collective-permute-start.9 = (f32[2,4,128,128]{3,2,1,0:T(8,128)S(1)}, f32[2,4,128,128]{3,2,1,0:T(8,128)S(1)}, u32[]{:S(2)}, u32[]{:S(2)}) collective-permute-start(f32[2,4,128,128]{3,2,1,0:T(8,128)S(1)} %trade.3.refs_12_), channel_id=1, source_target_pairs={{0,4},{4,0},{8,12},{12,8},{16,20},{20,16},{24,28},{28,24},{1,5},{5... | collective-permute-start | bytes 1572872 | tf_op jit(solution)/shard_map/ppermute | solution.py:219
  47.2 9.1 %collective-permute-start.13 = (f32[4,128,128]{2,1,0:T(8,128)S(1)}, f32[4,128,128]{2,1,0:T(8,128)S(1)}, u32[]{:S(2)}, u32[]{:S(2)}) collective-permute-start(f32[4,128,128]{2,1,0:T(8,128)S(1)} %hop.13.refs_3_), channel_id=1, source_target_pairs={{0,8},{1,9},{2,10},{3,11},{4,12},{5,13},{6,14},{7,15},{8,0},{9,1},... | collective-permute-start | bytes 786440 | tf_op jit(solution)/shard_map/ppermute | solution.py:275
  50.2 11.0 %collective-permute-start.12 = (f32[4,128,128]{2,1,0:T(8,128)S(1)}, f32[4,128,128]{2,1,0:T(8,128)S(1)}, u32[]{:S(2)}, u32[]{:S(2)}) collective-permute-start(f32[4,128,128]{2,1,0:T(8,128)S(1)} %hop.15.refs_16_), channel_id=1, source_target_pairs={{0,8},{1,9},{2,10},{3,11},{4,12},{5,13},{6,14},{7,15},{8,0},{9,1},... | collective-permute-start | bytes 786440 | tf_op jit(solution)/shard_map/ppermute | solution.py:275

commit v3 on v2

v3 whole, which is shorter than its diff:
```python
import functools

import jax
import jax.numpy as jnp
from jax import lax
from jax.experimental import pallas as pl
from jax.experimental.pallas import tpu as pltpu
from jax.sharding import PartitionSpec as P

DH = 128
F32 = jnp.float32
BF16 = jnp.bfloat16
ROWS = ((0,), (0,))
LANES = ((1,), (1,))
PLAIN = ((1,), (0,))
VMEM = pl.BlockSpec(memory_space=pltpu.VMEM)
HBM = pl.BlockSpec(memory_space=pltpu.HBM)
ACROSS_ROWS = 256
ORDER = (
    "L20", "X2", "E0", "L13", "X3", "O1", "E1", "W20", "W21", "W00", "E2", "W01", "O2", "W10",
    "W11", "X0", "O3", "E3", "W30", "W31", "E4", "O4", "X1", "A0", "E5", "A2", "A3", "A1",
)
PARAMS = pltpu.CompilerParams(vmem_limit_bytes=8 << 20)


def cost(us):
    return pl.CostEstimate(flops=int(us * 1.15e9), transcendentals=0, bytes_accessed=1)


def dot(a, b, dims):
    return lax.dot_general(a, b, (dims, ((), ())), preferred_element_type=F32)


def kept(arrays):
    return [pltpu.with_memory_space_constraint(a, pltpu.VMEM) for a in arrays]


def any_of(place, places):
    return functools.reduce(jnp.logical_or, [place == p for p in places])


def spot():
    place = lax.axis_index("ctx")
    return place // 2, place % 2


def load_kernel(firsts, q_hbm, k_hbm, v_hbm, g_hbm, *refs):
    *refs, sems = refs
    parts = [refs[len(refs) - 5 * (len(firsts) - n) :][:5] for n in range(len(firsts))]
    moves = []
    for n, (first, part) in enumerate(zip(firsts, parts, strict=True)):
        there = pl.ds(first * DH, part[0].shape[1])
        pairs = ((k_hbm, part[1]), (v_hbm, part[2]), (q_hbm, part[0]), (g_hbm, part[3]))
        moves.append([pltpu.make_async_copy(src.at[:, there], dst, sems.at[n, i]) for i, (src, dst) in enumerate(pairs)])
        for move in moves[-1]:
            move.start()
    for part, own in zip(parts, moves, strict=True):
        q_ref, k_ref, v_ref, g_ref, state_ref = part
        size = state_ref.shape[1]
        cols = [slice(h * DH, (h + 1) * DH) for h in range(size)]
        own[0].wait()
        own[1].wait()
        for h in range(size):
            state_ref[0, h] = dot(k_ref[:, cols[h]], v_ref[:, cols[h]], ROWS)
        own[2].wait()
        own[3].wait()
        for h in range(size):
            state_ref[1, h] = dot(q_ref[:, cols[h]], g_ref[:, cols[h]], ROWS)


def load(arrays, firsts, size, after):
    rows = arrays[0].shape[0]
    part = [pltpu.VMEM((rows, size * DH), BF16)] * 4 + [pltpu.VMEM((2, size, DH, DH), F32)]
    return pl.pallas_call(
        functools.partial(load_kernel, firsts),
        in_specs=[HBM] * 4 + [VMEM] * len(after),
        out_specs=[VMEM] * (5 * len(firsts)),
        out_shape=part * len(firsts),
        scratch_shapes=[pltpu.SemaphoreType.DMA((len(firsts), 4))],
        compiler_params=PARAMS,
        cost_estimate=cost(1.5 + 0.5 * len(firsts)),
        name="load",
    )(*[pltpu.with_memory_space_constraint(a, pltpu.HBM) for a in arrays], *kept(after))


def within_kernel(tile, first, *refs):
    q_ref, k_ref, v_ref, g_ref = refs[:4]
    attended_ref, query_ref, key_ref, value_ref = refs[-4:]
    rows, width = attended_ref.shape
    count = rows // tile
    causal = lax.broadcasted_iota(jnp.int32, (tile, tile), 1) <= lax.broadcasted_iota(jnp.int32, (tile, tile), 0)

    @pl.loop(0, width // DH)
    def _(h):
        lanes, source = (pl.ds(pl.multiple_of(n * DH, DH), DH) for n in (h, first + h))
        at = [pl.ds(i * tile, tile) for i in range(count)]
        q, k, v, g = ([ref[a, source] for a in at] for ref in (q_ref, k_ref, v_ref, g_ref))
        attn, grads = {}, {}
        for i in range(count):
            for j in range(i + 1):
                a, b = dot(q[i], k[j], LANES), dot(g[i], v[j], LANES)
                if i == j:
                    a, b = jnp.where(causal, a, 0.0), jnp.where(causal, b, 0.0)
                attn[i, j], grads[i, j] = a.astype(BF16), b.astype(BF16)
        for i in range(count):
            attended_ref[at[i], lanes] = sum(dot(attn[i, j], v[j], PLAIN) for j in range(i + 1))
            query_ref[at[i], lanes] = sum(dot(grads[i, j], k[j], PLAIN) for j in range(i + 1))
        for j in range(count):
            key_ref[at[j], lanes] = sum(dot(grads[i, j], q[i], ROWS) for i in range(j, count))
            value_ref[at[j], lanes] = sum(dot(attn[i, j], g[i], ROWS) for i in range(j, count))


def within(run, first, width, after):
    rows = run[0].shape[0]
    return pl.pallas_call(
        functools.partial(within_kernel, min(rows, 256), first),
        in_specs=[VMEM] * (4 + len(after)),
        out_specs=[VMEM] * 4,
        out_shape=[pltpu.VMEM((rows, width), F32)] * 4,
        compiler_params=PARAMS,
        cost_estimate=cost(1.5),
        name="within",
    )(*kept(run), *kept(after))


def mix(function, shape, arrays, after, name):
    def kernel(*refs):
        row, column = spot()
        function(row, column, refs[: len(arrays)], refs[-1])

    return pl.pallas_call(
        kernel,
        in_specs=[VMEM] * (len(arrays) + len(after)),
        out_specs=VMEM,
        out_shape=pltpu.VMEM(shape, F32),
        compiler_params=PARAMS,
        cost_estimate=cost(3),
        name=name,
    )(*kept(arrays), *kept(after))


def across_kernel(jobs, *refs):
    *outs, token_ref, done_ref, sems = refs[-7:]
    row, column = spot()
    moves, ready = [], []
    for total, first, pieces, count in jobs:
        run, refs = refs[:4], refs[4:]
        parts, refs = [refs[4 * n : 4 * n + 4] for n in range(pieces)], refs[4 * pieces :]
        sources, refs = refs[:count], refs[count:]
        ready.append((run, parts, first, [value.astype(BF16) for value in total(row, column, sources)]))
    for n, (run, parts, first, (before, after)) in enumerate(ready):
        q_ref, k_ref, v_ref, g_ref = run
        rows, width = q_ref.shape
        wide = width // len(parts)
        factors = ((q_ref, before, PLAIN), (g_ref, before, LANES), (v_ref, after, LANES), (k_ref, after, PLAIN))
        block = min(rows, ACROSS_ROWS)
        for start in range(0, rows, block):
            here = pl.ds(start, block)
            for i, (factor, state, dims) in enumerate(factors):
                for h in range(width // DH):
                    at = h * DH
                    part = parts[at // wide][i][here, pl.ds(at % wide, DH)]
                    term = dot(factor[here, pl.ds(at, DH)], state[h], dims)
                    done_ref[n, i, here, pl.ds(at, DH)] = (part + term).astype(BF16)
                there = outs[i].at[here, pl.ds(first * DH, width)]
                moves.append(pltpu.make_async_copy(done_ref.at[n, i, here], there, sems.at[len(moves)]))
                moves[-1].start()
    token_ref[...] = jnp.zeros_like(token_ref)
    for move in moves:
        move.wait()


def across(jobs, outs, shape, size, after):
    held = () if outs is None else tuple(outs)
    arrays = [a for _, _, run, parts, sources in jobs for a in [*run, *sum(map(list, parts), []), *sources]]
    *outs, token = pl.pallas_call(
        functools.partial(
            across_kernel, [(total, first, len(parts), len(sources)) for total, first, _, parts, sources in jobs]
        ),
        in_specs=[VMEM] * len(arrays) + [HBM] * len(held) + [VMEM] * len(after),
        out_specs=[HBM] * 4 + [VMEM],
        out_shape=[jax.ShapeDtypeStruct(shape, BF16)] * 4 + [pltpu.VMEM((8, DH), F32)],
        input_output_aliases={len(arrays) + i: i for i in range(len(held))},
        scratch_shapes=[
            pltpu.VMEM((len(jobs), 4, shape[0], size * DH), BF16),
            pltpu.SemaphoreType.DMA((4 * len(jobs) * max(1, shape[0] // ACROSS_ROWS),)),
        ],
        compiler_params=PARAMS,
        cost_estimate=cost(1.5 * len(jobs)),
        name="across",
    )(*kept(arrays), *held, *kept(after))
    return outs, token


def body(*arrays):
    heads = arrays[0].shape[1] // DH
    runs, groups_of_heads = lax.axis_size("ctx"), lax.axis_size("seq")
    chain = runs // 2
    parts = 4
    size = heads // parts
    shape = (size, DH, DH)
    run = [[None] * 4 for _ in range(parts)]
    own = [None] * parts
    pieces = min(size, 2)
    local = [[None] * pieces for _ in range(parts)]
    swapped = {}
    got = {}
    last = []
    pair = [(r, r ^ 1) for r in range(runs)]

    def swap(parity):
        perm = []
        for r in range(runs):
            z, c = r // 2, r % 2
            mate = z + 1 if z % 2 == parity else z - 1
            for s in range(groups_of_heads):
                if 0 <= mate < chain:
                    to = (2 * mate + c) * groups_of_heads + s
                else:
                    to = r * groups_of_heads + (s ^ 1)
                perm.append((r * groups_of_heads + s, to))
        return perm

    def arrival(p, z, way):
        if way == 0:
            return None if z == 0 else ((z - 1) % 2, p + z - 1)
        return None if z == chain - 1 else (z % 2, p + chain - 2 - z)

    def bring(*chosen):
        found = load(arrays, [p * size for p in chosen], size, last)
        for n, p in enumerate(chosen):
            *run[p], own[p] = found[5 * n : 5 * n + 5]
        last[:] = [own[chosen[0]]]

    def inside(p, piece):
        wide = max(1, size // 2)
        local[p][piece] = within(run[p], piece * wide, wide * DH, last)
        last[:] = [local[p][piece][0]]

    def trade(p):
        if p >= 2:
            swapped[p] = lax.ppermute(own[p], "ctx", pair)
            return
        keys = sorted({arrival(p, z, way) for z in range(chain) for way in range(2)} - {None})

        def function(row, column, refs, out):
            for way, near in ((0, 0), (1, 1)):
                value = jnp.where(column == near, refs[0][way], 0.0)
                out[way] = value + chained(p, way, row, refs[1:], keys)

        payload = mix(function, (2,) + shape, [own[p]] + [got[k] for k in keys], last, "trade")
        last[:] = [payload]
        swapped[p] = lax.ppermute(payload, "ctx", pair)

    def chained(p, way, row, refs, keys):
        total = jnp.zeros(shape, F32)
        for key, ref in zip(keys, refs, strict=True):
            places = [z for z in range(chain) if arrival(p, z, way) == key]
            if places:
                total = jnp.where(any_of(row, places), ref[...], total)
        return total

    def hop(parity, slot):
        groups = {}
        for link in range(parity, chain - 1, 2):
            for way, p, z in ((0, slot - link, link), (1, slot - (chain - 2 - link), link + 1)):
                if 0 <= p < parts:
                    groups.setdefault((p, arrival(p, z, way)), ([], []))[way].append(z)
        if not groups:
            return
        names = []

        def use(name):
            if name not in names:
                names.append(name)

        for p, key in groups:
            use(("own", p))
            if p >= 2:
                use(("swapped", p))
            if key is not None:
                use(("got", key))
        tables = {"own": own, "swapped": swapped, "got": got}
        values = [tables[kind][key] for kind, key in names]

        def function(row, column, refs, out):
            refs = dict(zip(names, refs, strict=True))
            payload = None
            for (p, key), (up, down) in groups.items():
                def state(way):
                    value = refs["own", p][way]
                    return value + refs["swapped", p][way] if p >= 2 else value

                if up and down:
                    value = jnp.where(any_of(row, up), state(0), state(1))
                else:
                    value = state(0 if up else 1)
                if key is not None:
                    value = value + refs["got", key][...]
                payload = value if payload is None else jnp.where(any_of(row, up + down), value, payload)
            out[...] = payload

        payload = mix(function, shape, values, last, "hop")
        last[:] = [payload]
        got[parity, slot] = lax.ppermute(payload, ("ctx", "seq"), swap(parity))

    outs = [None]

    def finish(*chosen):
        jobs = []
        for p in chosen:
            keys = sorted({arrival(p, z, way) for z in range(chain) for way in range(2)} - {None})

            def total(row, column, refs, p=p, keys=keys):
                for way, far in ((0, 1), (1, 0)):
                    value = refs[0][way]
                    if p >= 2:
                        value = jnp.where(column == far, value, 0.0)
                    yield value + chained(p, way, row, refs[1:], keys)

            jobs.append((total, p * size, run[p], local[p], [swapped[p]] + [got[k] for k in keys]))
        outs[0], token = across(jobs, outs[0], arrays[0].shape, size, last)
        last[:] = [token]

    steps = {"L": bring, "X": trade, "E": functools.partial(hop, 0), "O": functools.partial(hop, 1), "W": inside, "A": finish}
    order = [(name[0], [int(n) for n in name[1:]]) for name in ORDER]
    if chain != 4:
        order = [("L", [2, 0]), ("X", [2]), ("L", [1, 3]), ("X", [3])]
        order += [("W", [p, n]) for p in range(parts) for n in range(pieces)]
        order += [(kind, [t]) for t in range(parts + chain - 2) for kind in "EO"]
        order += [("X", [0]), ("X", [1]), ("A", [2, 3]), ("A", [0, 1])]
    for kind, numbers in order:
        steps[kind](*numbers)
    return tuple(outs[0])


def solution(mesh):
    spec = P("ctx", "seq")
    return jax.shard_map(body, mesh=mesh, in_specs=(spec,) * 4, out_specs=(spec,) * 4, check_vma=False)
```

time: 66.2 us -> 56.8 us (0.86)
  waiting for transfers between devices: 15.1 us -> 8.51 us
  Pallas kernels: 32.9 us -> 26.6 us
  starting transfers between devices: 17.2 us -> 20.5 us
    ppermute x10, waiting for transfers between devices: 15.1 us -> 7.04 us  [hop(): got[parity, slot] = lax.ppermute(payload, ('ctx', 'seq'), swap(parity))]
    pallas_call x12 -> x14, Pallas kernels: 32 us -> 25.6 us  [the longest x8 12.9 us: within(): pl.pallas_call(functools.partial(within_kernel, min(rows, 256), first), i...]
    ppermute x10, starting transfers between devices: 13 us -> 14.7 us  [hop(): got[parity, slot] = lax.ppermute(payload, ('ctx', 'seq'), swap(parity))]
    ppermute x2, starting transfers between devices: 2.02 us -> 3.6 us  [trade(): swapped[p] = lax.ppermute(own[p], 'ctx', pair)]
    ppermute x2, waiting for transfers between devices: 0.01 us -> 1.47 us  [trade(): swapped[p] = lax.ppermute(payload, 'ctx', pair)]
  transfers between devices with their start and end apart: 14 -> 14, of which waited for: 4 -> 6; matrix products, arithmetic and copies ran while one was open for 0% -> 0% of each run, Pallas kernels for 38% -> 38%
where the time goes in v3:
time: 56.8 us; the launch traced here: 56.6 us
  Pallas kernels  26.6 us (47%)
  starting transfers between devices  20.5 us (36%)
  waiting for transfers between devices  8.51 us (15%)
  between operations  1.04 us (2%)
    ppermute x10, starting transfers between devices, hop(): got[parity, slot] = lax.ppermute(payload, ('ctx', 'seq'), swap(parity))  14.7 us
    pallas_call x8, Pallas kernels, within(): pl.pallas_call(functools.partial(within_kernel, min(rows, 256), first), i...  12.9 us
    pallas_call x4, Pallas kernels, across(): pl.pallas_call(functools.partial(across_kernel, [(total, first, len(parts...  7.18 us
    ppermute x10, waiting for transfers between devices, hop(): got[parity, slot] = lax.ppermute(payload, ('ctx', 'seq'), swap(parity))  7.04 us
    pallas_call x2, Pallas kernels, load(): pl.pallas_call(functools.partial(load_kernel, firsts), in_specs=[HBM] * 4...  5.52 us
    ppermute x2, starting transfers between devices, trade(): swapped[p] = lax.ppermute(own[p], 'ctx', pair)  3.6 us
    ppermute x2, starting transfers between devices, trade(): swapped[p] = lax.ppermute(payload, 'ctx', pair)  2.16 us
    ppermute x2, waiting for transfers between devices, trade(): swapped[p] = lax.ppermute(payload, 'ctx', pair)  1.47 us
  transfers between devices with their start and end apart: 14, of which 6 were waited for; matrix products, arithmetic and copies ran while one was open for 0% of the time, Pallas kernels for 38%

profile of v3, /device:TPU:0, one launch (start us, length us, event | category | flops | bytes accessed | tf_op | source)
XLA Modules:
  0.0 56.6 jit_solution(119068218759149591)
XLA Ops:
  0.6 2.7 %load.2 = (bf16[512,512]{1,0:T(8,128)(2,1)S(1)}, bf16[512,512]{1,0:T(8,128)(2,1)S(1)}, bf16[512,512]{1,0:T(8,128)(2,1)S(1)}, bf16[512,512]{1,0:T(8,128)(2,1)S(1)...) custom-call(bf16[512,2048]{1,0:T(8,128)(2,1)} %q_hbm.3, ...), custom_call_target="tpu_custom_call" | custom-call | flops 2875000064 | bytes 1 | tf_op jit(solution)/shard_map/load/pallas_call | solution.py:74
  3.4 3.0 %collective-permute-start.2 = (f32[2,4,128,128]{3,2,1,0:T(8,128)S(1)}, f32[2,4,128,128]{3,2,1,0:T(8,128)S(1)}, u32[]{:S(2)}, u32[]{:S(2)}) collective-permute-start(f32[2,4,128,128]{3,2,1,0:T(8,128)S(1)} %get-tuple-element.76.refs_1_.refs_0_), channel_id=1, source_target_pairs={{0,4},{4,0},{8,12},{12,8},{16,20},{20,16},{24,28},{28,24},{1,5},{5... | collective-permute-start | bytes 1572872 | tf_op jit(solution)/shard_map/ppermute | solution.py:242
  6.4 1.6 %collective-permute-start = (f32[4,128,128]{2,1,0:T(8,128)S(1)}, f32[4,128,128]{2,1,0:T(8,128)S(1)}, u32[]{:S(2)}, u32[]{:S(2)}) collective-permute-start(f32[4,128,128]{2,1,0:T(8,128)S(1)} %hop.10.refs_0_), channel_id=1, source_target_pairs={{0,8},{1,9},{2,10},{3,11},{4,12},{5,13},{6,14},{7,15},{8,0},{9,1},... | collective-permute-start | bytes 786440 | tf_op jit(solution)/shard_map/ppermute | solution.py:305
  8.1 2.8 %load.3 = (bf16[512,512]{1,0:T(8,128)(2,1)S(1)}, bf16[512,512]{1,0:T(8,128)(2,1)S(1)}, bf16[512,512]{1,0:T(8,128)(2,1)S(1)}, bf16[512,512]{1,0:T(8,128)(2,1)S(1)...) custom-call(bf16[512,2048]{1,0:T(8,128)(2,1)} %q_hbm.3, ...), custom_call_target="tpu_custom_call" | custom-call | flops 2875000064 | bytes 1 | tf_op jit(solution)/shard_map/load/pallas_call | solution.py:74
  11.5 2.8 %collective-permute-done.refs_1_.refs_13_ = f32[4,128,128]{2,1,0:T(8,128)S(1)} collective-permute-done((f32[4,128,128]{2,1,0:T(8,128)S(1)}, f32[4,128,128]{2,1,0:T(8,128)S(1)}, u32[]{:S(2)}, u32[]{:S(2)}) %collective-permute-start) | collective-permute-done | bytes 262176 | tf_op jit(solution)/shard_map/ppermute | solution.py:305
  14.4 3.1 %collective-permute-start.1 = (f32[4,128,128]{2,1,0:T(8,128)S(1)}, f32[4,128,128]{2,1,0:T(8,128)S(1)}, u32[]{:S(2)}, u32[]{:S(2)}) collective-permute-start(f32[4,128,128]{2,1,0:T(8,128)S(1)} %hop.12.refs_4_), channel_id=1, source_target_pairs={{0,8},{1,9},{2,10},{3,11},{4,12},{5,13},{6,14},{7,15},{8,0},{9,1},... | collective-permute-start | bytes 786440 | tf_op jit(solution)/shard_map/ppermute | solution.py:305
  17.6 1.8 %within.8 = (f32[512,256]{1,0:T(8,128)S(1)}, f32[512,256]{1,0:T(8,128)S(1)}, f32[512,256]{1,0:T(8,128)S(1)}, f32[512,256]{1,0:T(8,128)S(1)}) custom-call(bf16[512,512]{1,0:T(8,128)(2,1)S(1)} %get-tuple-element.86.refs_0_, bf16[512,512]{1,0:T(8,128)(2,1)S(1)} %get-tuple-element.87.refs_1_, bf16[512,512]{1,0:T(8,128)(2,1)S(1)} %get-tuple-element.88.refs_2_, ...), custom_call_target="tpu_custom_call" | custom-call | flops 1724999936 | bytes 1 | tf_op jit(solution)/shard_map/within/pallas_call | solution.py:115
  19.4 1.6 %within.9 = (f32[512,256]{1,0:T(8,128)S(1)}, f32[512,256]{1,0:T(8,128)S(1)}, f32[512,256]{1,0:T(8,128)S(1)}, f32[512,256]{1,0:T(8,128)S(1)}) custom-call(bf16[512,512]{1,0:T(8,128)(2,1)S(1)} %get-tuple-element.86.refs_0_, bf16[512,512]{1,0:T(8,128)(2,1)S(1)} %get-tuple-element.87.refs_1_, bf16[512,512]{1,0:T(8,128)(2,1)S(1)} %get-tuple-element.88.refs_2_, ...), custom_call_target="tpu_custom_call" | custom-call | flops 1724999936 | bytes 1 | tf_op jit(solution)/shard_map/within/pallas_call | solution.py:115
  21.0 1.6 %within.10 = (f32[512,256]{1,0:T(8,128)S(1)}, f32[512,256]{1,0:T(8,128)S(1)}, f32[512,256]{1,0:T(8,128)S(1)}, f32[512,256]{1,0:T(8,128)S(1)}) custom-call(bf16[512,512]{1,0:T(8,128)(2,1)S(1)} %get-tuple-element.82.refs_0_, bf16[512,512]{1,0:T(8,128)(2,1)S(1)} %get-tuple-element.83.refs_1_, bf16[512,512]{1,0:T(8,128)(2,1)S(1)} %get-tuple-element.84.refs_2_, ...), custom_call_target="tpu_custom_call" | custom-call | flops 1724999936 | bytes 1 | tf_op jit(solution)/shard_map/within/pallas_call | solution.py:115
  23.0 1.6 %within.11 = (f32[512,256]{1,0:T(8,128)S(1)}, f32[512,256]{1,0:T(8,128)S(1)}, f32[512,256]{1,0:T(8,128)S(1)}, f32[512,256]{1,0:T(8,128)S(1)}) custom-call(bf16[512,512]{1,0:T(8,128)(2,1)S(1)} %get-tuple-element.82.refs_0_, bf16[512,512]{1,0:T(8,128)(2,1)S(1)} %get-tuple-element.83.refs_1_, bf16[512,512]{1,0:T(8,128)(2,1)S(1)} %get-tuple-element.84.refs_2_, ...), custom_call_target="tpu_custom_call" | custom-call | flops 1724999936 | bytes 1 | tf_op jit(solution)/shard_map/within/pallas_call | solution.py:115
  24.8 1.6 %within.12 = (f32[512,256]{1,0:T(8,128)S(1)}, f32[512,256]{1,0:T(8,128)S(1)}, f32[512,256]{1,0:T(8,128)S(1)}, f32[512,256]{1,0:T(8,128)S(1)}) custom-call(bf16[512,512]{1,0:T(8,128)(2,1)S(1)} %get-tuple-element.77.refs_0_, bf16[512,512]{1,0:T(8,128)(2,1)S(1)} %get-tuple-element.78.refs_1_, bf16[512,512]{1,0:T(8,128)(2,1)S(1)} %get-tuple-element.79.refs_2_, ...), custom_call_target="tpu_custom_call" | custom-call | flops 1724999936 | bytes 1 | tf_op jit(solution)/shard_map/within/pallas_call | solution.py:115
  26.4 1.6 %within.13 = (f32[512,256]{1,0:T(8,128)S(1)}, f32[512,256]{1,0:T(8,128)S(1)}, f32[512,256]{1,0:T(8,128)S(1)}, f32[512,256]{1,0:T(8,128)S(1)}) custom-call(bf16[512,512]{1,0:T(8,128)(2,1)S(1)} %get-tuple-element.77.refs_0_, bf16[512,512]{1,0:T(8,128)(2,1)S(1)} %get-tuple-element.78.refs_1_, bf16[512,512]{1,0:T(8,128)(2,1)S(1)} %get-tuple-element.79.refs_2_, ...), custom_call_target="tpu_custom_call" | custom-call | flops 1724999936 | bytes 1 | tf_op jit(solution)/shard_map/within/pallas_call | solution.py:115
  28.0 1.2 %collective-permute-done.6.refs_2_.refs_14_.refs_13_ = f32[4,128,128]{2,1,0:T(8,128)S(1)} collective-permute-done((f32[4,128,128]{2,1,0:T(8,128)S(1)}, f32[4,128,128]{2,1,0:T(8,128)S(1)}, u32[]{:S(2)}, u32[]{:S(2)}) %collective-permute-start.6) | collective-permute-done | bytes 262176 | tf_op jit(solution)/shard_map/ppermute | solution.py:305
  30.2 3.7 %collective-permute-start.7 = (f32[4,128,128]{2,1,0:T(8,128)S(1)}, f32[4,128,128]{2,1,0:T(8,128)S(1)}, u32[]{:S(2)}, u32[]{:S(2)}) collective-permute-start(f32[4,128,128]{2,1,0:T(8,128)S(1)} %hop.16.refs_4_), channel_id=1, source_target_pairs={{0,8},{1,9},{2,10},{3,11},{4,12},{5,13},{6,14},{7,15},{8,0},{9,1},... | collective-permute-start | bytes 786440 | tf_op jit(solution)/shard_map/ppermute | solution.py:305
  33.8 1.6 %within.14 = (f32[512,256]{1,0:T(8,128)S(1)}, f32[512,256]{1,0:T(8,128)S(1)}, f32[512,256]{1,0:T(8,128)S(1)}, f32[512,256]{1,0:T(8,128)S(1)}) custom-call(bf16[512,512]{1,0:T(8,128)(2,1)S(1)} %get-tuple-element.103.refs_0_, bf16[512,512]{1,0:T(8,128)(2,1)S(1)} %get-tuple-element.104.refs_1_, bf16[512,512]{1,0:T(8,128)(2,1)S(1)} %get-tuple-element.105.refs_2_, ...), custom_call_target="tpu_custom_call" | custom-call | flops 1724999936 | bytes 1 | tf_op jit(solution)/shard_map/within/pallas_call | solution.py:115
  35.5 1.6 %within.15 = (f32[512,256]{1,0:T(8,128)S(1)}, f32[512,256]{1,0:T(8,128)S(1)}, f32[512,256]{1,0:T(8,128)S(1)}, f32[512,256]{1,0:T(8,128)S(1)}) custom-call(bf16[512,512]{1,0:T(8,128)(2,1)S(1)} %get-tuple-element.103.refs_0_, bf16[512,512]{1,0:T(8,128)(2,1)S(1)} %get-tuple-element.104.refs_1_, bf16[512,512]{1,0:T(8,128)(2,1)S(1)} %get-tuple-element.105.refs_2_, ...), custom_call_target="tpu_custom_call" | custom-call | flops 1724999936 | bytes 1 | tf_op jit(solution)/shard_map/within/pallas_call | solution.py:115
  37.1 2.0 %collective-permute-start.13 = (f32[4,128,128]{2,1,0:T(8,128)S(1)}, f32[4,128,128]{2,1,0:T(8,128)S(1)}, u32[]{:S(2)}, u32[]{:S(2)}) collective-permute-start(f32[4,128,128]{2,1,0:T(8,128)S(1)} %hop.17.refs_3_), channel_id=1, source_target_pairs={{0,8},{1,9},{2,10},{3,11},{4,12},{5,13},{6,14},{7,15},{8,0},{9,1},... | collective-permute-start | bytes 786440 | tf_op jit(solution)/shard_map/ppermute | solution.py:305
  39.8 1.6 %collective-permute-start.9 = (f32[2,4,128,128]{3,2,1,0:T(8,128)S(1)}, f32[2,4,128,128]{3,2,1,0:T(8,128)S(1)}, u32[]{:S(2)}, u32[]{:S(2)}) collective-permute-start(f32[2,4,128,128]{3,2,1,0:T(8,128)S(1)} %trade.3.refs_16_), channel_id=1, source_target_pairs={{0,4},{4,0},{8,12},{12,8},{16,20},{20,16},{24,28},{28,24},{1,5},{5... | collective-permute-start | bytes 1572872 | tf_op jit(solution)/shard_map/ppermute | solution.py:253
  42.5 1.7 %across.4 = (bf16[512,2048]{1,0:T(8,128)(2,1)}, bf16[512,2048]{1,0:T(8,128)(2,1)}, bf16[512,2048]{1,0:T(8,128)(2,1)}, bf16[512,2048]{1,0:T(8,128)(2,1)}, f32[8,128]{1,0:T(8,128)S(1)}) custom-call(bf16[512,512]{1,0:T(8,128)(2,1)S(1)} %get-tuple-element.82.refs_0_, bf16[512,512]{1,0:T(8,128)(2,1)S(1)} %get-tuple-element.83.refs_1_, ...), custom_call_target="tpu_custom_call" | custom-call | flops 1724999936 | bytes 1 | tf_op jit(solution)/shard_map/across/pallas_call | solution.py:176
  44.3 3.6 %collective-permute-start.12 = (f32[4,128,128]{2,1,0:T(8,128)S(1)}, f32[4,128,128]{2,1,0:T(8,128)S(1)}, u32[]{:S(2)}, u32[]{:S(2)}) collective-permute-start(f32[4,128,128]{2,1,0:T(8,128)S(1)} %hop.19.refs_20_), channel_id=1, source_target_pairs={{0,8},{1,9},{2,10},{3,11},{4,12},{5,13},{6,14},{7,15},{8,0},{9,1},... | collective-permute-start | bytes 786440 | tf_op jit(solution)/shard_map/ppermute | solution.py:305
  47.9 1.7 %across.5 = (bf16[512,2048]{1,0:T(8,128)(2,1)}, bf16[512,2048]{1,0:T(8,128)(2,1)}, bf16[512,2048]{1,0:T(8,128)(2,1)}, bf16[512,2048]{1,0:T(8,128)(2,1)}, f32[8,128]{1,0:T(8,128)S(1)}) custom-call(bf16[512,512]{1,0:T(8,128)(2,1)S(1)} %get-tuple-element.86.refs_0_, ...), custom_call_target="tpu_custom_call", output_to_operand_aliasing={{0}: (16, {}), {1}: (17, {}), {2}: (18, {}), {3}: (19, {})} | custom-call | flops 1724999936 | bytes 1 | tf_op jit(solution)/shard_map/across/pallas_call | solution.py:176
  49.5 2.7 %collective-permute-done.12.refs_14_ = f32[4,128,128]{2,1,0:T(8,128)S(1)} collective-permute-done((f32[4,128,128]{2,1,0:T(8,128)S(1)}, f32[4,128,128]{2,1,0:T(8,128)S(1)}, u32[]{:S(2)}, u32[]{:S(2)}) %collective-permute-start.12) | collective-permute-done | bytes 262176 | tf_op jit(solution)/shard_map/ppermute | solution.py:305
  52.2 1.6 %across.6 = (bf16[512,2048]{1,0:T(8,128)(2,1)}, bf16[512,2048]{1,0:T(8,128)(2,1)}, bf16[512,2048]{1,0:T(8,128)(2,1)}, bf16[512,2048]{1,0:T(8,128)(2,1)}, f32[8,128]{1,0:T(8,128)S(1)}) custom-call(bf16[512,512]{1,0:T(8,128)(2,1)S(1)} %get-tuple-element.103.refs_0_, ...), custom_call_target="tpu_custom_call", output_to_operand_aliasing={{0}: (16, {}), {1}: (17, {}), {2}: (18, {}), {3}: (19, {})} | custom-call | flops 1724999936 | bytes 1 | tf_op jit(solution)/shard_map/across/pallas_call | solution.py:176
  54.2 2.2 %across.7 = (bf16[512,2048]{1,0:T(8,128)(2,1)}, bf16[512,2048]{1,0:T(8,128)(2,1)}, bf16[512,2048]{1,0:T(8,128)(2,1)}, bf16[512,2048]{1,0:T(8,128)(2,1)}, f32[8,128]{1,0:T(8,128)}) custom-call(bf16[512,512]{1,0:T(8,128)(2,1)S(1)} %get-tuple-element.77.refs_0_, ...), custom_call_target="tpu_custom_call", output_to_operand_aliasing={{0}: (16, {}), {1}: (17, {}), {2}: (18, {}), {3}: (19, {})} | custom-call | flops 1724999936 | bytes 1 | tf_op jit(solution)/shard_map/across/pallas_call | solution.py:176
  (30 shorter events, 4.6 us)
Async XLA Ops:
  3.4 19.2 %collective-permute-start.2 = (f32[2,4,128,128]{3,2,1,0:T(8,128)S(1)}, f32[2,4,128,128]{3,2,1,0:T(8,128)S(1)}, u32[]{:S(2)}, u32[]{:S(2)}) collective-permute-start(f32[2,4,128,128]{3,2,1,0:T(8,128)S(1)} %get-tuple-element.76.refs_1_.refs_0_), channel_id=1, source_target_pairs={{0,4},{4,0},{8,12},{12,8},{16,20},{20,16},{24,28},{28,24},{1,5},{5... | collective-permute-start | bytes 1572872 | tf_op jit(solution)/shard_map/ppermute | solution.py:242
  6.4 7.8 %collective-permute-start = (f32[4,128,128]{2,1,0:T(8,128)S(1)}, f32[4,128,128]{2,1,0:T(8,128)S(1)}, u32[]{:S(2)}, u32[]{:S(2)}) collective-permute-start(f32[4,128,128]{2,1,0:T(8,128)S(1)} %hop.10.refs_0_), channel_id=1, source_target_pairs={{0,8},{1,9},{2,10},{3,11},{4,12},{5,13},{6,14},{7,15},{8,0},{9,1},... | collective-permute-start | bytes 786440 | tf_op jit(solution)/shard_map/ppermute | solution.py:305
  10.9 19.2 %collective-permute-start.4 = (f32[2,4,128,128]{3,2,1,0:T(8,128)S(1)}, f32[2,4,128,128]{3,2,1,0:T(8,128)S(1)}, u32[]{:S(2)}, u32[]{:S(2)}) collective-permute-start(f32[2,4,128,128]{3,2,1,0:T(8,128)S(1)} %get-tuple-element.102.refs_0_), channel_id=1, source_target_pairs={{0,4},{4,0},{8,12},{12,8},{16,20},{20,16},{24,28},{28,24},{1,5},{5... | collective-permute-start | bytes 1572872 | tf_op jit(solution)/shard_map/ppermute | solution.py:242
  14.4 8.2 %collective-permute-start.3 = (f32[4,128,128]{2,1,0:T(8,128)S(1)}, f32[4,128,128]{2,1,0:T(8,128)S(1)}, u32[]{:S(2)}, u32[]{:S(2)}) collective-permute-start(f32[4,128,128]{2,1,0:T(8,128)S(1)} %hop.11.refs_1_), channel_id=1, source_target_pairs={{0,1},{1,0},{2,3},{3,2},{4,5},{5,4},{6,7},{7,6},{8,16},{9,17},{10,... | collective-permute-start | bytes 786440 | tf_op jit(solution)/shard_map/ppermute | solution.py:305
  14.4 10.2 %collective-permute-start.1 = (f32[4,128,128]{2,1,0:T(8,128)S(1)}, f32[4,128,128]{2,1,0:T(8,128)S(1)}, u32[]{:S(2)}, u32[]{:S(2)}) collective-permute-start(f32[4,128,128]{2,1,0:T(8,128)S(1)} %hop.12.refs_4_), channel_id=1, source_target_pairs={{0,8},{1,9},{2,10},{3,11},{4,12},{5,13},{6,14},{7,15},{8,0},{9,1},... | collective-permute-start | bytes 786440 | tf_op jit(solution)/shard_map/ppermute | solution.py:305
  22.7 6.4 %collective-permute-start.6 = (f32[4,128,128]{2,1,0:T(8,128)S(1)}, f32[4,128,128]{2,1,0:T(8,128)S(1)}, u32[]{:S(2)}, u32[]{:S(2)}) collective-permute-start(f32[4,128,128]{2,1,0:T(8,128)S(1)} %hop.13.refs_4_), channel_id=1, source_target_pairs={{0,8},{1,9},{2,10},{3,11},{4,12},{5,13},{6,14},{7,15},{8,0},{9,1},... | collective-permute-start | bytes 786440 | tf_op jit(solution)/shard_map/ppermute | solution.py:305
  24.7 5.4 %collective-permute-start.5 = (f32[4,128,128]{2,1,0:T(8,128)S(1)}, f32[4,128,128]{2,1,0:T(8,128)S(1)}, u32[]{:S(2)}, u32[]{:S(2)}) collective-permute-start(f32[4,128,128]{2,1,0:T(8,128)S(1)} %hop.14.refs_4_), channel_id=1, source_target_pairs={{0,1},{1,0},{2,3},{3,2},{4,5},{5,4},{6,7},{7,6},{8,16},{9,17},{10,... | collective-permute-start | bytes 786440 | tf_op jit(solution)/shard_map/ppermute | solution.py:305
  29.3 13.2 %collective-permute-start.11 = (f32[2,4,128,128]{3,2,1,0:T(8,128)S(1)}, f32[2,4,128,128]{3,2,1,0:T(8,128)S(1)}, u32[]{:S(2)}, u32[]{:S(2)}) collective-permute-start(f32[2,4,128,128]{3,2,1,0:T(8,128)S(1)} %trade.2.refs_3_), channel_id=1, source_target_pairs={{0,4},{4,0},{8,12},{12,8},{16,20},{20,16},{24,28},{28,24},{1,5},{5... | collective-permute-start | bytes 1572872 | tf_op jit(solution)/shard_map/ppermute | solution.py:253
  30.0 7.1 %collective-permute-start.8 = (f32[4,128,128]{2,1,0:T(8,128)S(1)}, f32[4,128,128]{2,1,0:T(8,128)S(1)}, u32[]{:S(2)}, u32[]{:S(2)}) collective-permute-start(f32[4,128,128]{2,1,0:T(8,128)S(1)} %hop.15.refs_4_), channel_id=1, source_target_pairs={{0,1},{1,0},{2,3},{3,2},{4,5},{5,4},{6,7},{7,6},{8,16},{9,17},{10,... | collective-permute-start | bytes 786440 | tf_op jit(solution)/shard_map/ppermute | solution.py:305
  30.2 9.4 %collective-permute-start.7 = (f32[4,128,128]{2,1,0:T(8,128)S(1)}, f32[4,128,128]{2,1,0:T(8,128)S(1)}, u32[]{:S(2)}, u32[]{:S(2)}) collective-permute-start(f32[4,128,128]{2,1,0:T(8,128)S(1)} %hop.16.refs_4_), channel_id=1, source_target_pairs={{0,8},{1,9},{2,10},{3,11},{4,12},{5,13},{6,14},{7,15},{8,0},{9,1},... | collective-permute-start | bytes 786440 | tf_op jit(solution)/shard_map/ppermute | solution.py:305
  37.1 10.7 %collective-permute-start.13 = (f32[4,128,128]{2,1,0:T(8,128)S(1)}, f32[4,128,128]{2,1,0:T(8,128)S(1)}, u32[]{:S(2)}, u32[]{:S(2)}) collective-permute-start(f32[4,128,128]{2,1,0:T(8,128)S(1)} %hop.17.refs_3_), channel_id=1, source_target_pairs={{0,8},{1,9},{2,10},{3,11},{4,12},{5,13},{6,14},{7,15},{8,0},{9,1},... | collective-permute-start | bytes 786440 | tf_op jit(solution)/shard_map/ppermute | solution.py:305
  39.6 4.6 %collective-permute-start.10 = (f32[4,128,128]{2,1,0:T(8,128)S(1)}, f32[4,128,128]{2,1,0:T(8,128)S(1)}, u32[]{:S(2)}, u32[]{:S(2)}) collective-permute-start(f32[4,128,128]{2,1,0:T(8,128)S(1)} %hop.18.refs_4_), channel_id=1, source_target_pairs={{0,1},{1,0},{2,3},{3,2},{4,5},{5,4},{6,7},{7,6},{8,16},{9,17},{10,... | collective-permute-start | bytes 786440 | tf_op jit(solution)/shard_map/ppermute | solution.py:305
  39.8 14.4 %collective-permute-start.9 = (f32[2,4,128,128]{3,2,1,0:T(8,128)S(1)}, f32[2,4,128,128]{3,2,1,0:T(8,128)S(1)}, u32[]{:S(2)}, u32[]{:S(2)}) collective-permute-start(f32[2,4,128,128]{3,2,1,0:T(8,128)S(1)} %trade.3.refs_16_), channel_id=1, source_target_pairs={{0,4},{4,0},{8,12},{12,8},{16,20},{20,16},{24,28},{28,24},{1,5},{5... | collective-permute-start | bytes 1572872 | tf_op jit(solution)/shard_map/ppermute | solution.py:253
  44.3 8.0 %collective-permute-start.12 = (f32[4,128,128]{2,1,0:T(8,128)S(1)}, f32[4,128,128]{2,1,0:T(8,128)S(1)}, u32[]{:S(2)}, u32[]{:S(2)}) collective-permute-start(f32[4,128,128]{2,1,0:T(8,128)S(1)} %hop.19.refs_20_), channel_id=1, source_target_pairs={{0,8},{1,9},{2,10},{3,11},{4,12},{5,13},{6,14},{7,15},{8,0},{9,1},... | collective-permute-start | bytes 786440 | tf_op jit(solution)/shard_map/ppermute | solution.py:305

commit v4 on v3

--- a/solution.py
+++ b/solution.py
@@ -17,8 +17,8 @@
 HBM = pl.BlockSpec(memory_space=pltpu.HBM)
 ACROSS_ROWS = 256
 ORDER = (
-    "L20", "X2", "E0", "L13", "X3", "O1", "E1", "W20", "W21", "W00", "E2", "W01", "O2", "W10",
-    "W11", "X0", "O3", "E3", "W30", "W31", "E4", "O4", "X1", "A0", "E5", "A2", "A3", "A1",
+    "L023", "E0", "S0", "L1", "E1", "W20", "O1", "S1", "W21", "W00", "E2", "O2", "W01", "W10",
+    "E3", "O3", "X0", "W11", "O4", "E4", "X1", "W30", "W31", "E5", "A0", "A2", "A31",
 )
 PARAMS = pltpu.CompilerParams(vmem_limit_bytes=8 << 20)
 
@@ -196,6 +196,7 @@
     heads = arrays[0].shape[1] // DH
     runs, groups_of_heads = lax.axis_size("ctx"), lax.axis_size("seq")
     chain = runs // 2
+    relay = chain == 4
     parts = 4
     size = heads // parts
     shape = (size, DH, DH)
@@ -203,10 +204,21 @@
     own = [None] * parts
     pieces = min(size, 2)
     local = [[None] * pieces for _ in range(parts)]
-    swapped = {}
-    got = {}
+    got, turns, swapped = {}, {}, {}
     last = []
     pair = [(r, r ^ 1) for r in range(runs)]
+
+    def early(row):
+        return row < chain // 2
+
+    def near(row, column):
+        return ((row == 0) & (column == 0)) | ((row == chain - 1) & (column == 1))
+
+    def end(row):
+        return (row == 0) | (row == chain - 1)
+
+    def far(row, column):
+        return end(row) & jnp.logical_not(near(row, column))
 
     def swap(parity):
         perm = []
@@ -237,24 +249,51 @@
         local[p][piece] = within(run[p], piece * wide, wide * DH, last)
         last[:] = [local[p][piece][0]]
 
+    def share(turn):
+        values = [own[2], own[3]]
+        if turn and relay:
+            values += [own[0], got[0, 0]]
+
+        def function(row, column, refs, out):
+            for n in range(2):
+                first, then = refs[n][0], refs[n][1]
+                value = jnp.where(early(row), *((then, first) if turn else (first, then)))
+                if turn and relay:
+                    mine = jnp.where(early(row), refs[2][0], refs[2][1])
+                    value = jnp.where(near(row, column), mine + refs[3][...] if n else mine, value)
+                    if n:
+                        value = jnp.where(far(row, column), mine, value)
+                out[n] = value
+
+        payload = mix(function, (2,) + shape, values, last, "share")
+        last[:] = [payload]
+        turns[turn] = lax.ppermute(payload, "ctx", pair)
+
     def trade(p):
-        if p >= 2:
-            swapped[p] = lax.ppermute(own[p], "ctx", pair)
-            return
         keys = sorted({arrival(p, z, way) for z in range(chain) for way in range(2)} - {None})
+        small = relay and p == 0
+        values = [own[p]] + [got[k] for k in keys] + ([own[3]] if relay and p == 1 else [])
 
         def function(row, column, refs, out):
-            for way, near in ((0, 0), (1, 1)):
-                value = jnp.where(column == near, refs[0][way], 0.0)
-                out[way] = value + chained(p, way, row, refs[1:], keys)
-
-        payload = mix(function, (2,) + shape, [own[p]] + [got[k] for k in keys], last, "trade")
+            sums = []
+            for way in range(2):
+                value = jnp.where(column == way, refs[0][way], 0.0) + chained(p, way, row, refs[1:], keys)
+                if relay and p == 1:
+                    late = (row == (0, chain - 1)[way]) & (column == 1 - way)
+                    value = jnp.where(late, refs[-1][1 - way], value)
+                sums.append(value)
+            if small:
+                out[...] = jnp.where(early(row), sums[1], sums[0])
+            else:
+                out[0], out[1] = sums
+
+        payload = mix(function, shape if small else (2,) + shape, values, last, "trade")
         last[:] = [payload]
         swapped[p] = lax.ppermute(payload, "ctx", pair)
 
     def chained(p, way, row, refs, keys):
         total = jnp.zeros(shape, F32)
-        for key, ref in zip(keys, refs, strict=True):
+        for key, ref in zip(keys, refs):
             places = [z for z in range(chain) if arrival(p, z, way) == key]
             if places:
                 total = jnp.where(any_of(row, places), ref[...], total)
@@ -268,36 +307,50 @@
                     groups.setdefault((p, arrival(p, z, way)), ([], []))[way].append(z)
         if not groups:
             return
+        def turn_of(way, z):
+            return 0 if early(z) == (way == 0) else 1
+
+        forward = relay and parity == 0 and slot == 4
         names = []
-
-        def use(name):
-            if name not in names:
-                names.append(name)
-
-        for p, key in groups:
-            use(("own", p))
+        for (p, key), ways in groups.items():
+            names.append(("own", p))
             if p >= 2:
-                use(("swapped", p))
+                names += [("turns", turn_of(way, z)) for way in range(2) for z in ways[way]]
             if key is not None:
-                use(("got", key))
-        tables = {"own": own, "swapped": swapped, "got": got}
+                names.append(("got", key))
+        if forward:
+            names.append(("turns", 1))
+        names = list(dict.fromkeys(names))
+        tables = {"own": own, "turns": turns, "got": got}
         values = [tables[kind][key] for kind, key in names]
 
         def function(row, column, refs, out):
             refs = dict(zip(names, refs, strict=True))
+
+            def state(p, way, rows):
+                value = refs["own", p][way]
+                if p >= 2:
+                    found = {turn_of(way, z) for z in rows}
+                    ways = [refs["turns", turn][p - 2] if turn in found else None for turn in range(2)]
+                    if len(found) == 2:
+                        other = jnp.where(early(row) == (way == 0), *ways)
+                    else:
+                        other = ways[found.pop()]
+                    value = value + other
+                return value
+
             payload = None
             for (p, key), (up, down) in groups.items():
-                def state(way):
-                    value = refs["own", p][way]
-                    return value + refs["swapped", p][way] if p >= 2 else value
-
                 if up and down:
-                    value = jnp.where(any_of(row, up), state(0), state(1))
+                    rising = early(row) if relay and slot == 0 else any_of(row, up)
+                    value = jnp.where(rising, state(p, 0, up), state(p, 1, down))
                 else:
-                    value = state(0 if up else 1)
+                    value = state(p, 0, up) if up else state(p, 1, down)
                 if key is not None:
                     value = value + refs["got", key][...]
                 payload = value if payload is None else jnp.where(any_of(row, up + down), value, payload)
+            if forward:
+                payload = jnp.where(end(row), refs["turns", 1][1], payload)
             out[...] = payload
 
         payload = mix(function, shape, values, last, "hop")
@@ -311,21 +364,42 @@
         for p in chosen:
             keys = sorted({arrival(p, z, way) for z in range(chain) for way in range(2)} - {None})
 
-            def total(row, column, refs, p=p, keys=keys):
-                for way, far in ((0, 1), (1, 0)):
-                    value = refs[0][way]
+            values = {("got", k): got[k] for k in keys}
+            if p >= 2:
+                values |= {("turns", n): turns[n] for n in range(2)}
+            else:
+                values["swapped", p] = swapped[p]
+            if relay and p == 3:
+                values["swapped", 1] = swapped[1]
+            if relay and p == 0:
+                values |= {("turns", 1): turns[1], ("got", (0, 4)): got[0, 4]}
+
+            def total(row, column, refs, p=p, keys=keys, names=tuple(values)):
+                refs = dict(zip(names, refs, strict=True))
+                for way in range(2):
+                    head, tail = (0, chain - 1) if way == 0 else (chain - 1, 0)
                     if p >= 2:
-                        value = jnp.where(column == far, value, 0.0)
-                    yield value + chained(p, way, row, refs[1:], keys)
-
-            jobs.append((total, p * size, run[p], local[p], [swapped[p]] + [got[k] for k in keys]))
+                        extra = jnp.where(early(row) == (way == 0), refs["turns", 0][p - 2], refs["turns", 1][p - 2])
+                        if relay and p == 3:
+                            extra = jnp.where(row == tail, refs["swapped", 1][1 - way], extra)
+                        extra = jnp.where(column == 1 - way, extra, 0.0)
+                    elif relay and p == 0:
+                        extra = jnp.where(early(row) == (way == 0), refs["got", (0, 4)][...], refs["swapped", 0][...])
+                        extra = jnp.where(row == head, refs["turns", 1][0], extra)
+                    else:
+                        extra = refs["swapped", p][way]
+                    if p < 2:
+                        extra = jnp.where((row == head) & (column == way), 0.0, extra)
+                    yield extra + chained(p, way, row, [refs["got", k] for k in keys], keys)
+
+            jobs.append((total, p * size, run[p], local[p], list(values.values())))
         outs[0], token = across(jobs, outs[0], arrays[0].shape, size, last)
         last[:] = [token]
 
-    steps = {"L": bring, "X": trade, "E": functools.partial(hop, 0), "O": functools.partial(hop, 1), "W": inside, "A": finish}
+    steps = {"L": bring, "S": share, "X": trade, "E": functools.partial(hop, 0), "O": functools.partial(hop, 1), "W": inside, "A": finish}
     order = [(name[0], [int(n) for n in name[1:]]) for name in ORDER]
     if chain != 4:
-        order = [("L", [2, 0]), ("X", [2]), ("L", [1, 3]), ("X", [3])]
+        order = [("L", [2, 3]), ("L", [0, 1]), ("S", [0]), ("S", [1])]
         order += [("W", [p, n]) for p in range(parts) for n in range(pieces)]
         order += [(kind, [t]) for t in range(parts + chain - 2) for kind in "EO"]
         order += [("X", [0]), ("X", [1]), ("A", [2, 3]), ("A", [0, 1])]

time: 56.8 us -> 55.2 us (0.972)
  starting transfers between devices: 20.5 us -> 19.4 us
    ppermute x10, waiting for transfers between devices: 7.04 us -> 3.94 us  [hop(): got[parity, slot] = lax.ppermute(payload, ('ctx', 'seq'), swap(parity))]
    ppermute x2, waiting for transfers between devices: 0.01 us -> 2.29 us  [share(): turns[turn] = lax.ppermute(payload, 'ctx', pair)]
    ppermute x10, starting transfers between devices: 14.7 us -> 13.6 us  [hop(): got[parity, slot] = lax.ppermute(payload, ('ctx', 'seq'), swap(parity))]
    ppermute x2, waiting for transfers between devices: 1.47 us -> 2.34 us  [trade(): swapped[p] = lax.ppermute(payload, 'ctx', pair)]
    pallas_call x4 -> x3, Pallas kernels: 7.18 us -> 6.46 us  [across(): pl.pallas_call(functools.partial(across_kernel, [(total, first, len(parts...]
    pallas_call x12 -> x14, Pallas kernels: 0.93 us -> 1.22 us  [mix(): pl.pallas_call(kernel, in_specs=[VMEM] * (len(arrays) + len(after)), out_...]
  transfers between devices with their start and end apart: 14 -> 14, of which waited for: 6 -> 5; matrix products, arithmetic and copies ran while one was open for 0% -> 0% of each run, Pallas kernels for 38% -> 35%
where the time goes in v4:
time: 55.2 us; the launch traced here: 55.1 us
  Pallas kernels  26.1 us (47%)
  starting transfers between devices  19.4 us (35%)
  waiting for transfers between devices  8.57 us (16%)
  between operations  1.01 us (2%)
    ppermute x10, starting transfers between devices, hop(): got[parity, slot] = lax.ppermute(payload, ('ctx', 'seq'), swap(parity))  13.6 us
    pallas_call x8, Pallas kernels, within(): pl.pallas_call(functools.partial(within_kernel, min(rows, 256), first), i...  12.9 us
    pallas_call x3, Pallas kernels, across(): pl.pallas_call(functools.partial(across_kernel, [(total, first, len(parts...  6.46 us
    pallas_call x2, Pallas kernels, load(): pl.pallas_call(functools.partial(load_kernel, firsts), in_specs=[HBM] * 4...  5.44 us
    ppermute x10, waiting for transfers between devices, hop(): got[parity, slot] = lax.ppermute(payload, ('ctx', 'seq'), swap(parity))  3.94 us
    ppermute x2, starting transfers between devices, share(): turns[turn] = lax.ppermute(payload, 'ctx', pair)  3.74 us
    ppermute x2, waiting for transfers between devices, trade(): swapped[p] = lax.ppermute(payload, 'ctx', pair)  2.34 us
    ppermute x2, waiting for transfers between devices, share(): turns[turn] = lax.ppermute(payload, 'ctx', pair)  2.29 us
  transfers between devices with their start and end apart: 14, of which 5 were waited for; matrix products, arithmetic and copies ran while one was open for 0% of the time, Pallas kernels for 35%

profile of v4, /device:TPU:0, one launch (start us, length us, event | category | flops | bytes accessed | tf_op | source)
XLA Modules:
  0.0 55.1 jit_solution(17622565722125262205)
XLA Ops:
  0.6 3.5 %load.2 = (bf16[512,512]{1,0:T(8,128)(2,1)S(1)}, bf16[512,512]{1,0:T(8,128)(2,1)S(1)}, bf16[512,512]{1,0:T(8,128)(2,1)S(1)}, bf16[512,512]{1,0:T(8,128)(2,1)S(1)...) custom-call(bf16[512,2048]{1,0:T(8,128)(2,1)} %q_hbm.3, ...), custom_call_target="tpu_custom_call" | custom-call | flops 3449999872 | bytes 1 | tf_op jit(solution)/shard_map/load/pallas_call | solution.py:74
  4.2 3.1 %collective-permute-start.2 = (f32[4,128,128]{2,1,0:T(8,128)S(1)}, f32[4,128,128]{2,1,0:T(8,128)S(1)}, u32[]{:S(2)}, u32[]{:S(2)}) collective-permute-start(f32[4,128,128]{2,1,0:T(8,128)S(1)} %hop.10.refs_2_), channel_id=1, source_target_pairs={{0,8},{1,9},{2,10},{3,11},{4,12},{5,13},{6,14},{7,15},{8,0},{9,1},... | collective-permute-start | bytes 786440 | tf_op jit(solution)/shard_map/ppermute | solution.py:358
  7.3 1.6 %collective-permute-start.1 = (f32[2,4,128,128]{3,2,1,0:T(8,128)S(1)}, f32[2,4,128,128]{3,2,1,0:T(8,128)S(1)}, u32[]{:S(2)}, u32[]{:S(2)}) collective-permute-start(f32[2,4,128,128]{3,2,1,0:T(8,128)S(1)} %share.2.refs_0_), channel_id=1, source_target_pairs={{0,4},{4,0},{8,12},{12,8},{16,20},{20,16},{24,28},{28,24},{1,5},{5... | collective-permute-start | bytes 1572872 | tf_op jit(solution)/shard_map/ppermute | solution.py:270
  8.9 1.9 %load.3 = (bf16[512,512]{1,0:T(8,128)(2,1)S(1)}, bf16[512,512]{1,0:T(8,128)(2,1)S(1)}, bf16[512,512]{1,0:T(8,128)(2,1)S(1)}, bf16[512,512]{1,0:T(8,128)(2,1)S(1)}, f32[2,4,128,128]{3,2,1,0:T(8,128)S(1)}) custom-call(bf16[512,2048]{1,0:T(8,128)(2,1)} %q_hbm.3, bf16[512,2048]{1,0:T(8,128)(2,1)} %k_hbm.3, bf16[512,2048]{1,0:T(8,128)(2,1)} %v_hbm.3, ...), custom_call_target="tpu_custom_call" | custom-call | flops 2300000000 | bytes 1 | tf_op jit(solution)/shard_map/load/pallas_call | solution.py:74
  11.4 1.8 %within.8 = (f32[512,256]{1,0:T(8,128)S(1)}, f32[512,256]{1,0:T(8,128)S(1)}, f32[512,256]{1,0:T(8,128)S(1)}, f32[512,256]{1,0:T(8,128)S(1)}) custom-call(bf16[512,512]{1,0:T(8,128)(2,1)S(1)} %get-tuple-element.78.refs_0_, bf16[512,512]{1,0:T(8,128)(2,1)S(1)} %get-tuple-element.79.refs_1_, bf16[512,512]{1,0:T(8,128)(2,1)S(1)} %get-tuple-element.80.refs_2_, ...), custom_call_target="tpu_custom_call" | custom-call | flops 1724999936 | bytes 1 | tf_op jit(solution)/shard_map/within/pallas_call | solution.py:115
  13.2 1.1 %collective-permute-done.2.refs_1_.refs_3_.refs_12_ = f32[4,128,128]{2,1,0:T(8,128)S(1)} collective-permute-done((f32[4,128,128]{2,1,0:T(8,128)S(1)}, f32[4,128,128]{2,1,0:T(8,128)S(1)}, u32[]{:S(2)}, u32[]{:S(2)}) %collective-permute-start.2) | collective-permute-done | bytes 262176 | tf_op jit(solution)/shard_map/ppermute | solution.py:358
  14.6 2.2 %collective-permute-start.6 = (f32[2,4,128,128]{3,2,1,0:T(8,128)S(1)}, f32[2,4,128,128]{3,2,1,0:T(8,128)S(1)}, u32[]{:S(2)}, u32[]{:S(2)}) collective-permute-start(f32[2,4,128,128]{3,2,1,0:T(8,128)S(1)} %share.3.refs_4_), channel_id=1, source_target_pairs={{0,4},{4,0},{8,12},{12,8},{16,20},{20,16},{24,28},{28,24},{1,5},{5... | collective-permute-start | bytes 1572872 | tf_op jit(solution)/shard_map/ppermute | solution.py:270
  16.8 1.6 %within.9 = (f32[512,256]{1,0:T(8,128)S(1)}, f32[512,256]{1,0:T(8,128)S(1)}, f32[512,256]{1,0:T(8,128)S(1)}, f32[512,256]{1,0:T(8,128)S(1)}) custom-call(bf16[512,512]{1,0:T(8,128)(2,1)S(1)} %get-tuple-element.78.refs_0_, bf16[512,512]{1,0:T(8,128)(2,1)S(1)} %get-tuple-element.79.refs_1_, bf16[512,512]{1,0:T(8,128)(2,1)S(1)} %get-tuple-element.80.refs_2_, ...), custom_call_target="tpu_custom_call" | custom-call | flops 1724999936 | bytes 1 | tf_op jit(solution)/shard_map/within/pallas_call | solution.py:115
  18.4 1.6 %within.10 = (f32[512,256]{1,0:T(8,128)S(1)}, f32[512,256]{1,0:T(8,128)S(1)}, f32[512,256]{1,0:T(8,128)S(1)}, f32[512,256]{1,0:T(8,128)S(1)}) custom-call(bf16[512,512]{1,0:T(8,128)(2,1)S(1)} %get-tuple-element.83.refs_0_, bf16[512,512]{1,0:T(8,128)(2,1)S(1)} %get-tuple-element.84.refs_1_, bf16[512,512]{1,0:T(8,128)(2,1)S(1)} %get-tuple-element.85.refs_2_, ...), custom_call_target="tpu_custom_call" | custom-call | flops 1724999936 | bytes 1 | tf_op jit(solution)/shard_map/within/pallas_call | solution.py:115
  20.0 2.3 %collective-permute-done.1.refs_1_.refs_15_ = f32[2,4,128,128]{3,2,1,0:T(8,128)S(1)} collective-permute-done((f32[2,4,128,128]{3,2,1,0:T(8,128)S(1)}, f32[2,4,128,128]{3,2,1,0:T(8,128)S(1)}, u32[]{:S(2)}, u32[]{:S(2)}) %collective-permute-start.1) | collective-permute-done | bytes 524320 | tf_op jit(solution)/shard_map/ppermute | solution.py:270
  23.4 1.6 %within.11 = (f32[512,256]{1,0:T(8,128)S(1)}, f32[512,256]{1,0:T(8,128)S(1)}, f32[512,256]{1,0:T(8,128)S(1)}, f32[512,256]{1,0:T(8,128)S(1)}) custom-call(bf16[512,512]{1,0:T(8,128)(2,1)S(1)} %get-tuple-element.83.refs_0_, bf16[512,512]{1,0:T(8,128)(2,1)S(1)} %get-tuple-element.84.refs_1_, bf16[512,512]{1,0:T(8,128)(2,1)S(1)} %get-tuple-element.85.refs_2_, ...), custom_call_target="tpu_custom_call" | custom-call | flops 1724999936 | bytes 1 | tf_op jit(solution)/shard_map/within/pallas_call | solution.py:115
  25.0 1.6 %within.12 = (f32[512,256]{1,0:T(8,128)S(1)}, f32[512,256]{1,0:T(8,128)S(1)}, f32[512,256]{1,0:T(8,128)S(1)}, f32[512,256]{1,0:T(8,128)S(1)}) custom-call(bf16[512,512]{1,0:T(8,128)(2,1)S(1)} %get-tuple-element.89.refs_0_.refs_18_, bf16[512,512]{1,0:T(8,128)(2,1)S(1)} %get-tuple-element.90.refs_1_.refs_19_, ...), custom_call_target="tpu_custom_call" | custom-call | flops 1724999936 | bytes 1 | tf_op jit(solution)/shard_map/within/pallas_call | solution.py:115
  26.8 4.8 %collective-permute-start.5 = (f32[4,128,128]{2,1,0:T(8,128)S(1)}, f32[4,128,128]{2,1,0:T(8,128)S(1)}, u32[]{:S(2)}, u32[]{:S(2)}) collective-permute-start(f32[4,128,128]{2,1,0:T(8,128)S(1)} %hop.15.refs_3_), channel_id=1, source_target_pairs={{0,8},{1,9},{2,10},{3,11},{4,12},{5,13},{6,14},{7,15},{8,0},{9,1},... | collective-permute-start | bytes 786440 | tf_op jit(solution)/shard_map/ppermute | solution.py:358
  31.9 1.1 %collective-permute-start.13 = (f32[4,128,128]{2,1,0:T(8,128)S(1)}, f32[4,128,128]{2,1,0:T(8,128)S(1)}, u32[]{:S(2)}, u32[]{:S(2)}) collective-permute-start(f32[4,128,128]{2,1,0:T(8,128)S(1)} %trade.2.refs_4_), channel_id=1, source_target_pairs={{0,4},{4,0},{8,12},{12,8},{16,20},{20,16},{24,28},{28,24},{1,5},{5... | collective-permute-start | bytes 786440 | tf_op jit(solution)/shard_map/ppermute | solution.py:292
  33.0 1.6 %within.13 = (f32[512,256]{1,0:T(8,128)S(1)}, f32[512,256]{1,0:T(8,128)S(1)}, f32[512,256]{1,0:T(8,128)S(1)}, f32[512,256]{1,0:T(8,128)S(1)}) custom-call(bf16[512,512]{1,0:T(8,128)(2,1)S(1)} %get-tuple-element.89.refs_0_.refs_18_, bf16[512,512]{1,0:T(8,128)(2,1)S(1)} %get-tuple-element.90.refs_1_.refs_19_, ...), custom_call_target="tpu_custom_call" | custom-call | flops 1724999936 | bytes 1 | tf_op jit(solution)/shard_map/within/pallas_call | solution.py:115
  34.6 1.3 %collective-permute-done.5.refs_2_.refs_12_.refs_31_ = f32[4,128,128]{2,1,0:T(8,128)S(1)} collective-permute-done((f32[4,128,128]{2,1,0:T(8,128)S(1)}, f32[4,128,128]{2,1,0:T(8,128)S(1)}, u32[]{:S(2)}, u32[]{:S(2)}) %collective-permute-start.5) | collective-permute-done | bytes 262176 | tf_op jit(solution)/shard_map/ppermute | solution.py:358
  36.2 3.8 %collective-permute-start.12 = (f32[4,128,128]{2,1,0:T(8,128)S(1)}, f32[4,128,128]{2,1,0:T(8,128)S(1)}, u32[]{:S(2)}, u32[]{:S(2)}) collective-permute-start(f32[4,128,128]{2,1,0:T(8,128)S(1)} %hop.18.refs_5_), channel_id=1, source_target_pairs={{0,8},{1,9},{2,10},{3,11},{4,12},{5,13},{6,14},{7,15},{8,0},{9,1},... | collective-permute-start | bytes 786440 | tf_op jit(solution)/shard_map/ppermute | solution.py:358
  41.1 1.6 %within.14 = (f32[512,256]{1,0:T(8,128)S(1)}, f32[512,256]{1,0:T(8,128)S(1)}, f32[512,256]{1,0:T(8,128)S(1)}, f32[512,256]{1,0:T(8,128)S(1)}) custom-call(bf16[512,512]{1,0:T(8,128)(2,1)S(1)} %get-tuple-element.70.refs_0_, bf16[512,512]{1,0:T(8,128)(2,1)S(1)} %get-tuple-element.71.refs_1_, bf16[512,512]{1,0:T(8,128)(2,1)S(1)} %get-tuple-element.72.refs_2_, ...), custom_call_target="tpu_custom_call" | custom-call | flops 1724999936 | bytes 1 | tf_op jit(solution)/shard_map/within/pallas_call | solution.py:115
  42.7 1.6 %within.15 = (f32[512,256]{1,0:T(8,128)S(1)}, f32[512,256]{1,0:T(8,128)S(1)}, f32[512,256]{1,0:T(8,128)S(1)}, f32[512,256]{1,0:T(8,128)S(1)}) custom-call(bf16[512,512]{1,0:T(8,128)(2,1)S(1)} %get-tuple-element.70.refs_0_, bf16[512,512]{1,0:T(8,128)(2,1)S(1)} %get-tuple-element.71.refs_1_, bf16[512,512]{1,0:T(8,128)(2,1)S(1)} %get-tuple-element.72.refs_2_, ...), custom_call_target="tpu_custom_call" | custom-call | flops 1724999936 | bytes 1 | tf_op jit(solution)/shard_map/within/pallas_call | solution.py:115
  44.6 1.5 %collective-permute-done.12.refs_17_.refs_13_ = f32[4,128,128]{2,1,0:T(8,128)S(1)} collective-permute-done((f32[4,128,128]{2,1,0:T(8,128)S(1)}, f32[4,128,128]{2,1,0:T(8,128)S(1)}, u32[]{:S(2)}, u32[]{:S(2)}) %collective-permute-start.12) | collective-permute-done | bytes 262176 | tf_op jit(solution)/shard_map/ppermute | solution.py:358
  46.1 1.7 %across.3 = (bf16[512,2048]{1,0:T(8,128)(2,1)}, bf16[512,2048]{1,0:T(8,128)(2,1)}, bf16[512,2048]{1,0:T(8,128)(2,1)}, bf16[512,2048]{1,0:T(8,128)(2,1)}, f32[8,128]{1,0:T(8,128)S(1)}) custom-call(bf16[512,512]{1,0:T(8,128)(2,1)S(1)} %get-tuple-element.83.refs_0_, bf16[512,512]{1,0:T(8,128)(2,1)S(1)} %get-tuple-element.84.refs_1_, ...), custom_call_target="tpu_custom_call" | custom-call | flops 1724999936 | bytes 1 | tf_op jit(solution)/shard_map/across/pallas_call | solution.py:176
  47.8 1.7 %across.4 = (bf16[512,2048]{1,0:T(8,128)(2,1)}, bf16[512,2048]{1,0:T(8,128)(2,1)}, bf16[512,2048]{1,0:T(8,128)(2,1)}, bf16[512,2048]{1,0:T(8,128)(2,1)}, f32[8,128]{1,0:T(8,128)S(1)}) custom-call(bf16[512,512]{1,0:T(8,128)(2,1)S(1)} %get-tuple-element.78.refs_0_, ...), custom_call_target="tpu_custom_call", output_to_operand_aliasing={{0}: (17, {}), {1}: (18, {}), {2}: (19, {}), {3}: (20, {})} | custom-call | flops 1724999936 | bytes 1 | tf_op jit(solution)/shard_map/across/pallas_call | solution.py:176
  49.5 2.3 %collective-permute-done.11.refs_17_.refs_33_ = f32[2,4,128,128]{3,2,1,0:T(8,128)S(1)} collective-permute-done((f32[2,4,128,128]{3,2,1,0:T(8,128)S(1)}, f32[2,4,128,128]{3,2,1,0:T(8,128)S(1)}, u32[]{:S(2)}, u32[]{:S(2)}) %collective-permute-start.11) | collective-permute-done | bytes 524320 | tf_op jit(solution)/shard_map/ppermute | solution.py:292
  51.9 3.1 %across.5 = (bf16[512,2048]{1,0:T(8,128)(2,1)}, bf16[512,2048]{1,0:T(8,128)(2,1)}, bf16[512,2048]{1,0:T(8,128)(2,1)}, bf16[512,2048]{1,0:T(8,128)(2,1)}, f32[8,128]{1,0:T(8,128)}) custom-call(bf16[512,512]{1,0:T(8,128)(2,1)S(1)} %get-tuple-element.70.refs_0_, ...), custom_call_target="tpu_custom_call", output_to_operand_aliasing={{0}: (34, {}), {1}: (35, {}), {2}: (36, {}), {3}: (37, {})} | custom-call | flops 3449999872 | bytes 1 | tf_op jit(solution)/shard_map/across/pallas_call | solution.py:176
  (31 shorter events, 4.1 us)
Async XLA Ops:
  4.2 10.1 %collective-permute-start.2 = (f32[4,128,128]{2,1,0:T(8,128)S(1)}, f32[4,128,128]{2,1,0:T(8,128)S(1)}, u32[]{:S(2)}, u32[]{:S(2)}) collective-permute-start(f32[4,128,128]{2,1,0:T(8,128)S(1)} %hop.10.refs_2_), channel_id=1, source_target_pairs={{0,8},{1,9},{2,10},{3,11},{4,12},{5,13},{6,14},{7,15},{8,0},{9,1},... | collective-permute-start | bytes 786440 | tf_op jit(solution)/shard_map/ppermute | solution.py:358
  7.3 14.9 %collective-permute-start.1 = (f32[2,4,128,128]{3,2,1,0:T(8,128)S(1)}, f32[2,4,128,128]{3,2,1,0:T(8,128)S(1)}, u32[]{:S(2)}, u32[]{:S(2)}) collective-permute-start(f32[2,4,128,128]{3,2,1,0:T(8,128)S(1)} %share.2.refs_0_), channel_id=1, source_target_pairs={{0,4},{4,0},{8,12},{12,8},{16,20},{20,16},{24,28},{28,24},{1,5},{5... | collective-permute-start | bytes 1572872 | tf_op jit(solution)/shard_map/ppermute | solution.py:270
  10.9 12.4 %collective-permute-start = (f32[4,128,128]{2,1,0:T(8,128)S(1)}, f32[4,128,128]{2,1,0:T(8,128)S(1)}, u32[]{:S(2)}, u32[]{:S(2)}) collective-permute-start(f32[4,128,128]{2,1,0:T(8,128)S(1)} %hop.11.refs_4_), channel_id=1, source_target_pairs={{0,8},{1,9},{2,10},{3,11},{4,12},{5,13},{6,14},{7,15},{8,0},{9,1},... | collective-permute-start | bytes 786440 | tf_op jit(solution)/shard_map/ppermute | solution.py:358
  14.3 7.9 %collective-permute-start.3 = (f32[4,128,128]{2,1,0:T(8,128)S(1)}, f32[4,128,128]{2,1,0:T(8,128)S(1)}, u32[]{:S(2)}, u32[]{:S(2)}) collective-permute-start(f32[4,128,128]{2,1,0:T(8,128)S(1)} %hop.12.refs_4_), channel_id=1, source_target_pairs={{0,1},{1,0},{2,3},{3,2},{4,5},{5,4},{6,7},{7,6},{8,16},{9,17},{10,... | collective-permute-start | bytes 786440 | tf_op jit(solution)/shard_map/ppermute | solution.py:358
  14.6 21.5 %collective-permute-start.6 = (f32[2,4,128,128]{3,2,1,0:T(8,128)S(1)}, f32[2,4,128,128]{3,2,1,0:T(8,128)S(1)}, u32[]{:S(2)}, u32[]{:S(2)}) collective-permute-start(f32[2,4,128,128]{3,2,1,0:T(8,128)S(1)} %share.3.refs_4_), channel_id=1, source_target_pairs={{0,4},{4,0},{8,12},{12,8},{16,20},{20,16},{24,28},{28,24},{1,5},{5... | collective-permute-start | bytes 1572872 | tf_op jit(solution)/shard_map/ppermute | solution.py:270
  22.4 9.2 %collective-permute-start.7 = (f32[4,128,128]{2,1,0:T(8,128)S(1)}, f32[4,128,128]{2,1,0:T(8,128)S(1)}, u32[]{:S(2)}, u32[]{:S(2)}) collective-permute-start(f32[4,128,128]{2,1,0:T(8,128)S(1)} %hop.13.refs_2_), channel_id=1, source_target_pairs={{0,8},{1,9},{2,10},{3,11},{4,12},{5,13},{6,14},{7,15},{8,0},{9,1},... | collective-permute-start | bytes 786440 | tf_op jit(solution)/shard_map/ppermute | solution.py:358
  23.3 3.3 %collective-permute-start.4 = (f32[4,128,128]{2,1,0:T(8,128)S(1)}, f32[4,128,128]{2,1,0:T(8,128)S(1)}, u32[]{:S(2)}, u32[]{:S(2)}) collective-permute-start(f32[4,128,128]{2,1,0:T(8,128)S(1)} %hop.14.refs_4_), channel_id=1, source_target_pairs={{0,1},{1,0},{2,3},{3,2},{4,5},{5,4},{6,7},{7,6},{8,16},{9,17},{10,... | collective-permute-start | bytes 786440 | tf_op jit(solution)/shard_map/ppermute | solution.py:358
  26.8 9.2 %collective-permute-start.5 = (f32[4,128,128]{2,1,0:T(8,128)S(1)}, f32[4,128,128]{2,1,0:T(8,128)S(1)}, u32[]{:S(2)}, u32[]{:S(2)}) collective-permute-start(f32[4,128,128]{2,1,0:T(8,128)S(1)} %hop.15.refs_3_), channel_id=1, source_target_pairs={{0,8},{1,9},{2,10},{3,11},{4,12},{5,13},{6,14},{7,15},{8,0},{9,1},... | collective-permute-start | bytes 786440 | tf_op jit(solution)/shard_map/ppermute | solution.py:358
  31.6 4.4 %collective-permute-start.8 = (f32[4,128,128]{2,1,0:T(8,128)S(1)}, f32[4,128,128]{2,1,0:T(8,128)S(1)}, u32[]{:S(2)}, u32[]{:S(2)}) collective-permute-start(f32[4,128,128]{2,1,0:T(8,128)S(1)} %hop.16.refs_4_), channel_id=1, source_target_pairs={{0,1},{1,0},{2,3},{3,2},{4,5},{5,4},{6,7},{7,6},{8,16},{9,17},{10,... | collective-permute-start | bytes 786440 | tf_op jit(solution)/shard_map/ppermute | solution.py:358
  31.9 12.7 %collective-permute-start.13 = (f32[4,128,128]{2,1,0:T(8,128)S(1)}, f32[4,128,128]{2,1,0:T(8,128)S(1)}, u32[]{:S(2)}, u32[]{:S(2)}) collective-permute-start(f32[4,128,128]{2,1,0:T(8,128)S(1)} %trade.2.refs_4_), channel_id=1, source_target_pairs={{0,4},{4,0},{8,12},{12,8},{16,20},{20,16},{24,28},{28,24},{1,5},{5... | collective-permute-start | bytes 786440 | tf_op jit(solution)/shard_map/ppermute | solution.py:292
  36.0 8.4 %collective-permute-start.9 = (f32[4,128,128]{2,1,0:T(8,128)S(1)}, f32[4,128,128]{2,1,0:T(8,128)S(1)}, u32[]{:S(2)}, u32[]{:S(2)}) collective-permute-start(f32[4,128,128]{2,1,0:T(8,128)S(1)} %hop.17.refs_3_), channel_id=1, source_target_pairs={{0,1},{1,0},{2,3},{3,2},{4,5},{5,4},{6,7},{7,6},{8,16},{9,17},{10,... | collective-permute-start | bytes 786440 | tf_op jit(solution)/shard_map/ppermute | solution.py:358
  36.2 9.9 %collective-permute-start.12 = (f32[4,128,128]{2,1,0:T(8,128)S(1)}, f32[4,128,128]{2,1,0:T(8,128)S(1)}, u32[]{:S(2)}, u32[]{:S(2)}) collective-permute-start(f32[4,128,128]{2,1,0:T(8,128)S(1)} %hop.18.refs_5_), channel_id=1, source_target_pairs={{0,8},{1,9},{2,10},{3,11},{4,12},{5,13},{6,14},{7,15},{8,0},{9,1},... | collective-permute-start | bytes 786440 | tf_op jit(solution)/shard_map/ppermute | solution.py:358
  40.1 11.7 %collective-permute-start.11 = (f32[2,4,128,128]{3,2,1,0:T(8,128)S(1)}, f32[2,4,128,128]{3,2,1,0:T(8,128)S(1)}, u32[]{:S(2)}, u32[]{:S(2)}) collective-permute-start(f32[2,4,128,128]{3,2,1,0:T(8,128)S(1)} %trade.3.refs_4_), channel_id=1, source_target_pairs={{0,4},{4,0},{8,12},{12,8},{16,20},{20,16},{24,28},{28,24},{1,5},{5... | collective-permute-start | bytes 1572872 | tf_op jit(solution)/shard_map/ppermute | solution.py:292
  44.4 7.4 %collective-permute-start.10 = (f32[4,128,128]{2,1,0:T(8,128)S(1)}, f32[4,128,128]{2,1,0:T(8,128)S(1)}, u32[]{:S(2)}, u32[]{:S(2)}) collective-permute-start(f32[4,128,128]{2,1,0:T(8,128)S(1)} %hop.19.refs_18_), channel_id=1, source_target_pairs={{0,8},{1,9},{2,10},{3,11},{4,12},{5,13},{6,14},{7,15},{8,0},{9,1},... | collective-permute-start | bytes 786440 | tf_op jit(solution)/shard_map/ppermute | solution.py:358

commit v5 on v4

--- a/solution.py
+++ b/solution.py
@@ -17,7 +17,7 @@
 HBM = pl.BlockSpec(memory_space=pltpu.HBM)
 ACROSS_ROWS = 256
 ORDER = (
-    "L023", "E0", "S0", "L1", "E1", "W20", "O1", "S1", "W21", "W00", "E2", "O2", "W01", "W10",
+    "F", "E0", "S0", "L0123", "E1", "O1", "W20", "S1", "W21", "O2", "E2", "W00", "W01", "W10",
     "E3", "O3", "X0", "W11", "O4", "E4", "X1", "W30", "W31", "E5", "A0", "A2", "A31",
 )
 PARAMS = pltpu.CompilerParams(vmem_limit_bytes=8 << 20)
@@ -42,6 +42,50 @@
 def spot():
     place = lax.axis_index("ctx")
     return place // 2, place % 2
+
+
+def first_kernel(firsts, chain, q_hbm, k_hbm, v_hbm, g_hbm, opening_ref, shared_ref, a_ref, b_ref, sems):
+    row, _ = spot()
+    size = opening_ref.shape[0]
+    upper = row < chain // 2
+
+    def moves(a_hbm, b_hbm):
+        for n, first in enumerate(firsts):
+            there = pl.ds(first * DH, size * DH)
+            yield pltpu.make_async_copy(a_hbm.at[:, there], a_ref.at[n], sems.at[n, 0])
+            yield pltpu.make_async_copy(b_hbm.at[:, there], b_ref.at[n], sems.at[n, 1])
+
+    @pl.when(upper)
+    def _():
+        for move in moves(k_hbm, v_hbm):
+            move.start()
+
+    @pl.when(jnp.logical_not(upper))
+    def _():
+        for move in moves(q_hbm, g_hbm):
+            move.start()
+
+    waits = list(moves(k_hbm, v_hbm))
+    for n, out in enumerate((opening_ref, shared_ref.at[0], shared_ref.at[1])):
+        waits[2 * n].wait()
+        waits[2 * n + 1].wait()
+        for h in range(size):
+            cols = slice(h * DH, (h + 1) * DH)
+            out[h] = dot(a_ref[n, :, cols], b_ref[n, :, cols], ROWS)
+
+
+def first_states(arrays, firsts, size, chain):
+    block = (3, arrays[0].shape[0], size * DH)
+    return pl.pallas_call(
+        functools.partial(first_kernel, firsts, chain),
+        in_specs=[HBM] * 4,
+        out_specs=[VMEM] * 2,
+        out_shape=[pltpu.VMEM((size, DH, DH), F32), pltpu.VMEM((2, size, DH, DH), F32)],
+        scratch_shapes=[pltpu.VMEM(block, BF16), pltpu.VMEM(block, BF16), pltpu.SemaphoreType.DMA((3, 2))],
+        compiler_params=PARAMS,
+        cost_estimate=cost(2.5),
+        name="first",
+    )(*[pltpu.with_memory_space_constraint(a, pltpu.HBM) for a in arrays])
 
 
 def load_kernel(firsts, q_hbm, k_hbm, v_hbm, g_hbm, *refs):
@@ -205,7 +249,7 @@
     pieces = min(size, 2)
     local = [[None] * pieces for _ in range(parts)]
     got, turns, swapped = {}, {}, {}
-    last = []
+    last, opening = [], []
     pair = [(r, r ^ 1) for r in range(runs)]
 
     def early(row):
@@ -244,12 +288,19 @@
             *run[p], own[p] = found[5 * n : 5 * n + 5]
         last[:] = [own[chosen[0]]]
 
+    def begin():
+        opening[:] = first_states(arrays, [p * size for p in (0, 2, 3)], size, chain)
+        last[:] = [opening[0]]
+
     def inside(p, piece):
         wide = max(1, size // 2)
         local[p][piece] = within(run[p], piece * wide, wide * DH, last)
         last[:] = [local[p][piece][0]]
 
     def share(turn):
+        if opening and not turn:
+            turns[0] = lax.ppermute(opening[1], "ctx", pair)
+            return
         values = [own[2], own[3]]
         if turn and relay:
             values += [own[0], got[0, 0]]
@@ -353,8 +404,11 @@
                 payload = jnp.where(end(row), refs["turns", 1][1], payload)
             out[...] = payload
 
-        payload = mix(function, shape, values, last, "hop")
-        last[:] = [payload]
+        if opening and (parity, slot) == (0, 0):
+            payload = opening[0]
+        else:
+            payload = mix(function, shape, values, last, "hop")
+            last[:] = [payload]
         got[parity, slot] = lax.ppermute(payload, ("ctx", "seq"), swap(parity))
 
     outs = [None]
@@ -396,7 +450,7 @@
         outs[0], token = across(jobs, outs[0], arrays[0].shape, size, last)
         last[:] = [token]
 
-    steps = {"L": bring, "S": share, "X": trade, "E": functools.partial(hop, 0), "O": functools.partial(hop, 1), "W": inside, "A": finish}
+    steps = {"F": begin, "L": bring, "S": share, "X": trade, "E": functools.partial(hop, 0), "O": functools.partial(hop, 1), "W": inside, "A": finish}
     order = [(name[0], [int(n) for n in name[1:]]) for name in ORDER]
     if chain != 4:
         order = [("L", [2, 3]), ("L", [0, 1]), ("S", [0]), ("S", [1])]

time: 55.2 us -> 52.8 us (0.957)
  starting transfers between devices: 19.4 us -> 15 us
  waiting for transfers between devices: 8.57 us -> 9.7 us
  Pallas kernels: 26.1 us -> 26.9 us
    ppermute x10, starting transfers between devices: 13.6 us -> 9.51 us  [hop(): got[parity, slot] = lax.ppermute(payload, ('ctx', 'seq'), swap(parity))]
    ppermute x10, waiting for transfers between devices: 3.94 us -> 7.54 us  [hop(): got[parity, slot] = lax.ppermute(payload, ('ctx', 'seq'), swap(parity))]
    pallas_call x0 -> x1, Pallas kernels: none -> 2.33 us  [first_states(): pl.pallas_call(functools.partial(first_kernel, firsts, chain), in_specs=[...]
    ppermute x2 -> x1, waiting for transfers between devices: 2.29 us -> 0.01 us  [share(): turns[turn] = lax.ppermute(payload, 'ctx', pair)]
    ppermute x2 -> x1, starting transfers between devices: 3.74 us -> 1.75 us  [share(): turns[turn] = lax.ppermute(payload, 'ctx', pair)]
    ppermute x2, waiting for transfers between devices: 2.34 us -> 0.69 us  [trade(): swapped[p] = lax.ppermute(payload, 'ctx', pair)]
    ppermute x0 -> x1, starting transfers between devices: none -> 1.49 us  [share(): turns[0] = lax.ppermute(opening[1], 'ctx', pair)]
    ppermute x0 -> x1, waiting for transfers between devices: none -> 1.46 us  [share(): turns[0] = lax.ppermute(opening[1], 'ctx', pair)]
  transfers between devices with their start and end apart: 14 -> 14, of which waited for: 5 -> 8; matrix products, arithmetic and copies ran while one was open for 0% -> 0% of each run, Pallas kernels for 35% -> 41%
where the time goes in v5:
time: 52.8 us; the launch traced here: 52.6 us
  Pallas kernels  26.9 us (51%)
  starting transfers between devices  15 us (28%)
  waiting for transfers between devices  9.7 us (18%)
  between operations  1 us (2%)
    pallas_call x8, Pallas kernels, within(): pl.pallas_call(functools.partial(within_kernel, min(rows, 256), first), i...  12.9 us
    ppermute x10, starting transfers between devices, hop(): got[parity, slot] = lax.ppermute(payload, ('ctx', 'seq'), swap(parity))  9.51 us
    ppermute x10, waiting for transfers between devices, hop(): got[parity, slot] = lax.ppermute(payload, ('ctx', 'seq'), swap(parity))  7.54 us
    pallas_call x3, Pallas kernels, across(): pl.pallas_call(functools.partial(across_kernel, [(total, first, len(parts...  6.45 us
    pallas_call x1, Pallas kernels, load(): pl.pallas_call(functools.partial(load_kernel, firsts), in_specs=[HBM] * 4...  4.17 us
    pallas_call x1, Pallas kernels, first_states(): pl.pallas_call(functools.partial(first_kernel, firsts, chain), in_specs=[...  2.33 us
    ppermute x2, starting transfers between devices, trade(): swapped[p] = lax.ppermute(payload, 'ctx', pair)  2.26 us
    ppermute x1, starting transfers between devices, share(): turns[turn] = lax.ppermute(payload, 'ctx', pair)  1.75 us
  transfers between devices with their start and end apart: 14, of which 8 were waited for; matrix products, arithmetic and copies ran while one was open for 0% of the time, Pallas kernels for 41%

profile of v5, /device:TPU:0, one launch (start us, length us, event | category | flops | bytes accessed | tf_op | source)
XLA Modules:
  0.0 52.6 jit_solution(8524198115683258930)
XLA Ops:
  0.6 2.3 %first.1 = (f32[4,128,128]{2,1,0:T(8,128)S(1)}, f32[2,4,128,128]{3,2,1,0:T(8,128)S(1)}) custom-call(bf16[512,2048]{1,0:T(8,128)(2,1)} %q_hbm.3, bf16[512,2048]{1,0:T(8,128)(2,1)} %k_hbm.3, bf16[512,2048]{1,0:T(8,128)(2,1)} %v_hbm.3, bf16[512,2048]{1,0:T(8,128)(2,1)} %g_hbm.3), custom_call_target="tpu_custom_call" | custom-call | flops 2875000064 | bytes 1 | tf_op jit(solution)/shard_map/first/pallas_call | solution.py:79
  3.0 3.1 %collective-permute-start.2 = (f32[4,128,128]{2,1,0:T(8,128)S(1)}, f32[4,128,128]{2,1,0:T(8,128)S(1)}, u32[]{:S(2)}, u32[]{:S(2)}) collective-permute-start(f32[4,128,128]{2,1,0:T(8,128)S(1)} %get-tuple-element.72.refs_0_), channel_id=1, source_target_pairs={{0,8},{1,9},{2,10},{3,11},{4,12},{5,13},{6,14},{7,15},{8,0},{9,1},... | collective-permute-start | bytes 786440 | tf_op jit(solution)/shard_map/ppermute | solution.py:412
  6.1 1.5 %collective-permute-start.1 = (f32[2,4,128,128]{3,2,1,0:T(8,128)S(1)}, f32[2,4,128,128]{3,2,1,0:T(8,128)S(1)}, u32[]{:S(2)}, u32[]{:S(2)}) collective-permute-start(f32[2,4,128,128]{3,2,1,0:T(8,128)S(1)} %get-tuple-element.80), channel_id=1, source_target_pairs={{0,4},{4,0},{8,12},{12,8},{16,20},{20,16},{24,28},{28,24},{1,5},{5... | collective-permute-start | bytes 1572872 | tf_op jit(solution)/shard_map/ppermute | solution.py:302
  7.5 4.2 %load.1 = (bf16[512,512]{1,0:T(8,128)(2,1)S(1)}, bf16[512,512]{1,0:T(8,128)(2,1)S(1)}, bf16[512,512]{1,0:T(8,128)(2,1)S(1)}, bf16[512,512]{1,0:T(8,128)(2,1)S(1)...) custom-call(bf16[512,2048]{1,0:T(8,128)(2,1)} %q_hbm.3, ...), custom_call_target="tpu_custom_call" | custom-call | flops 4024999936 | bytes 1 | tf_op jit(solution)/shard_map/load/pallas_call | solution.py:118
  12.5 1.8 %within.8 = (f32[512,256]{1,0:T(8,128)S(1)}, f32[512,256]{1,0:T(8,128)S(1)}, f32[512,256]{1,0:T(8,128)S(1)}, f32[512,256]{1,0:T(8,128)S(1)}) custom-call(bf16[512,512]{1,0:T(8,128)(2,1)S(1)} %get-tuple-element.81.refs_0_, bf16[512,512]{1,0:T(8,128)(2,1)S(1)} %get-tuple-element.82.refs_1_, bf16[512,512]{1,0:T(8,128)(2,1)S(1)} %get-tuple-element.83.refs_2_, ...), custom_call_target="tpu_custom_call" | custom-call | flops 1724999936 | bytes 1 | tf_op jit(solution)/shard_map/within/pallas_call | solution.py:159
  14.5 1.8 %collective-permute-start.6 = (f32[2,4,128,128]{3,2,1,0:T(8,128)S(1)}, f32[2,4,128,128]{3,2,1,0:T(8,128)S(1)}, u32[]{:S(2)}, u32[]{:S(2)}) collective-permute-start(f32[2,4,128,128]{3,2,1,0:T(8,128)S(1)} %share.1.refs_4_), channel_id=1, source_target_pairs={{0,4},{4,0},{8,12},{12,8},{16,20},{20,16},{24,28},{28,24},{1,5},{5... | collective-permute-start | bytes 1572872 | tf_op jit(solution)/shard_map/ppermute | solution.py:321
  16.2 1.6 %within.9 = (f32[512,256]{1,0:T(8,128)S(1)}, f32[512,256]{1,0:T(8,128)S(1)}, f32[512,256]{1,0:T(8,128)S(1)}, f32[512,256]{1,0:T(8,128)S(1)}) custom-call(bf16[512,512]{1,0:T(8,128)(2,1)S(1)} %get-tuple-element.81.refs_0_, bf16[512,512]{1,0:T(8,128)(2,1)S(1)} %get-tuple-element.82.refs_1_, bf16[512,512]{1,0:T(8,128)(2,1)S(1)} %get-tuple-element.83.refs_2_, ...), custom_call_target="tpu_custom_call" | custom-call | flops 1724999936 | bytes 1 | tf_op jit(solution)/shard_map/within/pallas_call | solution.py:159
  17.8 1.5 %collective-permute-done.refs_1_.refs_30_ = f32[4,128,128]{2,1,0:T(8,128)S(1)} collective-permute-done((f32[4,128,128]{2,1,0:T(8,128)S(1)}, f32[4,128,128]{2,1,0:T(8,128)S(1)}, u32[]{:S(2)}, u32[]{:S(2)}) %collective-permute-start) | collective-permute-done | bytes 262176 | tf_op jit(solution)/shard_map/ppermute | solution.py:412
  19.5 1.5 %collective-permute-done.1.refs_1_.refs_15_ = f32[2,4,128,128]{3,2,1,0:T(8,128)S(1)} collective-permute-done((f32[2,4,128,128]{3,2,1,0:T(8,128)S(1)}, f32[2,4,128,128]{3,2,1,0:T(8,128)S(1)}, u32[]{:S(2)}, u32[]{:S(2)}) %collective-permute-start.1) | collective-permute-done | bytes 524320 | tf_op jit(solution)/shard_map/ppermute | solution.py:302
  21.0 1.8 %collective-permute-start.7 = (f32[4,128,128]{2,1,0:T(8,128)S(1)}, f32[4,128,128]{2,1,0:T(8,128)S(1)}, u32[]{:S(2)}, u32[]{:S(2)}) collective-permute-start(f32[4,128,128]{2,1,0:T(8,128)S(1)} %hop.12.refs_4_), channel_id=1, source_target_pairs={{0,8},{1,9},{2,10},{3,11},{4,12},{5,13},{6,14},{7,15},{8,0},{9,1},... | collective-permute-start | bytes 786440 | tf_op jit(solution)/shard_map/ppermute | solution.py:412
  22.8 1.6 %within.10 = (f32[512,256]{1,0:T(8,128)S(1)}, f32[512,256]{1,0:T(8,128)S(1)}, f32[512,256]{1,0:T(8,128)S(1)}, f32[512,256]{1,0:T(8,128)S(1)}) custom-call(bf16[512,512]{1,0:T(8,128)(2,1)S(1)} %get-tuple-element.92.refs_0_, bf16[512,512]{1,0:T(8,128)(2,1)S(1)} %get-tuple-element.93.refs_1_, bf16[512,512]{1,0:T(8,128)(2,1)S(1)} %get-tuple-element.94.refs_2_, ...), custom_call_target="tpu_custom_call" | custom-call | flops 1724999936 | bytes 1 | tf_op jit(solution)/shard_map/within/pallas_call | solution.py:159
  24.4 1.6 %within.11 = (f32[512,256]{1,0:T(8,128)S(1)}, f32[512,256]{1,0:T(8,128)S(1)}, f32[512,256]{1,0:T(8,128)S(1)}, f32[512,256]{1,0:T(8,128)S(1)}) custom-call(bf16[512,512]{1,0:T(8,128)(2,1)S(1)} %get-tuple-element.92.refs_0_, bf16[512,512]{1,0:T(8,128)(2,1)S(1)} %get-tuple-element.93.refs_1_, bf16[512,512]{1,0:T(8,128)(2,1)S(1)} %get-tuple-element.94.refs_2_, ...), custom_call_target="tpu_custom_call" | custom-call | flops 1724999936 | bytes 1 | tf_op jit(solution)/shard_map/within/pallas_call | solution.py:159
  26.0 1.6 %within.12 = (f32[512,256]{1,0:T(8,128)S(1)}, f32[512,256]{1,0:T(8,128)S(1)}, f32[512,256]{1,0:T(8,128)S(1)}, f32[512,256]{1,0:T(8,128)S(1)}) custom-call(bf16[512,512]{1,0:T(8,128)(2,1)S(1)} %get-tuple-element.88.refs_0_.refs_18_, bf16[512,512]{1,0:T(8,128)(2,1)S(1)} %get-tuple-element.89.refs_1_.refs_19_, ...), custom_call_target="tpu_custom_call" | custom-call | flops 1724999936 | bytes 1 | tf_op jit(solution)/shard_map/within/pallas_call | solution.py:159
  28.7 1.2 %collective-permute-start.13 = (f32[4,128,128]{2,1,0:T(8,128)S(1)}, f32[4,128,128]{2,1,0:T(8,128)S(1)}, u32[]{:S(2)}, u32[]{:S(2)}) collective-permute-start(f32[4,128,128]{2,1,0:T(8,128)S(1)} %trade.2.refs_4_), channel_id=1, source_target_pairs={{0,4},{4,0},{8,12},{12,8},{16,20},{20,16},{24,28},{28,24},{1,5},{5... | collective-permute-start | bytes 786440 | tf_op jit(solution)/shard_map/ppermute | solution.py:343
  29.9 1.6 %within.13 = (f32[512,256]{1,0:T(8,128)S(1)}, f32[512,256]{1,0:T(8,128)S(1)}, f32[512,256]{1,0:T(8,128)S(1)}, f32[512,256]{1,0:T(8,128)S(1)}) custom-call(bf16[512,512]{1,0:T(8,128)(2,1)S(1)} %get-tuple-element.88.refs_0_.refs_18_, bf16[512,512]{1,0:T(8,128)(2,1)S(1)} %get-tuple-element.89.refs_1_.refs_19_, ...), custom_call_target="tpu_custom_call" | custom-call | flops 1724999936 | bytes 1 | tf_op jit(solution)/shard_map/within/pallas_call | solution.py:159
  31.5 2.6 %collective-permute-done.5.refs_2_.refs_12_.refs_31_ = f32[4,128,128]{2,1,0:T(8,128)S(1)} collective-permute-done((f32[4,128,128]{2,1,0:T(8,128)S(1)}, f32[4,128,128]{2,1,0:T(8,128)S(1)}, u32[]{:S(2)}, u32[]{:S(2)}) %collective-permute-start.5) | collective-permute-done | bytes 262176 | tf_op jit(solution)/shard_map/ppermute | solution.py:412
  34.3 3.0 %collective-permute-start.12 = (f32[4,128,128]{2,1,0:T(8,128)S(1)}, f32[4,128,128]{2,1,0:T(8,128)S(1)}, u32[]{:S(2)}, u32[]{:S(2)}) collective-permute-start(f32[4,128,128]{2,1,0:T(8,128)S(1)} %hop.16.refs_5_), channel_id=1, source_target_pairs={{0,8},{1,9},{2,10},{3,11},{4,12},{5,13},{6,14},{7,15},{8,0},{9,1},... | collective-permute-start | bytes 786440 | tf_op jit(solution)/shard_map/ppermute | solution.py:412
  37.5 1.1 %collective-permute-start.11 = (f32[2,4,128,128]{3,2,1,0:T(8,128)S(1)}, f32[2,4,128,128]{3,2,1,0:T(8,128)S(1)}, u32[]{:S(2)}, u32[]{:S(2)}) collective-permute-start(f32[2,4,128,128]{3,2,1,0:T(8,128)S(1)} %trade.3.refs_4_), channel_id=1, source_target_pairs={{0,4},{4,0},{8,12},{12,8},{16,20},{20,16},{24,28},{28,24},{1,5},{5... | collective-permute-start | bytes 1572872 | tf_op jit(solution)/shard_map/ppermute | solution.py:343
  38.6 1.6 %within.14 = (f32[512,256]{1,0:T(8,128)S(1)}, f32[512,256]{1,0:T(8,128)S(1)}, f32[512,256]{1,0:T(8,128)S(1)}, f32[512,256]{1,0:T(8,128)S(1)}) custom-call(bf16[512,512]{1,0:T(8,128)(2,1)S(1)} %get-tuple-element.73.refs_0_, bf16[512,512]{1,0:T(8,128)(2,1)S(1)} %get-tuple-element.74.refs_1_, bf16[512,512]{1,0:T(8,128)(2,1)S(1)} %get-tuple-element.75.refs_2_, ...), custom_call_target="tpu_custom_call" | custom-call | flops 1724999936 | bytes 1 | tf_op jit(solution)/shard_map/within/pallas_call | solution.py:159
  40.2 1.6 %within.15 = (f32[512,256]{1,0:T(8,128)S(1)}, f32[512,256]{1,0:T(8,128)S(1)}, f32[512,256]{1,0:T(8,128)S(1)}, f32[512,256]{1,0:T(8,128)S(1)}) custom-call(bf16[512,512]{1,0:T(8,128)(2,1)S(1)} %get-tuple-element.73.refs_0_, bf16[512,512]{1,0:T(8,128)(2,1)S(1)} %get-tuple-element.74.refs_1_, bf16[512,512]{1,0:T(8,128)(2,1)S(1)} %get-tuple-element.75.refs_2_, ...), custom_call_target="tpu_custom_call" | custom-call | flops 1724999936 | bytes 1 | tf_op jit(solution)/shard_map/within/pallas_call | solution.py:159
  42.4 1.8 %collective-permute-done.12.refs_17_.refs_13_ = f32[4,128,128]{2,1,0:T(8,128)S(1)} collective-permute-done((f32[4,128,128]{2,1,0:T(8,128)S(1)}, f32[4,128,128]{2,1,0:T(8,128)S(1)}, u32[]{:S(2)}, u32[]{:S(2)}) %collective-permute-start.12) | collective-permute-done | bytes 262176 | tf_op jit(solution)/shard_map/ppermute | solution.py:412
  44.2 1.7 %across.3 = (bf16[512,2048]{1,0:T(8,128)(2,1)}, bf16[512,2048]{1,0:T(8,128)(2,1)}, bf16[512,2048]{1,0:T(8,128)(2,1)}, bf16[512,2048]{1,0:T(8,128)(2,1)}, f32[8,128]{1,0:T(8,128)S(1)}) custom-call(bf16[512,512]{1,0:T(8,128)(2,1)S(1)} %get-tuple-element.92.refs_0_, bf16[512,512]{1,0:T(8,128)(2,1)S(1)} %get-tuple-element.93.refs_1_, ...), custom_call_target="tpu_custom_call" | custom-call | flops 1724999936 | bytes 1 | tf_op jit(solution)/shard_map/across/pallas_call | solution.py:220
  45.9 1.7 %across.4 = (bf16[512,2048]{1,0:T(8,128)(2,1)}, bf16[512,2048]{1,0:T(8,128)(2,1)}, bf16[512,2048]{1,0:T(8,128)(2,1)}, bf16[512,2048]{1,0:T(8,128)(2,1)}, f32[8,128]{1,0:T(8,128)S(1)}) custom-call(bf16[512,512]{1,0:T(8,128)(2,1)S(1)} %get-tuple-element.81.refs_0_, ...), custom_call_target="tpu_custom_call", output_to_operand_aliasing={{0}: (17, {}), {1}: (18, {}), {2}: (19, {}), {3}: (20, {})} | custom-call | flops 1724999936 | bytes 1 | tf_op jit(solution)/shard_map/across/pallas_call | solution.py:220
  49.4 3.1 %across.5 = (bf16[512,2048]{1,0:T(8,128)(2,1)}, bf16[512,2048]{1,0:T(8,128)(2,1)}, bf16[512,2048]{1,0:T(8,128)(2,1)}, bf16[512,2048]{1,0:T(8,128)(2,1)}, f32[8,128]{1,0:T(8,128)}) custom-call(bf16[512,512]{1,0:T(8,128)(2,1)S(1)} %get-tuple-element.73.refs_0_, ...), custom_call_target="tpu_custom_call", output_to_operand_aliasing={{0}: (34, {}), {1}: (35, {}), {2}: (36, {}), {3}: (37, {})} | custom-call | flops 3449999872 | bytes 1 | tf_op jit(solution)/shard_map/across/pallas_call | solution.py:220
  (29 shorter events, 5.0 us)
Async XLA Ops:
  3.0 9.4 %collective-permute-start.2 = (f32[4,128,128]{2,1,0:T(8,128)S(1)}, f32[4,128,128]{2,1,0:T(8,128)S(1)}, u32[]{:S(2)}, u32[]{:S(2)}) collective-permute-start(f32[4,128,128]{2,1,0:T(8,128)S(1)} %get-tuple-element.72.refs_0_), channel_id=1, source_target_pairs={{0,8},{1,9},{2,10},{3,11},{4,12},{5,13},{6,14},{7,15},{8,0},{9,1},... | collective-permute-start | bytes 786440 | tf_op jit(solution)/shard_map/ppermute | solution.py:412
  6.1 14.9 %collective-permute-start.1 = (f32[2,4,128,128]{3,2,1,0:T(8,128)S(1)}, f32[2,4,128,128]{3,2,1,0:T(8,128)S(1)}, u32[]{:S(2)}, u32[]{:S(2)}) collective-permute-start(f32[2,4,128,128]{3,2,1,0:T(8,128)S(1)} %get-tuple-element.80), channel_id=1, source_target_pairs={{0,4},{4,0},{8,12},{12,8},{16,20},{20,16},{24,28},{28,24},{1,5},{5... | collective-permute-start | bytes 1572872 | tf_op jit(solution)/shard_map/ppermute | solution.py:302
  11.8 7.6 %collective-permute-start = (f32[4,128,128]{2,1,0:T(8,128)S(1)}, f32[4,128,128]{2,1,0:T(8,128)S(1)}, u32[]{:S(2)}, u32[]{:S(2)}) collective-permute-start(f32[4,128,128]{2,1,0:T(8,128)S(1)} %hop.9.refs_2_), channel_id=1, source_target_pairs={{0,8},{1,9},{2,10},{3,11},{4,12},{5,13},{6,14},{7,15},{8,0},{9,1},... | collective-permute-start | bytes 786440 | tf_op jit(solution)/shard_map/ppermute | solution.py:412
  12.4 8.5 %collective-permute-start.4 = (f32[4,128,128]{2,1,0:T(8,128)S(1)}, f32[4,128,128]{2,1,0:T(8,128)S(1)}, u32[]{:S(2)}, u32[]{:S(2)}) collective-permute-start(f32[4,128,128]{2,1,0:T(8,128)S(1)} %hop.10.refs_4_), channel_id=1, source_target_pairs={{0,1},{1,0},{2,3},{3,2},{4,5},{5,4},{6,7},{7,6},{8,16},{9,17},{10,... | collective-permute-start | bytes 786440 | tf_op jit(solution)/shard_map/ppermute | solution.py:412
  14.5 19.8 %collective-permute-start.6 = (f32[2,4,128,128]{3,2,1,0:T(8,128)S(1)}, f32[2,4,128,128]{3,2,1,0:T(8,128)S(1)}, u32[]{:S(2)}, u32[]{:S(2)}) collective-permute-start(f32[2,4,128,128]{3,2,1,0:T(8,128)S(1)} %share.1.refs_4_), channel_id=1, source_target_pairs={{0,4},{4,0},{8,12},{12,8},{16,20},{20,16},{24,28},{28,24},{1,5},{5... | collective-permute-start | bytes 1572872 | tf_op jit(solution)/shard_map/ppermute | solution.py:321
  19.4 8.2 %collective-permute-start.3 = (f32[4,128,128]{2,1,0:T(8,128)S(1)}, f32[4,128,128]{2,1,0:T(8,128)S(1)}, u32[]{:S(2)}, u32[]{:S(2)}) collective-permute-start(f32[4,128,128]{2,1,0:T(8,128)S(1)} %hop.11.refs_4_), channel_id=1, source_target_pairs={{0,1},{1,0},{2,3},{3,2},{4,5},{5,4},{6,7},{7,6},{8,16},{9,17},{10,... | collective-permute-start | bytes 786440 | tf_op jit(solution)/shard_map/ppermute | solution.py:412
  21.0 7.5 %collective-permute-start.7 = (f32[4,128,128]{2,1,0:T(8,128)S(1)}, f32[4,128,128]{2,1,0:T(8,128)S(1)}, u32[]{:S(2)}, u32[]{:S(2)}) collective-permute-start(f32[4,128,128]{2,1,0:T(8,128)S(1)} %hop.12.refs_4_), channel_id=1, source_target_pairs={{0,8},{1,9},{2,10},{3,11},{4,12},{5,13},{6,14},{7,15},{8,0},{9,1},... | collective-permute-start | bytes 786440 | tf_op jit(solution)/shard_map/ppermute | solution.py:412
  27.7 6.4 %collective-permute-start.5 = (f32[4,128,128]{2,1,0:T(8,128)S(1)}, f32[4,128,128]{2,1,0:T(8,128)S(1)}, u32[]{:S(2)}, u32[]{:S(2)}) collective-permute-start(f32[4,128,128]{2,1,0:T(8,128)S(1)} %hop.13.refs_3_), channel_id=1, source_target_pairs={{0,8},{1,9},{2,10},{3,11},{4,12},{5,13},{6,14},{7,15},{8,0},{9,1},... | collective-permute-start | bytes 786440 | tf_op jit(solution)/shard_map/ppermute | solution.py:412
  28.5 5.7 %collective-permute-start.8 = (f32[4,128,128]{2,1,0:T(8,128)S(1)}, f32[4,128,128]{2,1,0:T(8,128)S(1)}, u32[]{:S(2)}, u32[]{:S(2)}) collective-permute-start(f32[4,128,128]{2,1,0:T(8,128)S(1)} %hop.14.refs_4_), channel_id=1, source_target_pairs={{0,1},{1,0},{2,3},{3,2},{4,5},{5,4},{6,7},{7,6},{8,16},{9,17},{10,... | collective-permute-start | bytes 786440 | tf_op jit(solution)/shard_map/ppermute | solution.py:412
  28.7 13.6 %collective-permute-start.13 = (f32[4,128,128]{2,1,0:T(8,128)S(1)}, f32[4,128,128]{2,1,0:T(8,128)S(1)}, u32[]{:S(2)}, u32[]{:S(2)}) collective-permute-start(f32[4,128,128]{2,1,0:T(8,128)S(1)} %trade.2.refs_4_), channel_id=1, source_target_pairs={{0,4},{4,0},{8,12},{12,8},{16,20},{20,16},{24,28},{28,24},{1,5},{5... | collective-permute-start | bytes 786440 | tf_op jit(solution)/shard_map/ppermute | solution.py:343
  34.2 7.6 %collective-permute-start.9 = (f32[4,128,128]{2,1,0:T(8,128)S(1)}, f32[4,128,128]{2,1,0:T(8,128)S(1)}, u32[]{:S(2)}, u32[]{:S(2)}) collective-permute-start(f32[4,128,128]{2,1,0:T(8,128)S(1)} %hop.15.refs_3_), channel_id=1, source_target_pairs={{0,1},{1,0},{2,3},{3,2},{4,5},{5,4},{6,7},{7,6},{8,16},{9,17},{10,... | collective-permute-start | bytes 786440 | tf_op jit(solution)/shard_map/ppermute | solution.py:412
  34.3 9.9 %collective-permute-start.12 = (f32[4,128,128]{2,1,0:T(8,128)S(1)}, f32[4,128,128]{2,1,0:T(8,128)S(1)}, u32[]{:S(2)}, u32[]{:S(2)}) collective-permute-start(f32[4,128,128]{2,1,0:T(8,128)S(1)} %hop.16.refs_5_), channel_id=1, source_target_pairs={{0,8},{1,9},{2,10},{3,11},{4,12},{5,13},{6,14},{7,15},{8,0},{9,1},... | collective-permute-start | bytes 786440 | tf_op jit(solution)/shard_map/ppermute | solution.py:412
  37.5 11.9 %collective-permute-start.11 = (f32[2,4,128,128]{3,2,1,0:T(8,128)S(1)}, f32[2,4,128,128]{3,2,1,0:T(8,128)S(1)}, u32[]{:S(2)}, u32[]{:S(2)}) collective-permute-start(f32[2,4,128,128]{3,2,1,0:T(8,128)S(1)} %trade.3.refs_4_), channel_id=1, source_target_pairs={{0,4},{4,0},{8,12},{12,8},{16,20},{20,16},{24,28},{28,24},{1,5},{5... | collective-permute-start | bytes 1572872 | tf_op jit(solution)/shard_map/ppermute | solution.py:343
  41.9 6.8 %collective-permute-start.10 = (f32[4,128,128]{2,1,0:T(8,128)S(1)}, f32[4,128,128]{2,1,0:T(8,128)S(1)}, u32[]{:S(2)}, u32[]{:S(2)}) collective-permute-start(f32[4,128,128]{2,1,0:T(8,128)S(1)} %hop.17.refs_18_), channel_id=1, source_target_pairs={{0,8},{1,9},{2,10},{3,11},{4,12},{5,13},{6,14},{7,15},{8,0},{9,1},... | collective-permute-start | bytes 786440 | tf_op jit(solution)/shard_map/ppermute | solution.py:412

commit v6 on v5

--- a/solution.py
+++ b/solution.py
@@ -18,7 +18,8 @@
 ACROSS_ROWS = 256
 ORDER = (
     "F", "E0", "S0", "L0123", "E1", "O1", "W20", "S1", "W21", "O2", "E2", "W00", "W01", "W10",
-    "E3", "O3", "X0", "W11", "O4", "E4", "X1", "W30", "W31", "E5", "A0", "A2", "A31",
+    "E3", "O3", "X0", "W11", "O4", "X10", "E4", "X11", "W30", "W31", "E5", "A0", "A2", "B31",
+    "C31",
 )
 PARAMS = pltpu.CompilerParams(vmem_limit_bytes=8 << 20)
 
@@ -183,54 +184,72 @@
     )(*kept(arrays), *kept(after))
 
 
-def across_kernel(jobs, *refs):
+def across_kernel(turn, chain, jobs, *refs):
     *outs, token_ref, done_ref, sems = refs[-7:]
     row, column = spot()
-    moves, ready = [], []
+    ready = []
     for total, first, pieces, count in jobs:
         run, refs = refs[:4], refs[4:]
         parts, refs = [refs[4 * n : 4 * n + 4] for n in range(pieces)], refs[4 * pieces :]
         sources, refs = refs[:count], refs[count:]
         ready.append((run, parts, first, [value.astype(BF16) for value in total(row, column, sources)]))
-    for n, (run, parts, first, (before, after)) in enumerate(ready):
-        q_ref, k_ref, v_ref, g_ref = run
-        rows, width = q_ref.shape
-        wide = width // len(parts)
-        factors = ((q_ref, before, PLAIN), (g_ref, before, LANES), (v_ref, after, LANES), (k_ref, after, PLAIN))
-        block = min(rows, ACROSS_ROWS)
+    _, slots, rows, width = done_ref.shape
+    block = min(rows, ACROSS_ROWS)
+
+    def copy(n, i, start, out):
+        here = pl.ds(start, block)
+        there = out.at[here, pl.ds(ready[n][2] * DH, width)]
+        return pltpu.make_async_copy(done_ref.at[n, i, here], there, sems.at[n, i, start // block])
+
+    def write(base):
+        for n, ((q_ref, k_ref, v_ref, g_ref), parts, _, states) in enumerate(ready):
+            wide = width // len(parts)
+            factors = ((q_ref, PLAIN), (g_ref, LANES), (v_ref, LANES), (k_ref, PLAIN))
+            for start in range(0, rows, block):
+                here = pl.ds(start, block)
+                for i in range(slots):
+                    factor, dims = factors[base + i]
+                    state = states[i // 2]
+                    for at in range(0, width, DH):
+                        part = parts[at // wide][base + i][here, pl.ds(at % wide, DH)]
+                        term = dot(factor[here, pl.ds(at, DH)], state[at // DH], dims)
+                        done_ref[n, i, here, pl.ds(at, DH)] = (part + term).astype(BF16)
+                    copy(n, i, start, outs[base + i]).start()
+
+    if turn is None:
+        write(0)
+    else:
+        upper = (row < chain // 2) == (turn == 0)
+        pl.when(upper)(lambda: write(0))
+        pl.when(jnp.logical_not(upper))(lambda: write(2))
+    token_ref[...] = jnp.zeros_like(token_ref)
+    for n in range(len(ready)):
         for start in range(0, rows, block):
-            here = pl.ds(start, block)
-            for i, (factor, state, dims) in enumerate(factors):
-                for h in range(width // DH):
-                    at = h * DH
-                    part = parts[at // wide][i][here, pl.ds(at % wide, DH)]
-                    term = dot(factor[here, pl.ds(at, DH)], state[h], dims)
-                    done_ref[n, i, here, pl.ds(at, DH)] = (part + term).astype(BF16)
-                there = outs[i].at[here, pl.ds(first * DH, width)]
-                moves.append(pltpu.make_async_copy(done_ref.at[n, i, here], there, sems.at[len(moves)]))
-                moves[-1].start()
-    token_ref[...] = jnp.zeros_like(token_ref)
-    for move in moves:
-        move.wait()
-
-
-def across(jobs, outs, shape, size, after):
+            for i in range(slots):
+                copy(n, i, start, outs[i]).wait()
+
+
+def across(jobs, turn, chain, outs, shape, size, after):
     held = () if outs is None else tuple(outs)
     arrays = [a for _, _, run, parts, sources in jobs for a in [*run, *sum(map(list, parts), []), *sources]]
+    slots = 4 if turn is None else 2
     *outs, token = pl.pallas_call(
         functools.partial(
-            across_kernel, [(total, first, len(parts), len(sources)) for total, first, _, parts, sources in jobs]
+            across_kernel,
+            turn,
+            chain,
+            [(total, first, len(parts), len(sources)) for total, first, _, parts, sources in jobs],
         ),
         in_specs=[VMEM] * len(arrays) + [HBM] * len(held) + [VMEM] * len(after),
         out_specs=[HBM] * 4 + [VMEM],
         out_shape=[jax.ShapeDtypeStruct(shape, BF16)] * 4 + [pltpu.VMEM((8, DH), F32)],
         input_output_aliases={len(arrays) + i: i for i in range(len(held))},
         scratch_shapes=[
-            pltpu.VMEM((len(jobs), 4, shape[0], size * DH), BF16),
-            pltpu.SemaphoreType.DMA((4 * len(jobs) * max(1, shape[0] // ACROSS_ROWS),)),
+            pltpu.VMEM((len(jobs), slots, shape[0], size * DH), BF16),
+            pltpu.SemaphoreType.DMA((len(jobs), slots, max(1, shape[0] // ACROSS_ROWS))),
         ],
         compiler_params=PARAMS,
-        cost_estimate=cost(1.5 * len(jobs)),
+        cost_estimate=cost(0.4 * slots * len(jobs)),
         name="across",
     )(*kept(arrays), *held, *kept(after))
     return outs, token
@@ -320,27 +339,35 @@
         last[:] = [payload]
         turns[turn] = lax.ppermute(payload, "ctx", pair)
 
-    def trade(p):
-        keys = sorted({arrival(p, z, way) for z in range(chain) for way in range(2)} - {None})
-        small = relay and p == 0
-        values = [own[p]] + [got[k] for k in keys] + ([own[3]] if relay and p == 1 else [])
+    def keys_of(p, turn):
+        places = [(z, way) for z in range(chain) for way in range(2) if turn in (None, turn_of(way, z))]
+        return sorted({arrival(p, z, way) for z, way in places} - {None})
+
+    def turn_of(way, z):
+        return 0 if early(z) == (way == 0) else 1
+
+    def trade(p, turn=None):
+        turn = 1 if relay and p == 0 else turn
+        keys = keys_of(p, turn)
+        late = relay and p == 1 and turn == 0
+        values = [own[p]] + [got[k] for k in keys] + ([own[3]] if late else [])
 
         def function(row, column, refs, out):
             sums = []
             for way in range(2):
                 value = jnp.where(column == way, refs[0][way], 0.0) + chained(p, way, row, refs[1:], keys)
-                if relay and p == 1:
-                    late = (row == (0, chain - 1)[way]) & (column == 1 - way)
-                    value = jnp.where(late, refs[-1][1 - way], value)
+                if late:
+                    spare = (row == (0, chain - 1)[way]) & (column == 1 - way)
+                    value = jnp.where(spare, refs[-1][1 - way], value)
                 sums.append(value)
-            if small:
-                out[...] = jnp.where(early(row), sums[1], sums[0])
+            if turn is None:
+                out[0], out[1] = sums
             else:
-                out[0], out[1] = sums
-
-        payload = mix(function, shape if small else (2,) + shape, values, last, "trade")
+                out[...] = jnp.where(early(row) == (turn == 0), *sums)
+
+        payload = mix(function, (2,) + shape if turn is None else shape, values, last, "trade")
         last[:] = [payload]
-        swapped[p] = lax.ppermute(payload, "ctx", pair)
+        swapped[p, turn] = lax.ppermute(payload, "ctx", pair)
 
     def chained(p, way, row, refs, keys):
         total = jnp.zeros(shape, F32)
@@ -358,9 +385,6 @@
                     groups.setdefault((p, arrival(p, z, way)), ([], []))[way].append(z)
         if not groups:
             return
-        def turn_of(way, z):
-            return 0 if early(z) == (way == 0) else 1
-
         forward = relay and parity == 0 and slot == 4
         names = []
         for (p, key), ways in groups.items():
@@ -413,44 +437,56 @@
 
     outs = [None]
 
-    def finish(*chosen):
+    def finish(turn, *chosen):
         jobs = []
         for p in chosen:
-            keys = sorted({arrival(p, z, way) for z in range(chain) for way in range(2)} - {None})
-
+            keys = keys_of(p, turn)
             values = {("got", k): got[k] for k in keys}
             if p >= 2:
-                values |= {("turns", n): turns[n] for n in range(2)}
+                values |= {("turns", n): turns[n] for n in range(2) if turn in (None, n)}
+            elif relay and p == 1:
+                values |= {("swapped", (1, n)): swapped[1, n] for n in range(2) if turn in (None, n)}
+            elif relay:
+                values |= {("swapped", (0, 1)): swapped[0, 1], ("turns", 1): turns[1], ("got", (0, 4)): got[0, 4]}
             else:
-                values["swapped", p] = swapped[p]
-            if relay and p == 3:
-                values["swapped", 1] = swapped[1]
-            if relay and p == 0:
-                values |= {("turns", 1): turns[1], ("got", (0, 4)): got[0, 4]}
+                values["swapped", (p, None)] = swapped[p, None]
+            if relay and p == 3 and turn != 0:
+                values["swapped", (1, 0)] = swapped[1, 0]
 
             def total(row, column, refs, p=p, keys=keys, names=tuple(values)):
                 refs = dict(zip(names, refs, strict=True))
+                sums = []
                 for way in range(2):
                     head, tail = (0, chain - 1) if way == 0 else (chain - 1, 0)
+
+                    def chosen_of(kind, pick):
+                        if turn is not None:
+                            return pick(refs[kind(turn)])
+                        return jnp.where(early(row) == (way == 0), pick(refs[kind(0)]), pick(refs[kind(1)]))
+
                     if p >= 2:
-                        extra = jnp.where(early(row) == (way == 0), refs["turns", 0][p - 2], refs["turns", 1][p - 2])
-                        if relay and p == 3:
-                            extra = jnp.where(row == tail, refs["swapped", 1][1 - way], extra)
+                        extra = chosen_of(lambda n: ("turns", n), lambda ref: ref[p - 2])
+                        if relay and p == 3 and turn != 0:
+                            extra = jnp.where(row == tail, refs["swapped", (1, 0)][...], extra)
                         extra = jnp.where(column == 1 - way, extra, 0.0)
-                    elif relay and p == 0:
-                        extra = jnp.where(early(row) == (way == 0), refs["got", (0, 4)][...], refs["swapped", 0][...])
+                    elif relay and p == 1:
+                        extra = chosen_of(lambda n: ("swapped", (1, n)), lambda ref: ref[...])
+                    elif relay:
+                        extra = jnp.where(early(row) == (way == 0), refs["got", (0, 4)][...], refs["swapped", (0, 1)][...])
                         extra = jnp.where(row == head, refs["turns", 1][0], extra)
                     else:
-                        extra = refs["swapped", p][way]
+                        extra = refs["swapped", (p, None)][way]
                     if p < 2:
                         extra = jnp.where((row == head) & (column == way), 0.0, extra)
-                    yield extra + chained(p, way, row, [refs["got", k] for k in keys], keys)
+                    sums.append(extra + chained(p, way, row, [refs["got", k] for k in keys], keys))
+                return sums if turn is None else [jnp.where(early(row) == (turn == 0), *sums)]
 
             jobs.append((total, p * size, run[p], local[p], list(values.values())))
-        outs[0], token = across(jobs, outs[0], arrays[0].shape, size, last)
+        outs[0], token = across(jobs, turn, chain, outs[0], arrays[0].shape, size, last)
         last[:] = [token]
 
-    steps = {"F": begin, "L": bring, "S": share, "X": trade, "E": functools.partial(hop, 0), "O": functools.partial(hop, 1), "W": inside, "A": finish}
+    steps = {"F": begin, "L": bring, "S": share, "X": trade, "E": functools.partial(hop, 0), "O": functools.partial(hop, 1), "W": inside, "A": functools.partial(finish, None)}
+    steps |= {"B": functools.partial(finish, 0), "C": functools.partial(finish, 1)}
     order = [(name[0], [int(n) for n in name[1:]]) for name in ORDER]
     if chain != 4:
         order = [("L", [2, 3]), ("L", [0, 1]), ("S", [0]), ("S", [1])]

time: 52.8 us -> 52.3 us (level)
  waiting for transfers between devices: 9.7 us -> 7.16 us
  Pallas kernels: 26.9 us -> 28.3 us
  starting transfers between devices: 15 us -> 15.7 us
    ppermute x10, waiting for transfers between devices: 7.54 us -> 5.69 us  [hop(): got[parity, slot] = lax.ppermute(payload, ('ctx', 'seq'), swap(parity))]
    pallas_call x3 -> x4, Pallas kernels: 6.45 us -> 7.89 us  [across(): pl.pallas_call(functools.partial(across_kernel, turn, chain, [(total, fir...]
    ppermute x2 -> x3, waiting for transfers between devices: 0.69 us -> 0.01 us  [trade(): swapped[p, turn] = lax.ppermute(payload, 'ctx', pair)]
    ppermute x2 -> x3, starting transfers between devices: 2.26 us -> 2.81 us  [trade(): swapped[p, turn] = lax.ppermute(payload, 'ctx', pair)]
  transfers between devices with their start and end apart: 14 -> 15, of which waited for: 8 -> 6; matrix products, arithmetic and copies ran while one was open for 0% -> 0% of each run, Pallas kernels for 41% -> 45%
where the time goes in v6:
time: 52.3 us; the launch traced here: 52.2 us
  Pallas kernels  28.3 us (54%)
  starting transfers between devices  15.7 us (30%)
  waiting for transfers between devices  7.16 us (14%)
  between operations  1.03 us (2%)
    pallas_call x8, Pallas kernels, within(): pl.pallas_call(functools.partial(within_kernel, min(rows, 256), first), i...  13 us
    ppermute x10, starting transfers between devices, hop(): got[parity, slot] = lax.ppermute(payload, ('ctx', 'seq'), swap(parity))  9.61 us
    pallas_call x4, Pallas kernels, across(): pl.pallas_call(functools.partial(across_kernel, turn, chain, [(total, fir...  7.89 us
    ppermute x10, waiting for transfers between devices, hop(): got[parity, slot] = lax.ppermute(payload, ('ctx', 'seq'), swap(parity))  5.69 us
    pallas_call x1, Pallas kernels, load(): pl.pallas_call(functools.partial(load_kernel, firsts), in_specs=[HBM] * 4...  4.17 us
    ppermute x3, starting transfers between devices, trade(): swapped[p, turn] = lax.ppermute(payload, 'ctx', pair)  2.81 us
    pallas_call x1, Pallas kernels, first_states(): pl.pallas_call(functools.partial(first_kernel, firsts, chain), in_specs=[...  2.33 us
    ppermute x1, starting transfers between devices, share(): turns[turn] = lax.ppermute(payload, 'ctx', pair)  1.75 us
  transfers between devices with their start and end apart: 15, of which 6 were waited for; matrix products, arithmetic and copies ran while one was open for 0% of the time, Pallas kernels for 45%

profile of v6, /device:TPU:0, one launch (start us, length us, event | category | flops | bytes accessed | tf_op | source)
XLA Modules:
  0.0 52.2 jit_solution(15307622713181599096)
XLA Ops:
  0.6 2.3 %first.1 = (f32[4,128,128]{2,1,0:T(8,128)S(1)}, f32[2,4,128,128]{3,2,1,0:T(8,128)S(1)}) custom-call(bf16[512,2048]{1,0:T(8,128)(2,1)} %q_hbm.3, bf16[512,2048]{1,0:T(8,128)(2,1)} %k_hbm.3, bf16[512,2048]{1,0:T(8,128)(2,1)} %v_hbm.3, bf16[512,2048]{1,0:T(8,128)(2,1)} %g_hbm.3), custom_call_target="tpu_custom_call" | custom-call | flops 2875000064 | bytes 1 | tf_op jit(solution)/shard_map/first/pallas_call | solution.py:80
  3.0 3.1 %collective-permute-start.2 = (f32[4,128,128]{2,1,0:T(8,128)S(1)}, f32[4,128,128]{2,1,0:T(8,128)S(1)}, u32[]{:S(2)}, u32[]{:S(2)}) collective-permute-start(f32[4,128,128]{2,1,0:T(8,128)S(1)} %get-tuple-element.77.refs_0_), channel_id=1, source_target_pairs={{0,8},{1,9},{2,10},{3,11},{4,12},{5,13},{6,14},{7,15},{8,0},{9,1},... | collective-permute-start | bytes 786440 | tf_op jit(solution)/shard_map/ppermute | solution.py:436
  6.1 1.5 %collective-permute-start = (f32[2,4,128,128]{3,2,1,0:T(8,128)S(1)}, f32[2,4,128,128]{3,2,1,0:T(8,128)S(1)}, u32[]{:S(2)}, u32[]{:S(2)}) collective-permute-start(f32[2,4,128,128]{3,2,1,0:T(8,128)S(1)} %get-tuple-element.84), channel_id=1, source_target_pairs={{0,4},{4,0},{8,12},{12,8},{16,20},{20,16},{24,28},{28,24},{1,5},{5... | collective-permute-start | bytes 1572872 | tf_op jit(solution)/shard_map/ppermute | solution.py:321
  7.5 4.2 %load.1 = (bf16[512,512]{1,0:T(8,128)(2,1)S(1)}, bf16[512,512]{1,0:T(8,128)(2,1)S(1)}, bf16[512,512]{1,0:T(8,128)(2,1)S(1)}, bf16[512,512]{1,0:T(8,128)(2,1)S(1)...) custom-call(bf16[512,2048]{1,0:T(8,128)(2,1)} %q_hbm.3, ...), custom_call_target="tpu_custom_call" | custom-call | flops 4024999936 | bytes 1 | tf_op jit(solution)/shard_map/load/pallas_call | solution.py:119
  12.5 1.8 %within.8 = (f32[512,256]{1,0:T(8,128)S(1)}, f32[512,256]{1,0:T(8,128)S(1)}, f32[512,256]{1,0:T(8,128)S(1)}, f32[512,256]{1,0:T(8,128)S(1)}) custom-call(bf16[512,512]{1,0:T(8,128)(2,1)S(1)} %get-tuple-element.86.refs_0_, bf16[512,512]{1,0:T(8,128)(2,1)S(1)} %get-tuple-element.87.refs_1_, bf16[512,512]{1,0:T(8,128)(2,1)S(1)} %get-tuple-element.88.refs_2_, ...), custom_call_target="tpu_custom_call" | custom-call | flops 1724999936 | bytes 1 | tf_op jit(solution)/shard_map/within/pallas_call | solution.py:160
  14.4 1.8 %collective-permute-start.6 = (f32[2,4,128,128]{3,2,1,0:T(8,128)S(1)}, f32[2,4,128,128]{3,2,1,0:T(8,128)S(1)}, u32[]{:S(2)}, u32[]{:S(2)}) collective-permute-start(f32[2,4,128,128]{3,2,1,0:T(8,128)S(1)} %share.1.refs_4_), channel_id=1, source_target_pairs={{0,4},{4,0},{8,12},{12,8},{16,20},{20,16},{24,28},{28,24},{1,5},{5... | collective-permute-start | bytes 1572872 | tf_op jit(solution)/shard_map/ppermute | solution.py:340
  16.1 1.6 %within.9 = (f32[512,256]{1,0:T(8,128)S(1)}, f32[512,256]{1,0:T(8,128)S(1)}, f32[512,256]{1,0:T(8,128)S(1)}, f32[512,256]{1,0:T(8,128)S(1)}) custom-call(bf16[512,512]{1,0:T(8,128)(2,1)S(1)} %get-tuple-element.86.refs_0_, bf16[512,512]{1,0:T(8,128)(2,1)S(1)} %get-tuple-element.87.refs_1_, bf16[512,512]{1,0:T(8,128)(2,1)S(1)} %get-tuple-element.88.refs_2_, ...), custom_call_target="tpu_custom_call" | custom-call | flops 1724999936 | bytes 1 | tf_op jit(solution)/shard_map/within/pallas_call | solution.py:160
  17.8 1.6 %collective-permute-done.1.refs_1_.refs_26_ = f32[4,128,128]{2,1,0:T(8,128)S(1)} collective-permute-done((f32[4,128,128]{2,1,0:T(8,128)S(1)}, f32[4,128,128]{2,1,0:T(8,128)S(1)}, u32[]{:S(2)}, u32[]{:S(2)}) %collective-permute-start.1) | collective-permute-done | bytes 262176 | tf_op jit(solution)/shard_map/ppermute | solution.py:436
  19.5 1.5 %collective-permute-done.refs_1_.refs_15_.refs_13_ = f32[2,4,128,128]{3,2,1,0:T(8,128)S(1)} collective-permute-done((f32[2,4,128,128]{3,2,1,0:T(8,128)S(1)}, f32[2,4,128,128]{3,2,1,0:T(8,128)S(1)}, u32[]{:S(2)}, u32[]{:S(2)}) %collective-permute-start) | collective-permute-done | bytes 524320 | tf_op jit(solution)/shard_map/ppermute | solution.py:321
  21.0 1.8 %collective-permute-start.7 = (f32[4,128,128]{2,1,0:T(8,128)S(1)}, f32[4,128,128]{2,1,0:T(8,128)S(1)}, u32[]{:S(2)}, u32[]{:S(2)}) collective-permute-start(f32[4,128,128]{2,1,0:T(8,128)S(1)} %hop.12.refs_4_), channel_id=1, source_target_pairs={{0,8},{1,9},{2,10},{3,11},{4,12},{5,13},{6,14},{7,15},{8,0},{9,1},... | collective-permute-start | bytes 786440 | tf_op jit(solution)/shard_map/ppermute | solution.py:436
  22.8 1.6 %within.10 = (f32[512,256]{1,0:T(8,128)S(1)}, f32[512,256]{1,0:T(8,128)S(1)}, f32[512,256]{1,0:T(8,128)S(1)}, f32[512,256]{1,0:T(8,128)S(1)}) custom-call(bf16[512,512]{1,0:T(8,128)(2,1)S(1)} %get-tuple-element.97.refs_0_, bf16[512,512]{1,0:T(8,128)(2,1)S(1)} %get-tuple-element.98.refs_1_, bf16[512,512]{1,0:T(8,128)(2,1)S(1)} %get-tuple-element.99.refs_2_, ...), custom_call_target="tpu_custom_call" | custom-call | flops 1724999936 | bytes 1 | tf_op jit(solution)/shard_map/within/pallas_call | solution.py:160
  24.4 1.6 %within.11 = (f32[512,256]{1,0:T(8,128)S(1)}, f32[512,256]{1,0:T(8,128)S(1)}, f32[512,256]{1,0:T(8,128)S(1)}, f32[512,256]{1,0:T(8,128)S(1)}) custom-call(bf16[512,512]{1,0:T(8,128)(2,1)S(1)} %get-tuple-element.97.refs_0_, bf16[512,512]{1,0:T(8,128)(2,1)S(1)} %get-tuple-element.98.refs_1_, bf16[512,512]{1,0:T(8,128)(2,1)S(1)} %get-tuple-element.99.refs_2_, ...), custom_call_target="tpu_custom_call" | custom-call | flops 1724999936 | bytes 1 | tf_op jit(solution)/shard_map/within/pallas_call | solution.py:160
  26.0 1.6 %within.12 = (f32[512,256]{1,0:T(8,128)S(1)}, f32[512,256]{1,0:T(8,128)S(1)}, f32[512,256]{1,0:T(8,128)S(1)}, f32[512,256]{1,0:T(8,128)S(1)}) custom-call(bf16[512,512]{1,0:T(8,128)(2,1)S(1)} %get-tuple-element.93.refs_0_.refs_14_.refs_16_, bf16[512,512]{1,0:T(8,128)(2,1)S(1)} %get-tuple-element.94.refs_1_.refs_15_.refs_17_, ...), custom_call_target="tpu_custom_call" | custom-call | flops 1724999936 | bytes 1 | tf_op jit(solution)/shard_map/within/pallas_call | solution.py:160
  28.7 1.2 %collective-permute-start.14 = (f32[4,128,128]{2,1,0:T(8,128)S(1)}, f32[4,128,128]{2,1,0:T(8,128)S(1)}, u32[]{:S(2)}, u32[]{:S(2)}) collective-permute-start(f32[4,128,128]{2,1,0:T(8,128)S(1)} %trade.3.refs_4_), channel_id=1, source_target_pairs={{0,4},{4,0},{8,12},{12,8},{16,20},{20,16},{24,28},{28,24},{1,5},{5... | collective-permute-start | bytes 786440 | tf_op jit(solution)/shard_map/ppermute | solution.py:370
  29.9 1.6 %within.13 = (f32[512,256]{1,0:T(8,128)S(1)}, f32[512,256]{1,0:T(8,128)S(1)}, f32[512,256]{1,0:T(8,128)S(1)}, f32[512,256]{1,0:T(8,128)S(1)}) custom-call(bf16[512,512]{1,0:T(8,128)(2,1)S(1)} %get-tuple-element.93.refs_0_.refs_14_.refs_16_, bf16[512,512]{1,0:T(8,128)(2,1)S(1)} %get-tuple-element.94.refs_1_.refs_15_.refs_17_, ...), custom_call_target="tpu_custom_call" | custom-call | flops 1724999936 | bytes 1 | tf_op jit(solution)/shard_map/within/pallas_call | solution.py:160
  31.5 2.6 %collective-permute-done.5.refs_2_.refs_1_.refs_12_.refs_28_ = f32[4,128,128]{2,1,0:T(8,128)S(1)} collective-permute-done((f32[4,128,128]{2,1,0:T(8,128)S(1)}, f32[4,128,128]{2,1,0:T(8,128)S(1)}, u32[]{:S(2)}, u32[]{:S(2)}) %collective-permute-start.5) | collective-permute-done | bytes 262176 | tf_op jit(solution)/shard_map/ppermute | solution.py:436
  35.1 3.5 %collective-permute-start.13 = (f32[4,128,128]{2,1,0:T(8,128)S(1)}, f32[4,128,128]{2,1,0:T(8,128)S(1)}, u32[]{:S(2)}, u32[]{:S(2)}) collective-permute-start(f32[4,128,128]{2,1,0:T(8,128)S(1)} %hop.16.refs_3_), channel_id=1, source_target_pairs={{0,8},{1,9},{2,10},{3,11},{4,12},{5,13},{6,14},{7,15},{8,0},{9,1},... | collective-permute-start | bytes 786440 | tf_op jit(solution)/shard_map/ppermute | solution.py:436
  38.6 1.0 %collective-permute-start.12 = (f32[4,128,128]{2,1,0:T(8,128)S(1)}, f32[4,128,128]{2,1,0:T(8,128)S(1)}, u32[]{:S(2)}, u32[]{:S(2)}) collective-permute-start(f32[4,128,128]{2,1,0:T(8,128)S(1)} %trade.5.refs_4_), channel_id=1, source_target_pairs={{0,4},{4,0},{8,12},{12,8},{16,20},{20,16},{24,28},{28,24},{1,5},{5... | collective-permute-start | bytes 786440 | tf_op jit(solution)/shard_map/ppermute | solution.py:370
  39.6 1.6 %within.14 = (f32[512,256]{1,0:T(8,128)S(1)}, f32[512,256]{1,0:T(8,128)S(1)}, f32[512,256]{1,0:T(8,128)S(1)}, f32[512,256]{1,0:T(8,128)S(1)}) custom-call(bf16[512,512]{1,0:T(8,128)(2,1)S(1)} %get-tuple-element.78.refs_0_, bf16[512,512]{1,0:T(8,128)(2,1)S(1)} %get-tuple-element.79.refs_1_, bf16[512,512]{1,0:T(8,128)(2,1)S(1)} %get-tuple-element.80.refs_2_, ...), custom_call_target="tpu_custom_call" | custom-call | flops 1724999936 | bytes 1 | tf_op jit(solution)/shard_map/within/pallas_call | solution.py:160
  41.2 1.6 %within.15 = (f32[512,256]{1,0:T(8,128)S(1)}, f32[512,256]{1,0:T(8,128)S(1)}, f32[512,256]{1,0:T(8,128)S(1)}, f32[512,256]{1,0:T(8,128)S(1)}) custom-call(bf16[512,512]{1,0:T(8,128)(2,1)S(1)} %get-tuple-element.78.refs_0_, bf16[512,512]{1,0:T(8,128)(2,1)S(1)} %get-tuple-element.79.refs_1_, bf16[512,512]{1,0:T(8,128)(2,1)S(1)} %get-tuple-element.80.refs_2_, ...), custom_call_target="tpu_custom_call" | custom-call | flops 1724999936 | bytes 1 | tf_op jit(solution)/shard_map/within/pallas_call | solution.py:160
  44.0 1.7 %across.4 = (bf16[512,2048]{1,0:T(8,128)(2,1)}, bf16[512,2048]{1,0:T(8,128)(2,1)}, bf16[512,2048]{1,0:T(8,128)(2,1)}, bf16[512,2048]{1,0:T(8,128)(2,1)}, f32[8,128]{1,0:T(8,128)S(1)}) custom-call(bf16[512,512]{1,0:T(8,128)(2,1)S(1)} %get-tuple-element.97.refs_0_, bf16[512,512]{1,0:T(8,128)(2,1)S(1)} %get-tuple-element.98.refs_1_, ...), custom_call_target="tpu_custom_call" | custom-call | flops 1840000000 | bytes 1 | tf_op jit(solution)/shard_map/across/pallas_call | solution.py:236
  45.7 1.7 %across.5 = (bf16[512,2048]{1,0:T(8,128)(2,1)}, bf16[512,2048]{1,0:T(8,128)(2,1)}, bf16[512,2048]{1,0:T(8,128)(2,1)}, bf16[512,2048]{1,0:T(8,128)(2,1)}, f32[8,128]{1,0:T(8,128)S(1)}) custom-call(bf16[512,512]{1,0:T(8,128)(2,1)S(1)} %get-tuple-element.86.refs_0_, ...), custom_call_target="tpu_custom_call", output_to_operand_aliasing={{0}: (17, {}), {1}: (18, {}), {2}: (19, {}), {3}: (20, {})} | custom-call | flops 1840000000 | bytes 1 | tf_op jit(solution)/shard_map/across/pallas_call | solution.py:236
  47.4 1.9 %across.6 = (bf16[512,2048]{1,0:T(8,128)(2,1)}, bf16[512,2048]{1,0:T(8,128)(2,1)}, bf16[512,2048]{1,0:T(8,128)(2,1)}, bf16[512,2048]{1,0:T(8,128)(2,1)}, f32[8,128]{1,0:T(8,128)S(1)}) custom-call(bf16[512,512]{1,0:T(8,128)(2,1)S(1)} %get-tuple-element.78.refs_0_, ...), custom_call_target="tpu_custom_call", output_to_operand_aliasing={{0}: (28, {}), {1}: (29, {}), {2}: (30, {}), {3}: (31, {})} | custom-call | flops 1840000000 | bytes 1 | tf_op jit(solution)/shard_map/across/pallas_call | solution.py:236
  49.3 2.6 %across.7 = (bf16[512,2048]{1,0:T(8,128)(2,1)}, bf16[512,2048]{1,0:T(8,128)(2,1)}, bf16[512,2048]{1,0:T(8,128)(2,1)}, bf16[512,2048]{1,0:T(8,128)(2,1)}, f32[8,128]{1,0:T(8,128)}) custom-call(bf16[512,512]{1,0:T(8,128)(2,1)S(1)} %get-tuple-element.78.refs_0_, ...), custom_call_target="tpu_custom_call", output_to_operand_aliasing={{0}: (31, {}), {1}: (32, {}), {2}: (33, {}), {3}: (34, {})} | custom-call | flops 1840000000 | bytes 1 | tf_op jit(solution)/shard_map/across/pallas_call | solution.py:236
  (33 shorter events, 4.4 us)
Async XLA Ops:
  3.0 9.4 %collective-permute-start.2 = (f32[4,128,128]{2,1,0:T(8,128)S(1)}, f32[4,128,128]{2,1,0:T(8,128)S(1)}, u32[]{:S(2)}, u32[]{:S(2)}) collective-permute-start(f32[4,128,128]{2,1,0:T(8,128)S(1)} %get-tuple-element.77.refs_0_), channel_id=1, source_target_pairs={{0,8},{1,9},{2,10},{3,11},{4,12},{5,13},{6,14},{7,15},{8,0},{9,1},... | collective-permute-start | bytes 786440 | tf_op jit(solution)/shard_map/ppermute | solution.py:436
  6.1 14.9 %collective-permute-start = (f32[2,4,128,128]{3,2,1,0:T(8,128)S(1)}, f32[2,4,128,128]{3,2,1,0:T(8,128)S(1)}, u32[]{:S(2)}, u32[]{:S(2)}) collective-permute-start(f32[2,4,128,128]{3,2,1,0:T(8,128)S(1)} %get-tuple-element.84), channel_id=1, source_target_pairs={{0,4},{4,0},{8,12},{12,8},{16,20},{20,16},{24,28},{28,24},{1,5},{5... | collective-permute-start | bytes 1572872 | tf_op jit(solution)/shard_map/ppermute | solution.py:321
  11.8 7.6 %collective-permute-start.1 = (f32[4,128,128]{2,1,0:T(8,128)S(1)}, f32[4,128,128]{2,1,0:T(8,128)S(1)}, u32[]{:S(2)}, u32[]{:S(2)}) collective-permute-start(f32[4,128,128]{2,1,0:T(8,128)S(1)} %hop.9.refs_2_), channel_id=1, source_target_pairs={{0,8},{1,9},{2,10},{3,11},{4,12},{5,13},{6,14},{7,15},{8,0},{9,1},... | collective-permute-start | bytes 786440 | tf_op jit(solution)/shard_map/ppermute | solution.py:436
  12.4 8.5 %collective-permute-start.4 = (f32[4,128,128]{2,1,0:T(8,128)S(1)}, f32[4,128,128]{2,1,0:T(8,128)S(1)}, u32[]{:S(2)}, u32[]{:S(2)}) collective-permute-start(f32[4,128,128]{2,1,0:T(8,128)S(1)} %hop.10.refs_4_), channel_id=1, source_target_pairs={{0,1},{1,0},{2,3},{3,2},{4,5},{5,4},{6,7},{7,6},{8,16},{9,17},{10,... | collective-permute-start | bytes 786440 | tf_op jit(solution)/shard_map/ppermute | solution.py:436
  14.4 20.6 %collective-permute-start.6 = (f32[2,4,128,128]{3,2,1,0:T(8,128)S(1)}, f32[2,4,128,128]{3,2,1,0:T(8,128)S(1)}, u32[]{:S(2)}, u32[]{:S(2)}) collective-permute-start(f32[2,4,128,128]{3,2,1,0:T(8,128)S(1)} %share.1.refs_4_), channel_id=1, source_target_pairs={{0,4},{4,0},{8,12},{12,8},{16,20},{20,16},{24,28},{28,24},{1,5},{5... | collective-permute-start | bytes 1572872 | tf_op jit(solution)/shard_map/ppermute | solution.py:340
  19.4 8.2 %collective-permute-start.3 = (f32[4,128,128]{2,1,0:T(8,128)S(1)}, f32[4,128,128]{2,1,0:T(8,128)S(1)}, u32[]{:S(2)}, u32[]{:S(2)}) collective-permute-start(f32[4,128,128]{2,1,0:T(8,128)S(1)} %hop.11.refs_4_), channel_id=1, source_target_pairs={{0,1},{1,0},{2,3},{3,2},{4,5},{5,4},{6,7},{7,6},{8,16},{9,17},{10,... | collective-permute-start | bytes 786440 | tf_op jit(solution)/shard_map/ppermute | solution.py:436
  21.0 7.4 %collective-permute-start.7 = (f32[4,128,128]{2,1,0:T(8,128)S(1)}, f32[4,128,128]{2,1,0:T(8,128)S(1)}, u32[]{:S(2)}, u32[]{:S(2)}) collective-permute-start(f32[4,128,128]{2,1,0:T(8,128)S(1)} %hop.12.refs_4_), channel_id=1, source_target_pairs={{0,8},{1,9},{2,10},{3,11},{4,12},{5,13},{6,14},{7,15},{8,0},{9,1},... | collective-permute-start | bytes 786440 | tf_op jit(solution)/shard_map/ppermute | solution.py:436
  27.7 6.4 %collective-permute-start.5 = (f32[4,128,128]{2,1,0:T(8,128)S(1)}, f32[4,128,128]{2,1,0:T(8,128)S(1)}, u32[]{:S(2)}, u32[]{:S(2)}) collective-permute-start(f32[4,128,128]{2,1,0:T(8,128)S(1)} %hop.13.refs_3_), channel_id=1, source_target_pairs={{0,8},{1,9},{2,10},{3,11},{4,12},{5,13},{6,14},{7,15},{8,0},{9,1},... | collective-permute-start | bytes 786440 | tf_op jit(solution)/shard_map/ppermute | solution.py:436
  28.5 6.5 %collective-permute-start.8 = (f32[4,128,128]{2,1,0:T(8,128)S(1)}, f32[4,128,128]{2,1,0:T(8,128)S(1)}, u32[]{:S(2)}, u32[]{:S(2)}) collective-permute-start(f32[4,128,128]{2,1,0:T(8,128)S(1)} %hop.14.refs_3_), channel_id=1, source_target_pairs={{0,1},{1,0},{2,3},{3,2},{4,5},{5,4},{6,7},{7,6},{8,16},{9,17},{10,... | collective-permute-start | bytes 786440 | tf_op jit(solution)/shard_map/ppermute | solution.py:436
  28.7 14.3 %collective-permute-start.14 = (f32[4,128,128]{2,1,0:T(8,128)S(1)}, f32[4,128,128]{2,1,0:T(8,128)S(1)}, u32[]{:S(2)}, u32[]{:S(2)}) collective-permute-start(f32[4,128,128]{2,1,0:T(8,128)S(1)} %trade.3.refs_4_), channel_id=1, source_target_pairs={{0,4},{4,0},{8,12},{12,8},{16,20},{20,16},{24,28},{28,24},{1,5},{5... | collective-permute-start | bytes 786440 | tf_op jit(solution)/shard_map/ppermute | solution.py:370
  34.2 8.7 %collective-permute-start.9 = (f32[4,128,128]{2,1,0:T(8,128)S(1)}, f32[4,128,128]{2,1,0:T(8,128)S(1)}, u32[]{:S(2)}, u32[]{:S(2)}) collective-permute-start(f32[4,128,128]{2,1,0:T(8,128)S(1)} %hop.15.refs_3_), channel_id=1, source_target_pairs={{0,1},{1,0},{2,3},{3,2},{4,5},{5,4},{6,7},{7,6},{8,16},{9,17},{10,... | collective-permute-start | bytes 786440 | tf_op jit(solution)/shard_map/ppermute | solution.py:436
  34.4 13.0 %collective-permute-start.11 = (f32[4,128,128]{2,1,0:T(8,128)S(1)}, f32[4,128,128]{2,1,0:T(8,128)S(1)}, u32[]{:S(2)}, u32[]{:S(2)}) collective-permute-start(f32[4,128,128]{2,1,0:T(8,128)S(1)} %trade.4.refs_3_), channel_id=1, source_target_pairs={{0,4},{4,0},{8,12},{12,8},{16,20},{20,16},{24,28},{28,24},{1,5},{5... | collective-permute-start | bytes 786440 | tf_op jit(solution)/shard_map/ppermute | solution.py:370
  35.1 9.0 %collective-permute-start.13 = (f32[4,128,128]{2,1,0:T(8,128)S(1)}, f32[4,128,128]{2,1,0:T(8,128)S(1)}, u32[]{:S(2)}, u32[]{:S(2)}) collective-permute-start(f32[4,128,128]{2,1,0:T(8,128)S(1)} %hop.16.refs_3_), channel_id=1, source_target_pairs={{0,8},{1,9},{2,10},{3,11},{4,12},{5,13},{6,14},{7,15},{8,0},{9,1},... | collective-permute-start | bytes 786440 | tf_op jit(solution)/shard_map/ppermute | solution.py:436
  38.6 10.7 %collective-permute-start.12 = (f32[4,128,128]{2,1,0:T(8,128)S(1)}, f32[4,128,128]{2,1,0:T(8,128)S(1)}, u32[]{:S(2)}, u32[]{:S(2)}) collective-permute-start(f32[4,128,128]{2,1,0:T(8,128)S(1)} %trade.5.refs_4_), channel_id=1, source_target_pairs={{0,4},{4,0},{8,12},{12,8},{16,20},{20,16},{24,28},{28,24},{1,5},{5... | collective-permute-start | bytes 786440 | tf_op jit(solution)/shard_map/ppermute | solution.py:370
  42.9 6.4 %collective-permute-start.10 = (f32[4,128,128]{2,1,0:T(8,128)S(1)}, f32[4,128,128]{2,1,0:T(8,128)S(1)}, u32[]{:S(2)}, u32[]{:S(2)}) collective-permute-start(f32[4,128,128]{2,1,0:T(8,128)S(1)} %hop.17.refs_18_), channel_id=1, source_target_pairs={{0,8},{1,9},{2,10},{3,11},{4,12},{5,13},{6,14},{7,15},{8,0},{9,1},... | collective-permute-start | bytes 786440 | tf_op jit(solution)/shard_map/ppermute | solution.py:436

commit v7 on v6

--- a/solution.py
+++ b/solution.py
@@ -18,7 +18,7 @@
 ACROSS_ROWS = 256
 ORDER = (
     "F", "E0", "S0", "L0123", "E1", "O1", "W20", "S1", "W21", "O2", "E2", "W00", "W01", "W10",
-    "E3", "O3", "X0", "W11", "O4", "X10", "E4", "X11", "W30", "W31", "E5", "A0", "A2", "B31",
+    "E3", "O3", "X0", "W11", "O4", "X10", "E4", "X11", "W30", "W31", "E5", "A02", "B31",
     "C31",
 )
 PARAMS = pltpu.CompilerParams(vmem_limit_bytes=8 << 20)

time: 52.3 us -> 52.2 us (level)
  Pallas kernels: 28.3 us -> 27.4 us
  waiting for transfers between devices: 7.16 us -> 8.01 us
    pallas_call x4 -> x3, Pallas kernels: 7.89 us -> 7.03 us  [across(): pl.pallas_call(functools.partial(across_kernel, turn, chain, [(total, fir...]
    ppermute x10, waiting for transfers between devices: 5.69 us -> 6.3 us  [hop(): got[parity, slot] = lax.ppermute(payload, ('ctx', 'seq'), swap(parity))]
  transfers between devices with their start and end apart: 15 -> 15, of which waited for: 6 -> 8; matrix products, arithmetic and copies ran while one was open for 0% -> 0% of each run, Pallas kernels for 45% -> 43%
where the time goes in v7:
time: 52.2 us; the launch traced here: 52.1 us
  Pallas kernels  27.4 us (52%)
  starting transfers between devices  15.7 us (30%)
  waiting for transfers between devices  8.01 us (15%)
  between operations  1.02 us (2%)
    pallas_call x8, Pallas kernels, within(): pl.pallas_call(functools.partial(within_kernel, min(rows, 256), first), i...  13 us
    ppermute x10, starting transfers between devices, hop(): got[parity, slot] = lax.ppermute(payload, ('ctx', 'seq'), swap(parity))  9.59 us
    pallas_call x3, Pallas kernels, across(): pl.pallas_call(functools.partial(across_kernel, turn, chain, [(total, fir...  7.03 us
    ppermute x10, waiting for transfers between devices, hop(): got[parity, slot] = lax.ppermute(payload, ('ctx', 'seq'), swap(parity))  6.3 us
    pallas_call x1, Pallas kernels, load(): pl.pallas_call(functools.partial(load_kernel, firsts), in_specs=[HBM] * 4...  4.17 us
    ppermute x3, starting transfers between devices, trade(): swapped[p, turn] = lax.ppermute(payload, 'ctx', pair)  2.83 us
    pallas_call x1, Pallas kernels, first_states(): pl.pallas_call(functools.partial(first_kernel, firsts, chain), in_specs=[...  2.33 us
    ppermute x1, starting transfers between devices, share(): turns[turn] = lax.ppermute(payload, 'ctx', pair)  1.75 us
  transfers between devices with their start and end apart: 15, of which 8 were waited for; matrix products, arithmetic and copies ran while one was open for 0% of the time, Pallas kernels for 43%

profile of v7, /device:TPU:0, one launch (start us, length us, event | category | flops | bytes accessed | tf_op | source)
XLA Modules:
  0.0 52.1 jit_solution(1505075474076493532)
XLA Ops:
  0.6 2.3 %first.1 = (f32[4,128,128]{2,1,0:T(8,128)S(1)}, f32[2,4,128,128]{3,2,1,0:T(8,128)S(1)}) custom-call(bf16[512,2048]{1,0:T(8,128)(2,1)} %q_hbm.3, bf16[512,2048]{1,0:T(8,128)(2,1)} %k_hbm.3, bf16[512,2048]{1,0:T(8,128)(2,1)} %v_hbm.3, bf16[512,2048]{1,0:T(8,128)(2,1)} %g_hbm.3), custom_call_target="tpu_custom_call" | custom-call | flops 2875000064 | bytes 1 | tf_op jit(solution)/shard_map/first/pallas_call | solution.py:80
  3.0 3.1 %collective-permute-start.2 = (f32[4,128,128]{2,1,0:T(8,128)S(1)}, f32[4,128,128]{2,1,0:T(8,128)S(1)}, u32[]{:S(2)}, u32[]{:S(2)}) collective-permute-start(f32[4,128,128]{2,1,0:T(8,128)S(1)} %get-tuple-element.72.refs_0_), channel_id=1, source_target_pairs={{0,8},{1,9},{2,10},{3,11},{4,12},{5,13},{6,14},{7,15},{8,0},{9,1},... | collective-permute-start | bytes 786440 | tf_op jit(solution)/shard_map/ppermute | solution.py:436
  6.1 1.5 %collective-permute-start = (f32[2,4,128,128]{3,2,1,0:T(8,128)S(1)}, f32[2,4,128,128]{3,2,1,0:T(8,128)S(1)}, u32[]{:S(2)}, u32[]{:S(2)}) collective-permute-start(f32[2,4,128,128]{3,2,1,0:T(8,128)S(1)} %get-tuple-element.79), channel_id=1, source_target_pairs={{0,4},{4,0},{8,12},{12,8},{16,20},{20,16},{24,28},{28,24},{1,5},{5... | collective-permute-start | bytes 1572872 | tf_op jit(solution)/shard_map/ppermute | solution.py:321
  7.5 4.2 %load.1 = (bf16[512,512]{1,0:T(8,128)(2,1)S(1)}, bf16[512,512]{1,0:T(8,128)(2,1)S(1)}, bf16[512,512]{1,0:T(8,128)(2,1)S(1)}, bf16[512,512]{1,0:T(8,128)(2,1)S(1)...) custom-call(bf16[512,2048]{1,0:T(8,128)(2,1)} %q_hbm.3, ...), custom_call_target="tpu_custom_call" | custom-call | flops 4024999936 | bytes 1 | tf_op jit(solution)/shard_map/load/pallas_call | solution.py:119
  12.5 1.8 %within.8 = (f32[512,256]{1,0:T(8,128)S(1)}, f32[512,256]{1,0:T(8,128)S(1)}, f32[512,256]{1,0:T(8,128)S(1)}, f32[512,256]{1,0:T(8,128)S(1)}) custom-call(bf16[512,512]{1,0:T(8,128)(2,1)S(1)} %get-tuple-element.81.refs_0_.refs_18_, bf16[512,512]{1,0:T(8,128)(2,1)S(1)} %get-tuple-element.82.refs_1_.refs_19_, ...), custom_call_target="tpu_custom_call" | custom-call | flops 1724999936 | bytes 1 | tf_op jit(solution)/shard_map/within/pallas_call | solution.py:160
  14.4 1.7 %collective-permute-start.6 = (f32[2,4,128,128]{3,2,1,0:T(8,128)S(1)}, f32[2,4,128,128]{3,2,1,0:T(8,128)S(1)}, u32[]{:S(2)}, u32[]{:S(2)}) collective-permute-start(f32[2,4,128,128]{3,2,1,0:T(8,128)S(1)} %share.1.refs_4_), channel_id=1, source_target_pairs={{0,4},{4,0},{8,12},{12,8},{16,20},{20,16},{24,28},{28,24},{1,5},{5... | collective-permute-start | bytes 1572872 | tf_op jit(solution)/shard_map/ppermute | solution.py:340
  16.2 1.6 %within.9 = (f32[512,256]{1,0:T(8,128)S(1)}, f32[512,256]{1,0:T(8,128)S(1)}, f32[512,256]{1,0:T(8,128)S(1)}, f32[512,256]{1,0:T(8,128)S(1)}) custom-call(bf16[512,512]{1,0:T(8,128)(2,1)S(1)} %get-tuple-element.81.refs_0_.refs_18_, bf16[512,512]{1,0:T(8,128)(2,1)S(1)} %get-tuple-element.82.refs_1_.refs_19_, ...), custom_call_target="tpu_custom_call" | custom-call | flops 1724999936 | bytes 1 | tf_op jit(solution)/shard_map/within/pallas_call | solution.py:160
  17.8 1.6 %collective-permute-done.1.refs_1_.refs_26_ = f32[4,128,128]{2,1,0:T(8,128)S(1)} collective-permute-done((f32[4,128,128]{2,1,0:T(8,128)S(1)}, f32[4,128,128]{2,1,0:T(8,128)S(1)}, u32[]{:S(2)}, u32[]{:S(2)}) %collective-permute-start.1) | collective-permute-done | bytes 262176 | tf_op jit(solution)/shard_map/ppermute | solution.py:436
  19.5 1.5 %collective-permute-done.refs_1_.refs_33_.refs_13_ = f32[2,4,128,128]{3,2,1,0:T(8,128)S(1)} collective-permute-done((f32[2,4,128,128]{3,2,1,0:T(8,128)S(1)}, f32[2,4,128,128]{3,2,1,0:T(8,128)S(1)}, u32[]{:S(2)}, u32[]{:S(2)}) %collective-permute-start) | collective-permute-done | bytes 524320 | tf_op jit(solution)/shard_map/ppermute | solution.py:321
  21.0 1.8 %collective-permute-start.7 = (f32[4,128,128]{2,1,0:T(8,128)S(1)}, f32[4,128,128]{2,1,0:T(8,128)S(1)}, u32[]{:S(2)}, u32[]{:S(2)}) collective-permute-start(f32[4,128,128]{2,1,0:T(8,128)S(1)} %hop.12.refs_4_), channel_id=1, source_target_pairs={{0,8},{1,9},{2,10},{3,11},{4,12},{5,13},{6,14},{7,15},{8,0},{9,1},... | collective-permute-start | bytes 786440 | tf_op jit(solution)/shard_map/ppermute | solution.py:436
  22.8 1.6 %within.10 = (f32[512,256]{1,0:T(8,128)S(1)}, f32[512,256]{1,0:T(8,128)S(1)}, f32[512,256]{1,0:T(8,128)S(1)}, f32[512,256]{1,0:T(8,128)S(1)}) custom-call(bf16[512,512]{1,0:T(8,128)(2,1)S(1)} %get-tuple-element.92.refs_0_, bf16[512,512]{1,0:T(8,128)(2,1)S(1)} %get-tuple-element.93.refs_1_, bf16[512,512]{1,0:T(8,128)(2,1)S(1)} %get-tuple-element.94.refs_2_, ...), custom_call_target="tpu_custom_call" | custom-call | flops 1724999936 | bytes 1 | tf_op jit(solution)/shard_map/within/pallas_call | solution.py:160
  24.4 1.6 %within.11 = (f32[512,256]{1,0:T(8,128)S(1)}, f32[512,256]{1,0:T(8,128)S(1)}, f32[512,256]{1,0:T(8,128)S(1)}, f32[512,256]{1,0:T(8,128)S(1)}) custom-call(bf16[512,512]{1,0:T(8,128)(2,1)S(1)} %get-tuple-element.92.refs_0_, bf16[512,512]{1,0:T(8,128)(2,1)S(1)} %get-tuple-element.93.refs_1_, bf16[512,512]{1,0:T(8,128)(2,1)S(1)} %get-tuple-element.94.refs_2_, ...), custom_call_target="tpu_custom_call" | custom-call | flops 1724999936 | bytes 1 | tf_op jit(solution)/shard_map/within/pallas_call | solution.py:160
  26.0 1.6 %within.12 = (f32[512,256]{1,0:T(8,128)S(1)}, f32[512,256]{1,0:T(8,128)S(1)}, f32[512,256]{1,0:T(8,128)S(1)}, f32[512,256]{1,0:T(8,128)S(1)}) custom-call(bf16[512,512]{1,0:T(8,128)(2,1)S(1)} %get-tuple-element.88.refs_0_.refs_14_.refs_16_, bf16[512,512]{1,0:T(8,128)(2,1)S(1)} %get-tuple-element.89.refs_1_.refs_15_.refs_17_, ...), custom_call_target="tpu_custom_call" | custom-call | flops 1724999936 | bytes 1 | tf_op jit(solution)/shard_map/within/pallas_call | solution.py:160
  28.7 1.2 %collective-permute-start.13 = (f32[4,128,128]{2,1,0:T(8,128)S(1)}, f32[4,128,128]{2,1,0:T(8,128)S(1)}, u32[]{:S(2)}, u32[]{:S(2)}) collective-permute-start(f32[4,128,128]{2,1,0:T(8,128)S(1)} %trade.3.refs_4_), channel_id=1, source_target_pairs={{0,4},{4,0},{8,12},{12,8},{16,20},{20,16},{24,28},{28,24},{1,5},{5... | collective-permute-start | bytes 786440 | tf_op jit(solution)/shard_map/ppermute | solution.py:370
  29.9 1.6 %within.13 = (f32[512,256]{1,0:T(8,128)S(1)}, f32[512,256]{1,0:T(8,128)S(1)}, f32[512,256]{1,0:T(8,128)S(1)}, f32[512,256]{1,0:T(8,128)S(1)}) custom-call(bf16[512,512]{1,0:T(8,128)(2,1)S(1)} %get-tuple-element.88.refs_0_.refs_14_.refs_16_, bf16[512,512]{1,0:T(8,128)(2,1)S(1)} %get-tuple-element.89.refs_1_.refs_15_.refs_17_, ...), custom_call_target="tpu_custom_call" | custom-call | flops 1724999936 | bytes 1 | tf_op jit(solution)/shard_map/within/pallas_call | solution.py:160
  31.5 2.7 %collective-permute-done.5.refs_2_.refs_1_.refs_12_.refs_28_ = f32[4,128,128]{2,1,0:T(8,128)S(1)} collective-permute-done((f32[4,128,128]{2,1,0:T(8,128)S(1)}, f32[4,128,128]{2,1,0:T(8,128)S(1)}, u32[]{:S(2)}, u32[]{:S(2)}) %collective-permute-start.5) | collective-permute-done | bytes 262176 | tf_op jit(solution)/shard_map/ppermute | solution.py:436
  35.1 3.4 %collective-permute-start.14 = (f32[4,128,128]{2,1,0:T(8,128)S(1)}, f32[4,128,128]{2,1,0:T(8,128)S(1)}, u32[]{:S(2)}, u32[]{:S(2)}) collective-permute-start(f32[4,128,128]{2,1,0:T(8,128)S(1)} %hop.16.refs_3_), channel_id=1, source_target_pairs={{0,8},{1,9},{2,10},{3,11},{4,12},{5,13},{6,14},{7,15},{8,0},{9,1},... | collective-permute-start | bytes 786440 | tf_op jit(solution)/shard_map/ppermute | solution.py:436
  38.6 1.0 %collective-permute-start.12 = (f32[4,128,128]{2,1,0:T(8,128)S(1)}, f32[4,128,128]{2,1,0:T(8,128)S(1)}, u32[]{:S(2)}, u32[]{:S(2)}) collective-permute-start(f32[4,128,128]{2,1,0:T(8,128)S(1)} %trade.5.refs_4_), channel_id=1, source_target_pairs={{0,4},{4,0},{8,12},{12,8},{16,20},{20,16},{24,28},{28,24},{1,5},{5... | collective-permute-start | bytes 786440 | tf_op jit(solution)/shard_map/ppermute | solution.py:370
  39.6 1.6 %within.14 = (f32[512,256]{1,0:T(8,128)S(1)}, f32[512,256]{1,0:T(8,128)S(1)}, f32[512,256]{1,0:T(8,128)S(1)}, f32[512,256]{1,0:T(8,128)S(1)}) custom-call(bf16[512,512]{1,0:T(8,128)(2,1)S(1)} %get-tuple-element.73.refs_0_, bf16[512,512]{1,0:T(8,128)(2,1)S(1)} %get-tuple-element.74.refs_1_, bf16[512,512]{1,0:T(8,128)(2,1)S(1)} %get-tuple-element.75.refs_2_, ...), custom_call_target="tpu_custom_call" | custom-call | flops 1724999936 | bytes 1 | tf_op jit(solution)/shard_map/within/pallas_call | solution.py:160
  41.2 1.6 %within.15 = (f32[512,256]{1,0:T(8,128)S(1)}, f32[512,256]{1,0:T(8,128)S(1)}, f32[512,256]{1,0:T(8,128)S(1)}, f32[512,256]{1,0:T(8,128)S(1)}) custom-call(bf16[512,512]{1,0:T(8,128)(2,1)S(1)} %get-tuple-element.73.refs_0_, bf16[512,512]{1,0:T(8,128)(2,1)S(1)} %get-tuple-element.74.refs_1_, bf16[512,512]{1,0:T(8,128)(2,1)S(1)} %get-tuple-element.75.refs_2_, ...), custom_call_target="tpu_custom_call" | custom-call | flops 1724999936 | bytes 1 | tf_op jit(solution)/shard_map/within/pallas_call | solution.py:160
  43.0 1.0 %collective-permute-done.14.refs_17_.refs_31_ = f32[4,128,128]{2,1,0:T(8,128)S(1)} collective-permute-done((f32[4,128,128]{2,1,0:T(8,128)S(1)}, f32[4,128,128]{2,1,0:T(8,128)S(1)}, u32[]{:S(2)}, u32[]{:S(2)}) %collective-permute-start.14) | collective-permute-done | bytes 262176 | tf_op jit(solution)/shard_map/ppermute | solution.py:436
  44.0 2.6 %across.3 = (bf16[512,2048]{1,0:T(8,128)(2,1)}, bf16[512,2048]{1,0:T(8,128)(2,1)}, bf16[512,2048]{1,0:T(8,128)(2,1)}, bf16[512,2048]{1,0:T(8,128)(2,1)}, f32[8,128]{1,0:T(8,128)S(1)}) custom-call(bf16[512,512]{1,0:T(8,128)(2,1)S(1)} %get-tuple-element.92.refs_0_, bf16[512,512]{1,0:T(8,128)(2,1)S(1)} %get-tuple-element.93.refs_1_, ...), custom_call_target="tpu_custom_call" | custom-call | flops 3680000000 | bytes 1 | tf_op jit(solution)/shard_map/across/pallas_call | solution.py:236
  46.6 1.9 %across.4 = (bf16[512,2048]{1,0:T(8,128)(2,1)}, bf16[512,2048]{1,0:T(8,128)(2,1)}, bf16[512,2048]{1,0:T(8,128)(2,1)}, bf16[512,2048]{1,0:T(8,128)(2,1)}, f32[8,128]{1,0:T(8,128)S(1)}) custom-call(bf16[512,512]{1,0:T(8,128)(2,1)S(1)} %get-tuple-element.73.refs_0_, ...), custom_call_target="tpu_custom_call", output_to_operand_aliasing={{0}: (28, {}), {1}: (29, {}), {2}: (30, {}), {3}: (31, {})} | custom-call | flops 1840000000 | bytes 1 | tf_op jit(solution)/shard_map/across/pallas_call | solution.py:236
  49.3 2.6 %across.5 = (bf16[512,2048]{1,0:T(8,128)(2,1)}, bf16[512,2048]{1,0:T(8,128)(2,1)}, bf16[512,2048]{1,0:T(8,128)(2,1)}, bf16[512,2048]{1,0:T(8,128)(2,1)}, f32[8,128]{1,0:T(8,128)}) custom-call(bf16[512,512]{1,0:T(8,128)(2,1)S(1)} %get-tuple-element.73.refs_0_, ...), custom_call_target="tpu_custom_call", output_to_operand_aliasing={{0}: (31, {}), {1}: (32, {}), {2}: (33, {}), {3}: (34, {})} | custom-call | flops 1840000000 | bytes 1 | tf_op jit(solution)/shard_map/across/pallas_call | solution.py:236
  (32 shorter events, 4.1 us)
Async XLA Ops:
  3.0 9.4 %collective-permute-start.2 = (f32[4,128,128]{2,1,0:T(8,128)S(1)}, f32[4,128,128]{2,1,0:T(8,128)S(1)}, u32[]{:S(2)}, u32[]{:S(2)}) collective-permute-start(f32[4,128,128]{2,1,0:T(8,128)S(1)} %get-tuple-element.72.refs_0_), channel_id=1, source_target_pairs={{0,8},{1,9},{2,10},{3,11},{4,12},{5,13},{6,14},{7,15},{8,0},{9,1},... | collective-permute-start | bytes 786440 | tf_op jit(solution)/shard_map/ppermute | solution.py:436
  6.1 14.9 %collective-permute-start = (f32[2,4,128,128]{3,2,1,0:T(8,128)S(1)}, f32[2,4,128,128]{3,2,1,0:T(8,128)S(1)}, u32[]{:S(2)}, u32[]{:S(2)}) collective-permute-start(f32[2,4,128,128]{3,2,1,0:T(8,128)S(1)} %get-tuple-element.79), channel_id=1, source_target_pairs={{0,4},{4,0},{8,12},{12,8},{16,20},{20,16},{24,28},{28,24},{1,5},{5... | collective-permute-start | bytes 1572872 | tf_op jit(solution)/shard_map/ppermute | solution.py:321
  11.8 7.6 %collective-permute-start.1 = (f32[4,128,128]{2,1,0:T(8,128)S(1)}, f32[4,128,128]{2,1,0:T(8,128)S(1)}, u32[]{:S(2)}, u32[]{:S(2)}) collective-permute-start(f32[4,128,128]{2,1,0:T(8,128)S(1)} %hop.9.refs_2_), channel_id=1, source_target_pairs={{0,8},{1,9},{2,10},{3,11},{4,12},{5,13},{6,14},{7,15},{8,0},{9,1},... | collective-permute-start | bytes 786440 | tf_op jit(solution)/shard_map/ppermute | solution.py:436
  12.4 8.5 %collective-permute-start.4 = (f32[4,128,128]{2,1,0:T(8,128)S(1)}, f32[4,128,128]{2,1,0:T(8,128)S(1)}, u32[]{:S(2)}, u32[]{:S(2)}) collective-permute-start(f32[4,128,128]{2,1,0:T(8,128)S(1)} %hop.10.refs_4_), channel_id=1, source_target_pairs={{0,1},{1,0},{2,3},{3,2},{4,5},{5,4},{6,7},{7,6},{8,16},{9,17},{10,... | collective-permute-start | bytes 786440 | tf_op jit(solution)/shard_map/ppermute | solution.py:436
  14.4 20.5 %collective-permute-start.6 = (f32[2,4,128,128]{3,2,1,0:T(8,128)S(1)}, f32[2,4,128,128]{3,2,1,0:T(8,128)S(1)}, u32[]{:S(2)}, u32[]{:S(2)}) collective-permute-start(f32[2,4,128,128]{3,2,1,0:T(8,128)S(1)} %share.1.refs_4_), channel_id=1, source_target_pairs={{0,4},{4,0},{8,12},{12,8},{16,20},{20,16},{24,28},{28,24},{1,5},{5... | collective-permute-start | bytes 1572872 | tf_op jit(solution)/shard_map/ppermute | solution.py:340
  19.4 8.2 %collective-permute-start.3 = (f32[4,128,128]{2,1,0:T(8,128)S(1)}, f32[4,128,128]{2,1,0:T(8,128)S(1)}, u32[]{:S(2)}, u32[]{:S(2)}) collective-permute-start(f32[4,128,128]{2,1,0:T(8,128)S(1)} %hop.11.refs_4_), channel_id=1, source_target_pairs={{0,1},{1,0},{2,3},{3,2},{4,5},{5,4},{6,7},{7,6},{8,16},{9,17},{10,... | collective-permute-start | bytes 786440 | tf_op jit(solution)/shard_map/ppermute | solution.py:436
  21.0 7.4 %collective-permute-start.7 = (f32[4,128,128]{2,1,0:T(8,128)S(1)}, f32[4,128,128]{2,1,0:T(8,128)S(1)}, u32[]{:S(2)}, u32[]{:S(2)}) collective-permute-start(f32[4,128,128]{2,1,0:T(8,128)S(1)} %hop.12.refs_4_), channel_id=1, source_target_pairs={{0,8},{1,9},{2,10},{3,11},{4,12},{5,13},{6,14},{7,15},{8,0},{9,1},... | collective-permute-start | bytes 786440 | tf_op jit(solution)/shard_map/ppermute | solution.py:436
  27.7 6.4 %collective-permute-start.5 = (f32[4,128,128]{2,1,0:T(8,128)S(1)}, f32[4,128,128]{2,1,0:T(8,128)S(1)}, u32[]{:S(2)}, u32[]{:S(2)}) collective-permute-start(f32[4,128,128]{2,1,0:T(8,128)S(1)} %hop.13.refs_3_), channel_id=1, source_target_pairs={{0,8},{1,9},{2,10},{3,11},{4,12},{5,13},{6,14},{7,15},{8,0},{9,1},... | collective-permute-start | bytes 786440 | tf_op jit(solution)/shard_map/ppermute | solution.py:436
  28.5 6.5 %collective-permute-start.8 = (f32[4,128,128]{2,1,0:T(8,128)S(1)}, f32[4,128,128]{2,1,0:T(8,128)S(1)}, u32[]{:S(2)}, u32[]{:S(2)}) collective-permute-start(f32[4,128,128]{2,1,0:T(8,128)S(1)} %hop.14.refs_3_), channel_id=1, source_target_pairs={{0,1},{1,0},{2,3},{3,2},{4,5},{5,4},{6,7},{7,6},{8,16},{9,17},{10,... | collective-permute-start | bytes 786440 | tf_op jit(solution)/shard_map/ppermute | solution.py:436
  28.7 14.3 %collective-permute-start.13 = (f32[4,128,128]{2,1,0:T(8,128)S(1)}, f32[4,128,128]{2,1,0:T(8,128)S(1)}, u32[]{:S(2)}, u32[]{:S(2)}) collective-permute-start(f32[4,128,128]{2,1,0:T(8,128)S(1)} %trade.3.refs_4_), channel_id=1, source_target_pairs={{0,4},{4,0},{8,12},{12,8},{16,20},{20,16},{24,28},{28,24},{1,5},{5... | collective-permute-start | bytes 786440 | tf_op jit(solution)/shard_map/ppermute | solution.py:370
  34.2 8.6 %collective-permute-start.9 = (f32[4,128,128]{2,1,0:T(8,128)S(1)}, f32[4,128,128]{2,1,0:T(8,128)S(1)}, u32[]{:S(2)}, u32[]{:S(2)}) collective-permute-start(f32[4,128,128]{2,1,0:T(8,128)S(1)} %hop.15.refs_3_), channel_id=1, source_target_pairs={{0,1},{1,0},{2,3},{3,2},{4,5},{5,4},{6,7},{7,6},{8,16},{9,17},{10,... | collective-permute-start | bytes 786440 | tf_op jit(solution)/shard_map/ppermute | solution.py:436
  34.4 12.2 %collective-permute-start.11 = (f32[4,128,128]{2,1,0:T(8,128)S(1)}, f32[4,128,128]{2,1,0:T(8,128)S(1)}, u32[]{:S(2)}, u32[]{:S(2)}) collective-permute-start(f32[4,128,128]{2,1,0:T(8,128)S(1)} %trade.4.refs_3_), channel_id=1, source_target_pairs={{0,4},{4,0},{8,12},{12,8},{16,20},{20,16},{24,28},{28,24},{1,5},{5... | collective-permute-start | bytes 786440 | tf_op jit(solution)/shard_map/ppermute | solution.py:370
  35.1 9.0 %collective-permute-start.14 = (f32[4,128,128]{2,1,0:T(8,128)S(1)}, f32[4,128,128]{2,1,0:T(8,128)S(1)}, u32[]{:S(2)}, u32[]{:S(2)}) collective-permute-start(f32[4,128,128]{2,1,0:T(8,128)S(1)} %hop.16.refs_3_), channel_id=1, source_target_pairs={{0,8},{1,9},{2,10},{3,11},{4,12},{5,13},{6,14},{7,15},{8,0},{9,1},... | collective-permute-start | bytes 786440 | tf_op jit(solution)/shard_map/ppermute | solution.py:436
  38.6 10.2 %collective-permute-start.12 = (f32[4,128,128]{2,1,0:T(8,128)S(1)}, f32[4,128,128]{2,1,0:T(8,128)S(1)}, u32[]{:S(2)}, u32[]{:S(2)}) collective-permute-start(f32[4,128,128]{2,1,0:T(8,128)S(1)} %trade.5.refs_4_), channel_id=1, source_target_pairs={{0,4},{4,0},{8,12},{12,8},{16,20},{20,16},{24,28},{28,24},{1,5},{5... | collective-permute-start | bytes 786440 | tf_op jit(solution)/shard_map/ppermute | solution.py:370
  42.9 6.4 %collective-permute-start.10 = (f32[4,128,128]{2,1,0:T(8,128)S(1)}, f32[4,128,128]{2,1,0:T(8,128)S(1)}, u32[]{:S(2)}, u32[]{:S(2)}) collective-permute-start(f32[4,128,128]{2,1,0:T(8,128)S(1)} %hop.17.refs_35_), channel_id=1, source_target_pairs={{0,8},{1,9},{2,10},{3,11},{4,12},{5,13},{6,14},{7,15},{8,0},{9,1},... | collective-permute-start | bytes 786440 | tf_op jit(solution)/shard_map/ppermute | solution.py:436

commit v8 on v7

--- a/solution.py
+++ b/solution.py
@@ -18,7 +18,7 @@
 ACROSS_ROWS = 256
 ORDER = (
     "F", "E0", "S0", "L0123", "E1", "O1", "W20", "S1", "W21", "O2", "E2", "W00", "W01", "W10",
-    "E3", "O3", "X0", "W11", "O4", "X10", "E4", "X11", "W30", "W31", "E5", "A02", "B31",
+    "E3", "O3", "X0", "W11", "O4", "E4", "X10", "X11", "W30", "W31", "E5", "A02", "B31",
     "C31",
 )
 PARAMS = pltpu.CompilerParams(vmem_limit_bytes=8 << 20)

time: 52.2 us -> 52.2 us (level)
    ppermute x3, waiting for transfers between devices: 0.25 us -> 1.69 us  [trade(): swapped[p, turn] = lax.ppermute(payload, 'ctx', pair)]
    ppermute x10, waiting for transfers between devices: 6.3 us -> 4.94 us  [hop(): got[parity, slot] = lax.ppermute(payload, ('ctx', 'seq'), swap(parity))]
    ppermute x10, starting transfers between devices: 9.59 us -> 9.06 us  [hop(): got[parity, slot] = lax.ppermute(payload, ('ctx', 'seq'), swap(parity))]
    ppermute x3, starting transfers between devices: 2.83 us -> 3.36 us  [trade(): swapped[p, turn] = lax.ppermute(payload, 'ctx', pair)]
where the time goes in v8:
time: 52.2 us; the launch traced here: 52.1 us
  Pallas kernels  27.3 us (52%)
  starting transfers between devices  15.6 us (30%)
  waiting for transfers between devices  8.09 us (15%)
  between operations  1.02 us (2%)
    pallas_call x8, Pallas kernels, within(): pl.pallas_call(functools.partial(within_kernel, min(rows, 256), first), i...  13 us
    ppermute x10, starting transfers between devices, hop(): got[parity, slot] = lax.ppermute(payload, ('ctx', 'seq'), swap(parity))  9.06 us
    pallas_call x3, Pallas kernels, across(): pl.pallas_call(functools.partial(across_kernel, turn, chain, [(total, fir...  6.95 us
    ppermute x10, waiting for transfers between devices, hop(): got[parity, slot] = lax.ppermute(payload, ('ctx', 'seq'), swap(parity))  4.94 us
    pallas_call x1, Pallas kernels, load(): pl.pallas_call(functools.partial(load_kernel, firsts), in_specs=[HBM] * 4...  4.17 us
    ppermute x3, starting transfers between devices, trade(): swapped[p, turn] = lax.ppermute(payload, 'ctx', pair)  3.36 us
    pallas_call x1, Pallas kernels, first_states(): pl.pallas_call(functools.partial(first_kernel, firsts, chain), in_specs=[...  2.33 us
    ppermute x1, starting transfers between devices, share(): turns[turn] = lax.ppermute(payload, 'ctx', pair)  1.75 us
  transfers between devices with their start and end apart: 15, of which 8 were waited for; matrix products, arithmetic and copies ran while one was open for 0% of the time, Pallas kernels for 43%

profile of v8, /device:TPU:0, one launch (start us, length us, event | category | flops | bytes accessed | tf_op | source)
XLA Modules:
  0.0 52.1 jit_solution(696963560609535839)
XLA Ops:
  0.6 2.3 %first.1 = (f32[4,128,128]{2,1,0:T(8,128)S(1)}, f32[2,4,128,128]{3,2,1,0:T(8,128)S(1)}) custom-call(bf16[512,2048]{1,0:T(8,128)(2,1)} %q_hbm.3, bf16[512,2048]{1,0:T(8,128)(2,1)} %k_hbm.3, bf16[512,2048]{1,0:T(8,128)(2,1)} %v_hbm.3, bf16[512,2048]{1,0:T(8,128)(2,1)} %g_hbm.3), custom_call_target="tpu_custom_call" | custom-call | flops 2875000064 | bytes 1 | tf_op jit(solution)/shard_map/first/pallas_call | solution.py:80
  3.0 3.1 %collective-permute-start.2 = (f32[4,128,128]{2,1,0:T(8,128)S(1)}, f32[4,128,128]{2,1,0:T(8,128)S(1)}, u32[]{:S(2)}, u32[]{:S(2)}) collective-permute-start(f32[4,128,128]{2,1,0:T(8,128)S(1)} %get-tuple-element.72.refs_0_), channel_id=1, source_target_pairs={{0,8},{1,9},{2,10},{3,11},{4,12},{5,13},{6,14},{7,15},{8,0},{9,1},... | collective-permute-start | bytes 786440 | tf_op jit(solution)/shard_map/ppermute | solution.py:436
  6.1 1.5 %collective-permute-start = (f32[2,4,128,128]{3,2,1,0:T(8,128)S(1)}, f32[2,4,128,128]{3,2,1,0:T(8,128)S(1)}, u32[]{:S(2)}, u32[]{:S(2)}) collective-permute-start(f32[2,4,128,128]{3,2,1,0:T(8,128)S(1)} %get-tuple-element.79), channel_id=1, source_target_pairs={{0,4},{4,0},{8,12},{12,8},{16,20},{20,16},{24,28},{28,24},{1,5},{5... | collective-permute-start | bytes 1572872 | tf_op jit(solution)/shard_map/ppermute | solution.py:321
  7.5 4.2 %load.1 = (bf16[512,512]{1,0:T(8,128)(2,1)S(1)}, bf16[512,512]{1,0:T(8,128)(2,1)S(1)}, bf16[512,512]{1,0:T(8,128)(2,1)S(1)}, bf16[512,512]{1,0:T(8,128)(2,1)S(1)...) custom-call(bf16[512,2048]{1,0:T(8,128)(2,1)} %q_hbm.3, ...), custom_call_target="tpu_custom_call" | custom-call | flops 4024999936 | bytes 1 | tf_op jit(solution)/shard_map/load/pallas_call | solution.py:119
  12.5 1.8 %within.8 = (f32[512,256]{1,0:T(8,128)S(1)}, f32[512,256]{1,0:T(8,128)S(1)}, f32[512,256]{1,0:T(8,128)S(1)}, f32[512,256]{1,0:T(8,128)S(1)}) custom-call(bf16[512,512]{1,0:T(8,128)(2,1)S(1)} %get-tuple-element.81.refs_0_.refs_18_, bf16[512,512]{1,0:T(8,128)(2,1)S(1)} %get-tuple-element.82.refs_1_.refs_19_, ...), custom_call_target="tpu_custom_call" | custom-call | flops 1724999936 | bytes 1 | tf_op jit(solution)/shard_map/within/pallas_call | solution.py:160
  14.4 1.7 %collective-permute-start.6 = (f32[2,4,128,128]{3,2,1,0:T(8,128)S(1)}, f32[2,4,128,128]{3,2,1,0:T(8,128)S(1)}, u32[]{:S(2)}, u32[]{:S(2)}) collective-permute-start(f32[2,4,128,128]{3,2,1,0:T(8,128)S(1)} %share.1.refs_4_), channel_id=1, source_target_pairs={{0,4},{4,0},{8,12},{12,8},{16,20},{20,16},{24,28},{28,24},{1,5},{5... | collective-permute-start | bytes 1572872 | tf_op jit(solution)/shard_map/ppermute | solution.py:340
  16.2 1.6 %within.9 = (f32[512,256]{1,0:T(8,128)S(1)}, f32[512,256]{1,0:T(8,128)S(1)}, f32[512,256]{1,0:T(8,128)S(1)}, f32[512,256]{1,0:T(8,128)S(1)}) custom-call(bf16[512,512]{1,0:T(8,128)(2,1)S(1)} %get-tuple-element.81.refs_0_.refs_18_, bf16[512,512]{1,0:T(8,128)(2,1)S(1)} %get-tuple-element.82.refs_1_.refs_19_, ...), custom_call_target="tpu_custom_call" | custom-call | flops 1724999936 | bytes 1 | tf_op jit(solution)/shard_map/within/pallas_call | solution.py:160
  17.8 1.6 %collective-permute-done.1.refs_1_.refs_26_ = f32[4,128,128]{2,1,0:T(8,128)S(1)} collective-permute-done((f32[4,128,128]{2,1,0:T(8,128)S(1)}, f32[4,128,128]{2,1,0:T(8,128)S(1)}, u32[]{:S(2)}, u32[]{:S(2)}) %collective-permute-start.1) | collective-permute-done | bytes 262176 | tf_op jit(solution)/shard_map/ppermute | solution.py:436
  19.5 1.5 %collective-permute-done.refs_1_.refs_33_.refs_13_ = f32[2,4,128,128]{3,2,1,0:T(8,128)S(1)} collective-permute-done((f32[2,4,128,128]{3,2,1,0:T(8,128)S(1)}, f32[2,4,128,128]{3,2,1,0:T(8,128)S(1)}, u32[]{:S(2)}, u32[]{:S(2)}) %collective-permute-start) | collective-permute-done | bytes 524320 | tf_op jit(solution)/shard_map/ppermute | solution.py:321
  21.0 1.8 %collective-permute-start.7 = (f32[4,128,128]{2,1,0:T(8,128)S(1)}, f32[4,128,128]{2,1,0:T(8,128)S(1)}, u32[]{:S(2)}, u32[]{:S(2)}) collective-permute-start(f32[4,128,128]{2,1,0:T(8,128)S(1)} %hop.12.refs_4_), channel_id=1, source_target_pairs={{0,8},{1,9},{2,10},{3,11},{4,12},{5,13},{6,14},{7,15},{8,0},{9,1},... | collective-permute-start | bytes 786440 | tf_op jit(solution)/shard_map/ppermute | solution.py:436
  22.8 1.6 %within.10 = (f32[512,256]{1,0:T(8,128)S(1)}, f32[512,256]{1,0:T(8,128)S(1)}, f32[512,256]{1,0:T(8,128)S(1)}, f32[512,256]{1,0:T(8,128)S(1)}) custom-call(bf16[512,512]{1,0:T(8,128)(2,1)S(1)} %get-tuple-element.92.refs_0_, bf16[512,512]{1,0:T(8,128)(2,1)S(1)} %get-tuple-element.93.refs_1_, bf16[512,512]{1,0:T(8,128)(2,1)S(1)} %get-tuple-element.94.refs_2_, ...), custom_call_target="tpu_custom_call" | custom-call | flops 1724999936 | bytes 1 | tf_op jit(solution)/shard_map/within/pallas_call | solution.py:160
  24.4 1.6 %within.11 = (f32[512,256]{1,0:T(8,128)S(1)}, f32[512,256]{1,0:T(8,128)S(1)}, f32[512,256]{1,0:T(8,128)S(1)}, f32[512,256]{1,0:T(8,128)S(1)}) custom-call(bf16[512,512]{1,0:T(8,128)(2,1)S(1)} %get-tuple-element.92.refs_0_, bf16[512,512]{1,0:T(8,128)(2,1)S(1)} %get-tuple-element.93.refs_1_, bf16[512,512]{1,0:T(8,128)(2,1)S(1)} %get-tuple-element.94.refs_2_, ...), custom_call_target="tpu_custom_call" | custom-call | flops 1724999936 | bytes 1 | tf_op jit(solution)/shard_map/within/pallas_call | solution.py:160
  26.0 1.6 %within.12 = (f32[512,256]{1,0:T(8,128)S(1)}, f32[512,256]{1,0:T(8,128)S(1)}, f32[512,256]{1,0:T(8,128)S(1)}, f32[512,256]{1,0:T(8,128)S(1)}) custom-call(bf16[512,512]{1,0:T(8,128)(2,1)S(1)} %get-tuple-element.88.refs_0_.refs_14_.refs_16_, bf16[512,512]{1,0:T(8,128)(2,1)S(1)} %get-tuple-element.89.refs_1_.refs_15_.refs_17_, ...), custom_call_target="tpu_custom_call" | custom-call | flops 1724999936 | bytes 1 | tf_op jit(solution)/shard_map/within/pallas_call | solution.py:160
  28.7 1.2 %collective-permute-start.13 = (f32[4,128,128]{2,1,0:T(8,128)S(1)}, f32[4,128,128]{2,1,0:T(8,128)S(1)}, u32[]{:S(2)}, u32[]{:S(2)}) collective-permute-start(f32[4,128,128]{2,1,0:T(8,128)S(1)} %trade.3.refs_4_), channel_id=1, source_target_pairs={{0,4},{4,0},{8,12},{12,8},{16,20},{20,16},{24,28},{28,24},{1,5},{5... | collective-permute-start | bytes 786440 | tf_op jit(solution)/shard_map/ppermute | solution.py:370
  29.9 1.6 %within.13 = (f32[512,256]{1,0:T(8,128)S(1)}, f32[512,256]{1,0:T(8,128)S(1)}, f32[512,256]{1,0:T(8,128)S(1)}, f32[512,256]{1,0:T(8,128)S(1)}) custom-call(bf16[512,512]{1,0:T(8,128)(2,1)S(1)} %get-tuple-element.88.refs_0_.refs_14_.refs_16_, bf16[512,512]{1,0:T(8,128)(2,1)S(1)} %get-tuple-element.89.refs_1_.refs_15_.refs_17_, ...), custom_call_target="tpu_custom_call" | custom-call | flops 1724999936 | bytes 1 | tf_op jit(solution)/shard_map/within/pallas_call | solution.py:160
  31.5 2.7 %collective-permute-done.5.refs_2_.refs_1_.refs_12_.refs_28_ = f32[4,128,128]{2,1,0:T(8,128)S(1)} collective-permute-done((f32[4,128,128]{2,1,0:T(8,128)S(1)}, f32[4,128,128]{2,1,0:T(8,128)S(1)}, u32[]{:S(2)}, u32[]{:S(2)}) %collective-permute-start.5) | collective-permute-done | bytes 262176 | tf_op jit(solution)/shard_map/ppermute | solution.py:436
  34.4 2.9 %collective-permute-start.14 = (f32[4,128,128]{2,1,0:T(8,128)S(1)}, f32[4,128,128]{2,1,0:T(8,128)S(1)}, u32[]{:S(2)}, u32[]{:S(2)}) collective-permute-start(f32[4,128,128]{2,1,0:T(8,128)S(1)} %hop.16.refs_3_), channel_id=1, source_target_pairs={{0,8},{1,9},{2,10},{3,11},{4,12},{5,13},{6,14},{7,15},{8,0},{9,1},... | collective-permute-start | bytes 786440 | tf_op jit(solution)/shard_map/ppermute | solution.py:436
  37.4 1.1 %collective-permute-start.11 = (f32[4,128,128]{2,1,0:T(8,128)S(1)}, f32[4,128,128]{2,1,0:T(8,128)S(1)}, u32[]{:S(2)}, u32[]{:S(2)}) collective-permute-start(f32[4,128,128]{2,1,0:T(8,128)S(1)} %trade.4.refs_3_), channel_id=1, source_target_pairs={{0,4},{4,0},{8,12},{12,8},{16,20},{20,16},{24,28},{28,24},{1,5},{5... | collective-permute-start | bytes 786440 | tf_op jit(solution)/shard_map/ppermute | solution.py:370
  38.6 1.0 %collective-permute-start.12 = (f32[4,128,128]{2,1,0:T(8,128)S(1)}, f32[4,128,128]{2,1,0:T(8,128)S(1)}, u32[]{:S(2)}, u32[]{:S(2)}) collective-permute-start(f32[4,128,128]{2,1,0:T(8,128)S(1)} %trade.5.refs_4_), channel_id=1, source_target_pairs={{0,4},{4,0},{8,12},{12,8},{16,20},{20,16},{24,28},{28,24},{1,5},{5... | collective-permute-start | bytes 786440 | tf_op jit(solution)/shard_map/ppermute | solution.py:370
  39.6 1.6 %within.14 = (f32[512,256]{1,0:T(8,128)S(1)}, f32[512,256]{1,0:T(8,128)S(1)}, f32[512,256]{1,0:T(8,128)S(1)}, f32[512,256]{1,0:T(8,128)S(1)}) custom-call(bf16[512,512]{1,0:T(8,128)(2,1)S(1)} %get-tuple-element.73.refs_0_, bf16[512,512]{1,0:T(8,128)(2,1)S(1)} %get-tuple-element.74.refs_1_, bf16[512,512]{1,0:T(8,128)(2,1)S(1)} %get-tuple-element.75.refs_2_, ...), custom_call_target="tpu_custom_call" | custom-call | flops 1724999936 | bytes 1 | tf_op jit(solution)/shard_map/within/pallas_call | solution.py:160
  41.2 1.6 %within.15 = (f32[512,256]{1,0:T(8,128)S(1)}, f32[512,256]{1,0:T(8,128)S(1)}, f32[512,256]{1,0:T(8,128)S(1)}, f32[512,256]{1,0:T(8,128)S(1)}) custom-call(bf16[512,512]{1,0:T(8,128)(2,1)S(1)} %get-tuple-element.73.refs_0_, bf16[512,512]{1,0:T(8,128)(2,1)S(1)} %get-tuple-element.74.refs_1_, bf16[512,512]{1,0:T(8,128)(2,1)S(1)} %get-tuple-element.75.refs_2_, ...), custom_call_target="tpu_custom_call" | custom-call | flops 1724999936 | bytes 1 | tf_op jit(solution)/shard_map/within/pallas_call | solution.py:160
  43.2 2.5 %across.3 = (bf16[512,2048]{1,0:T(8,128)(2,1)}, bf16[512,2048]{1,0:T(8,128)(2,1)}, bf16[512,2048]{1,0:T(8,128)(2,1)}, bf16[512,2048]{1,0:T(8,128)(2,1)}, f32[8,128]{1,0:T(8,128)S(1)}) custom-call(bf16[512,512]{1,0:T(8,128)(2,1)S(1)} %get-tuple-element.92.refs_0_, bf16[512,512]{1,0:T(8,128)(2,1)S(1)} %get-tuple-element.93.refs_1_, ...), custom_call_target="tpu_custom_call" | custom-call | flops 3680000000 | bytes 1 | tf_op jit(solution)/shard_map/across/pallas_call | solution.py:236
  46.5 1.8 %across.4 = (bf16[512,2048]{1,0:T(8,128)(2,1)}, bf16[512,2048]{1,0:T(8,128)(2,1)}, bf16[512,2048]{1,0:T(8,128)(2,1)}, bf16[512,2048]{1,0:T(8,128)(2,1)}, f32[8,128]{1,0:T(8,128)S(1)}) custom-call(bf16[512,512]{1,0:T(8,128)(2,1)S(1)} %get-tuple-element.73.refs_0_, ...), custom_call_target="tpu_custom_call", output_to_operand_aliasing={{0}: (28, {}), {1}: (29, {}), {2}: (30, {}), {3}: (31, {})} | custom-call | flops 1840000000 | bytes 1 | tf_op jit(solution)/shard_map/across/pallas_call | solution.py:236
  49.3 2.6 %across.5 = (bf16[512,2048]{1,0:T(8,128)(2,1)}, bf16[512,2048]{1,0:T(8,128)(2,1)}, bf16[512,2048]{1,0:T(8,128)(2,1)}, bf16[512,2048]{1,0:T(8,128)(2,1)}, f32[8,128]{1,0:T(8,128)}) custom-call(bf16[512,512]{1,0:T(8,128)(2,1)S(1)} %get-tuple-element.73.refs_0_, ...), custom_call_target="tpu_custom_call", output_to_operand_aliasing={{0}: (31, {}), {1}: (32, {}), {2}: (33, {}), {3}: (34, {})} | custom-call | flops 1840000000 | bytes 1 | tf_op jit(solution)/shard_map/across/pallas_call | solution.py:236
  (32 shorter events, 4.6 us)
Async XLA Ops:
  3.0 9.4 %collective-permute-start.2 = (f32[4,128,128]{2,1,0:T(8,128)S(1)}, f32[4,128,128]{2,1,0:T(8,128)S(1)}, u32[]{:S(2)}, u32[]{:S(2)}) collective-permute-start(f32[4,128,128]{2,1,0:T(8,128)S(1)} %get-tuple-element.72.refs_0_), channel_id=1, source_target_pairs={{0,8},{1,9},{2,10},{3,11},{4,12},{5,13},{6,14},{7,15},{8,0},{9,1},... | collective-permute-start | bytes 786440 | tf_op jit(solution)/shard_map/ppermute | solution.py:436
  6.1 14.9 %collective-permute-start = (f32[2,4,128,128]{3,2,1,0:T(8,128)S(1)}, f32[2,4,128,128]{3,2,1,0:T(8,128)S(1)}, u32[]{:S(2)}, u32[]{:S(2)}) collective-permute-start(f32[2,4,128,128]{3,2,1,0:T(8,128)S(1)} %get-tuple-element.79), channel_id=1, source_target_pairs={{0,4},{4,0},{8,12},{12,8},{16,20},{20,16},{24,28},{28,24},{1,5},{5... | collective-permute-start | bytes 1572872 | tf_op jit(solution)/shard_map/ppermute | solution.py:321
  11.8 7.5 %collective-permute-start.1 = (f32[4,128,128]{2,1,0:T(8,128)S(1)}, f32[4,128,128]{2,1,0:T(8,128)S(1)}, u32[]{:S(2)}, u32[]{:S(2)}) collective-permute-start(f32[4,128,128]{2,1,0:T(8,128)S(1)} %hop.9.refs_2_), channel_id=1, source_target_pairs={{0,8},{1,9},{2,10},{3,11},{4,12},{5,13},{6,14},{7,15},{8,0},{9,1},... | collective-permute-start | bytes 786440 | tf_op jit(solution)/shard_map/ppermute | solution.py:436
  12.4 8.5 %collective-permute-start.4 = (f32[4,128,128]{2,1,0:T(8,128)S(1)}, f32[4,128,128]{2,1,0:T(8,128)S(1)}, u32[]{:S(2)}, u32[]{:S(2)}) collective-permute-start(f32[4,128,128]{2,1,0:T(8,128)S(1)} %hop.10.refs_4_), channel_id=1, source_target_pairs={{0,1},{1,0},{2,3},{3,2},{4,5},{5,4},{6,7},{7,6},{8,16},{9,17},{10,... | collective-permute-start | bytes 786440 | tf_op jit(solution)/shard_map/ppermute | solution.py:436
  14.4 19.8 %collective-permute-start.6 = (f32[2,4,128,128]{3,2,1,0:T(8,128)S(1)}, f32[2,4,128,128]{3,2,1,0:T(8,128)S(1)}, u32[]{:S(2)}, u32[]{:S(2)}) collective-permute-start(f32[2,4,128,128]{3,2,1,0:T(8,128)S(1)} %share.1.refs_4_), channel_id=1, source_target_pairs={{0,4},{4,0},{8,12},{12,8},{16,20},{20,16},{24,28},{28,24},{1,5},{5... | collective-permute-start | bytes 1572872 | tf_op jit(solution)/shard_map/ppermute | solution.py:340
  19.4 8.2 %collective-permute-start.3 = (f32[4,128,128]{2,1,0:T(8,128)S(1)}, f32[4,128,128]{2,1,0:T(8,128)S(1)}, u32[]{:S(2)}, u32[]{:S(2)}) collective-permute-start(f32[4,128,128]{2,1,0:T(8,128)S(1)} %hop.11.refs_4_), channel_id=1, source_target_pairs={{0,1},{1,0},{2,3},{3,2},{4,5},{5,4},{6,7},{7,6},{8,16},{9,17},{10,... | collective-permute-start | bytes 786440 | tf_op jit(solution)/shard_map/ppermute | solution.py:436
  21.0 7.4 %collective-permute-start.7 = (f32[4,128,128]{2,1,0:T(8,128)S(1)}, f32[4,128,128]{2,1,0:T(8,128)S(1)}, u32[]{:S(2)}, u32[]{:S(2)}) collective-permute-start(f32[4,128,128]{2,1,0:T(8,128)S(1)} %hop.12.refs_4_), channel_id=1, source_target_pairs={{0,8},{1,9},{2,10},{3,11},{4,12},{5,13},{6,14},{7,15},{8,0},{9,1},... | collective-permute-start | bytes 786440 | tf_op jit(solution)/shard_map/ppermute | solution.py:436
  27.7 6.4 %collective-permute-start.5 = (f32[4,128,128]{2,1,0:T(8,128)S(1)}, f32[4,128,128]{2,1,0:T(8,128)S(1)}, u32[]{:S(2)}, u32[]{:S(2)}) collective-permute-start(f32[4,128,128]{2,1,0:T(8,128)S(1)} %hop.13.refs_3_), channel_id=1, source_target_pairs={{0,8},{1,9},{2,10},{3,11},{4,12},{5,13},{6,14},{7,15},{8,0},{9,1},... | collective-permute-start | bytes 786440 | tf_op jit(solution)/shard_map/ppermute | solution.py:436
  28.5 5.8 %collective-permute-start.8 = (f32[4,128,128]{2,1,0:T(8,128)S(1)}, f32[4,128,128]{2,1,0:T(8,128)S(1)}, u32[]{:S(2)}, u32[]{:S(2)}) collective-permute-start(f32[4,128,128]{2,1,0:T(8,128)S(1)} %hop.14.refs_3_), channel_id=1, source_target_pairs={{0,1},{1,0},{2,3},{3,2},{4,5},{5,4},{6,7},{7,6},{8,16},{9,17},{10,... | collective-permute-start | bytes 786440 | tf_op jit(solution)/shard_map/ppermute | solution.py:436
  28.7 14.3 %collective-permute-start.13 = (f32[4,128,128]{2,1,0:T(8,128)S(1)}, f32[4,128,128]{2,1,0:T(8,128)S(1)}, u32[]{:S(2)}, u32[]{:S(2)}) collective-permute-start(f32[4,128,128]{2,1,0:T(8,128)S(1)} %trade.3.refs_4_), channel_id=1, source_target_pairs={{0,4},{4,0},{8,12},{12,8},{16,20},{20,16},{24,28},{28,24},{1,5},{5... | collective-permute-start | bytes 786440 | tf_op jit(solution)/shard_map/ppermute | solution.py:370
  34.2 8.6 %collective-permute-start.9 = (f32[4,128,128]{2,1,0:T(8,128)S(1)}, f32[4,128,128]{2,1,0:T(8,128)S(1)}, u32[]{:S(2)}, u32[]{:S(2)}) collective-permute-start(f32[4,128,128]{2,1,0:T(8,128)S(1)} %hop.15.refs_3_), channel_id=1, source_target_pairs={{0,1},{1,0},{2,3},{3,2},{4,5},{5,4},{6,7},{7,6},{8,16},{9,17},{10,... | collective-permute-start | bytes 786440 | tf_op jit(solution)/shard_map/ppermute | solution.py:436
  34.4 8.8 %collective-permute-start.14 = (f32[4,128,128]{2,1,0:T(8,128)S(1)}, f32[4,128,128]{2,1,0:T(8,128)S(1)}, u32[]{:S(2)}, u32[]{:S(2)}) collective-permute-start(f32[4,128,128]{2,1,0:T(8,128)S(1)} %hop.16.refs_3_), channel_id=1, source_target_pairs={{0,8},{1,9},{2,10},{3,11},{4,12},{5,13},{6,14},{7,15},{8,0},{9,1},... | collective-permute-start | bytes 786440 | tf_op jit(solution)/shard_map/ppermute | solution.py:436
  37.4 9.1 %collective-permute-start.11 = (f32[4,128,128]{2,1,0:T(8,128)S(1)}, f32[4,128,128]{2,1,0:T(8,128)S(1)}, u32[]{:S(2)}, u32[]{:S(2)}) collective-permute-start(f32[4,128,128]{2,1,0:T(8,128)S(1)} %trade.4.refs_3_), channel_id=1, source_target_pairs={{0,4},{4,0},{8,12},{12,8},{16,20},{20,16},{24,28},{28,24},{1,5},{5... | collective-permute-start | bytes 786440 | tf_op jit(solution)/shard_map/ppermute | solution.py:370
  38.6 10.7 %collective-permute-start.12 = (f32[4,128,128]{2,1,0:T(8,128)S(1)}, f32[4,128,128]{2,1,0:T(8,128)S(1)}, u32[]{:S(2)}, u32[]{:S(2)}) collective-permute-start(f32[4,128,128]{2,1,0:T(8,128)S(1)} %trade.5.refs_4_), channel_id=1, source_target_pairs={{0,4},{4,0},{8,12},{12,8},{16,20},{20,16},{24,28},{28,24},{1,5},{5... | collective-permute-start | bytes 786440 | tf_op jit(solution)/shard_map/ppermute | solution.py:370
  42.9 6.4 %collective-permute-start.10 = (f32[4,128,128]{2,1,0:T(8,128)S(1)}, f32[4,128,128]{2,1,0:T(8,128)S(1)}, u32[]{:S(2)}, u32[]{:S(2)}) collective-permute-start(f32[4,128,128]{2,1,0:T(8,128)S(1)} %hop.17.refs_35_), channel_id=1, source_target_pairs={{0,8},{1,9},{2,10},{3,11},{4,12},{5,13},{6,14},{7,15},{8,0},{9,1},... | collective-permute-start | bytes 786440 | tf_op jit(solution)/shard_map/ppermute | solution.py:436
